TPU v7x, 128 devices: a whole 4x4x4 slice. The times are simulated.
128 devices in a mesh: dp: 16 (over y, x), tensor: 8 (over z, core).
Axes of the slice: x: 4, y: 4, z: 4, core: 2. Of those that a mesh axis runs over, the one named last changes fastest.
Arguments:
- tokens: bfloat16 [8192, 2048], P('dp'), may hold values from -6 to 6
- segments: int32 [8192], P('dp'), may hold values from 0 to 8191, as said below
- weight_qkv: float32 [2048, 3072], P('dp', 'tensor'), may hold values from -0.125 to 0.125
- weight_out: float32 [2048, 2048], P('tensor', 'dp'), may hold values from -0.5 to 0.5
- weight_gate_up: float32 [2, 2048, 8192], P(None, 'dp', 'tensor'), may hold values from -0.125 to 0.125
- weight_down: float32 [8192, 2048], P('tensor', 'dp'), may hold values from -0.0625 to 0.0625
- norm_gains: float32 [2, 2048], replicated, may hold values from 0.5 to 1.5
- head_gains: float32 [2, 64], replicated, may hold values from 1 to 2
- first_qkv: float32 [2048, 3072], P('dp', 'tensor'), may hold values from -2048 to 2048
- first_out: float32 [2048, 2048], P('tensor', 'dp'), may hold values from -320 to 320
- first_gate_up: float32 [2, 2048, 8192], P(None, 'dp', 'tensor'), may hold values from -320 to 320
- first_down: float32 [8192, 2048], P('tensor', 'dp'), may hold values from -640 to 640
- first_norm: float32 [2, 2048], replicated, may hold values from -1536 to 1536
- first_head: float32 [2, 64], replicated, may hold values from -8192 to 8192
- second_qkv: float32 [2048, 3072], P('dp', 'tensor'), may hold values from 131072 to 524288
- second_out: float32 [2048, 2048], P('tensor', 'dp'), may hold values from 2949.12 to 11796.48
- second_gate_up: float32 [2, 2048, 8192], P(None, 'dp', 'tensor'), may hold values from 2949.12 to 11796.48
- second_down: float32 [8192, 2048], P('tensor', 'dp'), may hold values from 11796.48 to 47185.92
- second_norm: float32 [2, 2048], replicated, may hold values from 73728 to 294912
- second_head: float32 [2, 64], replicated, may hold values from 2097152 to 8388608
- cotangent: bfloat16 [8192, 2048], P('dp'), may hold values from -18 to 18
Outputs:
- block_out: bfloat16 [8192, 2048], P('dp')
- input_grad: bfloat16 [8192, 2048], P('dp')
- qkv_new: float32 [2048, 3072], P('dp', 'tensor')
- out_new: float32 [2048, 2048], P('tensor', 'dp')
- gate_up_new: float32 [2, 2048, 8192], P(None, 'dp', 'tensor')
- down_new: float32 [8192, 2048], P('tensor', 'dp')
- norm_gains_new: float32 [2, 2048], replicated
- head_gains_new: float32 [2, 64], replicated
- qkv_first: float32 [2048, 3072], P('dp', 'tensor')
- out_first: float32 [2048, 2048], P('tensor', 'dp')
- gate_up_first: float32 [2, 2048, 8192], P(None, 'dp', 'tensor')
- down_first: float32 [8192, 2048], P('tensor', 'dp')
- norm_first: float32 [2, 2048], replicated
- head_first: float32 [2, 64], replicated
- qkv_second: float32 [2048, 3072], P('dp', 'tensor')
- out_second: float32 [2048, 2048], P('tensor', 'dp')
- gate_up_second: float32 [2, 2048, 8192], P(None, 'dp', 'tensor')
- down_second: float32 [8192, 2048], P('tensor', 'dp')
- norm_second: float32 [2, 2048], replicated
- head_second: float32 [2, 64], replicated
- trust_stats: float32 [3, 6], replicated
Inputs may be any that keep to these rules, and one draw needn't show every extreme that they name: `segments`: segment numbers never fall and start at 0; the last document of the sequence has the number 8192 - 1; one document begins within the first 512 tokens and ends within the last 512 tokens, the others lie before or after it.
All inputs are finite; a program needn't handle non-finite values.
Results may differ from a plain program's by a relative error of at most 0.03.
Values may be sent and summed in bfloat16 or wider, within the bound.
No kernel may reach another device: no remote copies, remote signals or barrier semaphores. Data moves between devices by JAX's collectives and lax.ppermute only.
A program may use at most 576 MiB of HBM per device.

v0:
```python
import functools

import jax
import jax.numpy as jnp
from jax import lax
from jax.experimental import pallas as pl
from jax.experimental.pallas import tpu as pltpu
from jax.sharding import PartitionSpec as P

H = 32
KVH = 8
HD = 64
STEP = 5
D = 2048
ROWS = 512
QPK = 4
CH = 64
FLAT_GRAD = 2048 + 1024

EPS_NORM = 1e-05
ROPE_BASE = 1000000.0
BETA_ONE = 0.5
BETA_TWO = 0.5
EPS_ADAM = 1e-06
DECAY = 0.01
RATE = 0.5
F32 = jnp.float32
BF16 = jnp.bfloat16
OFF = -1e5
VMEM_LIMIT = 50 * 1024 * 1024
BACK_US = 8


def inverse_rms(array_in):
    return lax.rsqrt(jnp.mean(array_in * array_in, axis=-1, keepdims=True) + EPS_NORM)


def adapt(weight, first_old, second_old, grad_in):
    first_new = BETA_ONE * first_old + (1.0 - BETA_ONE) * grad_in
    second_new = BETA_TWO * second_old + (1.0 - BETA_TWO) * grad_in * grad_in
    direction = (
        first_new
        / (1.0 - BETA_ONE**STEP)
        / (jnp.sqrt(second_new / (1.0 - BETA_TWO**STEP)) + EPS_ADAM)
        + DECAY * weight
    )
    return (first_new, second_new, direction)


def perm_x(k):
    return [(i, (i // 4) * 4 + (i % 4 - k) % 4) for i in range(16)]


def perm_y(k):
    return [(i, ((i // 4 - k) % 4) * 4 + i % 4) for i in range(16)]


def perm_z(k):
    return [(i, ((i // 2 - k) % 4) * 2 + i % 2) for i in range(8)]


PERM_CORE = [(i, i ^ 1) for i in range(8)]
PERM_PARTNER = [(i, 15 - i) for i in range(16)]


def from_x(a, k):
    return lax.ppermute(a, "dp", perm_x(k))


def from_y(a, k):
    return lax.ppermute(a, "dp", perm_y(k))


def from_z(a, k):
    return lax.ppermute(a, "tensor", perm_z(k))


def from_core(a):
    return lax.ppermute(a, "tensor", PERM_CORE)


def from_partner(a):
    return lax.ppermute(a, "dp", PERM_PARTNER)


def beside(arrays, work):
    return lax.optimization_barrier((arrays, work))


def gather_both(u, v, later):
    row = {k: from_x(u, k) for k in (2, 1, 3)}
    column = {k: from_y(v, k) for k in (2, 1, 3)}
    (row, column), later = beside((row, column), later)
    row = jnp.stack([u, row[1], row[2], row[3]])
    column = jnp.stack([v, column[1], column[2], column[3]])
    second = {k: (from_y(row, k), from_x(column, k)) for k in (2, 1, 3)}
    first = [row] + [second[k][0] for k in (1, 2, 3)]
    return first, [column] + [second[k][1] for k in (1, 2, 3)], later


def gather_dp(a, later):
    row = {k: from_x(a, k) for k in (2, 1, 3)}
    row, later = beside(row, later)
    row = jnp.stack([a, row[1], row[2], row[3]])
    second = {k: from_y(row, k) for k in (2, 1, 3)}
    return [row] + [second[k] for k in (1, 2, 3)], later


def sum_four(own, got):
    return (own.astype(F32) + got[2].astype(F32)) + (got[1].astype(F32) + got[3].astype(F32))


def send(parts, step):
    return {k: step(parts[k], -k) for k in (2, 1, 3)}


def scatter_rest(own, got, step):
    line = sum_four(own, got)
    low = line.astype(BF16)
    return sum_four(line[0], {k: step(low[k], -k) for k in (2, 1, 3)})


def scatter_tensor(near, far, work=None):
    return scatter_ring(near.astype(F32) + from_core(far.astype(BF16)).astype(F32), work)


def scatter_ring(near, work=None):
    parts = near.reshape(4, CH, near.shape[-1])
    low = parts.astype(BF16)
    got = {k: from_z(low[k], -k) for k in (2, 1, 3)}
    if work is None:
        return sum_four(parts[0], got)
    got, work = beside(got, work)
    return sum_four(parts[0], got), work


def gather_tensor(a, work=None):
    got = {k: from_z(a, k) for k in (2, 1, 3)}
    if work is not None:
        got, work = beside(got, work)
    near = jnp.concatenate([a, got[1], got[2], got[3]], axis=0)
    halves = (near, from_core(near))
    return halves if work is None else (halves, work)


def sum_all(a):
    for step in (from_x, from_y, from_z):
        a = (a + step(a, 2)) + (step(a, 1) + step(a, 3))
    return a + from_core(a)


def params(vmem=VMEM_LIMIT):
    return pltpu.CompilerParams(vmem_limit_bytes=vmem)


def takes(us):
    return pl.CostEstimate(flops=int(us * 1.1e9), bytes_accessed=0, transcendentals=0)


def whole_specs(arrays):
    return [pl.BlockSpec(a.shape, lambda i, n=len(a.shape): (0,) * n) for a in arrays]


def prepare_kernel(row_ref, tok_ref, gain_ref, in_ref):
    x = tok_ref[...].astype(F32)
    in_ref[...] = (x * inverse_rms(x) * gain_ref[...]).astype(BF16)


def prepare(row_table, tokens, gain):
    return pl.pallas_call(
        prepare_kernel,
        grid_spec=pltpu.PrefetchScalarGridSpec(
            num_scalar_prefetch=1,
            grid=(8,),
            in_specs=[
                pl.BlockSpec((CH, D), lambda i, r: (r[i], 0)),
                pl.BlockSpec((1, D), lambda i, r: (0, 0)),
            ],
            out_specs=pl.BlockSpec((CH, D), lambda i, r: (i, 0)),
        ),
        out_shape=jax.ShapeDtypeStruct((ROWS, D), BF16),
        compiler_params=params(),
        name="prepare",
        cost_estimate=takes(4),
    )(row_table, tokens, gain)


def arrange_kernel(row_ref, tok_ref, cot_ref, in_ref, across_ref, x_ref, dy_ref):
    x_ref[...] = tok_ref[...]
    dy_ref[...] = cot_ref[...]

    @pl.when(pl.program_id(0) % 2 == 0)
    def _():
        across_ref[...] = in_ref[...].astype(F32).T.astype(BF16)


def arrange(row_table, tokens, cotangent, attn_in):
    pick = pl.BlockSpec((CH, D), lambda i, r: (r[i], 0))
    put = pl.BlockSpec((CH, D), lambda i, r: (i, 0))
    return pl.pallas_call(
        arrange_kernel,
        grid_spec=pltpu.PrefetchScalarGridSpec(
            num_scalar_prefetch=1,
            grid=(8,),
            in_specs=[pick, pick, pl.BlockSpec((128, D), lambda i, r: (i // 2, 0))],
            out_specs=[pl.BlockSpec((D, 128), lambda i, r: (0, i // 2)), put, put],
        ),
        out_shape=[
            jax.ShapeDtypeStruct((D, ROWS), BF16),
            jax.ShapeDtypeStruct((ROWS, D), BF16),
            jax.ShapeDtypeStruct((ROWS, D), BF16),
        ],
        compiler_params=params(),
        name="arrange",
        cost_estimate=takes(7),
    )(row_table, tokens, cotangent, attn_in)


def lane_of(shape):
    return lax.broadcasted_iota(jnp.int32, shape, len(shape) - 1)


def head_sums(a, low_half):
    left = jnp.sum(jnp.where(low_half, a, 0.0), axis=-1, keepdims=True)
    right = jnp.sum(jnp.where(low_half, 0.0, a), axis=-1, keepdims=True)
    return jnp.where(low_half, left, right)


def turn(a, first):
    return jnp.where(first, pltpu.roll(a, 96, 1), pltpu.roll(a, 32, 1))


def vmem_specs(count):
    return [pl.BlockSpec(memory_space=pltpu.VMEM)] * count


def shape(dims, kind):
    return jax.ShapeDtypeStruct(dims, kind)


def column_squares(a):
    total = None
    for at in range(0, a.shape[-1], 128):
        part = a[:, at : at + 128]
        part = jnp.sum(part * part, axis=0, keepdims=True)
        total = part if total is None else total + part
    return total


def eight_rows(rows):
    row = lax.broadcasted_iota(jnp.int32, (8, 128), 0)
    out = jnp.zeros((8, 128), F32)
    for index, value in enumerate(rows):
        if value is not None:
            out = jnp.where(row == index, value, out)
    return out


def pack_kernel(qkv_in, out_in, gate_up_in, down_in, first_ref, second_ref, squares_ref, qkv, out_w, gate_up, down, sems):
    pairs = ((down_in, down), (out_in, out_w), (gate_up_in, gate_up), (qkv_in, qkv))
    copies = [pltpu.make_async_copy(a, b, sems.at[i]) for i, (a, b) in enumerate(pairs)]
    for copy in copies:
        copy.start()
    copies[0].wait()
    first_ref[:, :1024] = down[...].T.astype(BF16)
    copies[1].wait()
    first_ref[:, 1024:] = out_w[...].T.astype(BF16)
    copies[2].wait()
    second_ref[:, :1024] = gate_up[0].astype(BF16)
    second_ref[:, 1024:] = gate_up[1].astype(BF16)
    copies[3].wait()
    squares_ref[...] = eight_rows(
        [
            column_squares(qkv[...]),
            column_squares(out_w[...]),
            column_squares(gate_up[0]) + column_squares(gate_up[1]),
            column_squares(down[...]),
        ]
    )


def pack(weight_qkv, weight_out, weight_gate_up, weight_down):
    given = (weight_qkv, weight_out, weight_gate_up, weight_down)
    return pl.pallas_call(
        pack_kernel,
        in_specs=[pl.BlockSpec(memory_space=pl.ANY)] * 4,
        out_specs=vmem_specs(3),
        out_shape=[shape((128, 1280), BF16), shape((128, 2048), BF16), shape((8, 128), F32)],
        scratch_shapes=[pltpu.VMEM(a.shape, F32) for a in given] + [pltpu.SemaphoreType.DMA((4,))],
        compiler_params=params(),
        name="pack",
        cost_estimate=takes(2),
    )(*given)


def project_kernel(
    blk_ref, x_ref, u0, u1, u2, u3, v0, v1, v2, v3, cos_ref, sin_ref, gain_ref,
    proj_ref, q_own_ref, q_send_ref, kv_ref, w_ref, seg_ref,
):
    @pl.when(pl.program_id(0) == 0)
    def _():
        for at_y in range(4):
            for at_x in range(4):
                slot = at_y * 4 + at_x
                start = pl.multiple_of(blk_ref[slot] * 128, 128)
                w_ref[pl.ds(start, 64), :] = (u0, u1, u2, u3)[at_y][at_x, :64, :]
                w_ref[pl.ds(start + 64, 64), :] = (v0, v1, v2, v3)[at_x][at_y]
                seg_ref[slot] = (u0, u1, u2, u3)[at_y][at_x, 64:, :]

    acc = jnp.dot(x_ref[...], w_ref[...], preferred_element_type=F32)
    proj_ref[...] = acc
    lane = lane_of((x_ref.shape[0], 128))
    low_half = lane < 64
    first = (lane & 63) < 32
    cosine = cos_ref[...]
    sine = jnp.where(first, -sin_ref[...], sin_ref[...])
    for pair in range(3):
        u = acc[:, pair * 128 : (pair + 1) * 128]
        scale = lax.rsqrt(head_sums(u * u, low_half) * (1.0 / HD) + EPS_NORM)
        hat = u * scale * gain_ref[pair // 2 : pair // 2 + 1, :]
        turned = hat * cosine + turn(hat, first) * sine
        if pair < 2:
            across = (turned.astype(BF16).astype(F32) * 0.125).T.astype(BF16)
            out = (q_own_ref, q_send_ref)[pair]
            out[0] = across[:64]
            out[1] = across[64:]
        else:
            kv_ref[...] = jnp.where(low_half, turned, u).astype(BF16)


def project(blocks, x, w_first, w_second, cosine, sine, gains):
    tile = 128
    whole = lambda dims: pl.BlockSpec(dims, lambda i, b: (0,) * len(dims))
    row = lambda width: pl.BlockSpec((tile, width), lambda i, b: (i, 0))
    pair = pl.BlockSpec((2, HD, tile), lambda i, b: (0, 0, i))
    return pl.pallas_call(
        project_kernel,
        grid_spec=pltpu.PrefetchScalarGridSpec(
            num_scalar_prefetch=1,
            grid=(ROWS // tile,),
            in_specs=[row(D)]
            + [whole((4, 80, 384))] * 4
            + [whole((4, 64, 384))] * 4
            + [row(128), row(128), whole((8, 128))],
            out_specs=[row(384), pair, pair, row(128), whole((D, 384)), whole((16, 16, 384))],
        ),
        out_shape=[
            shape((ROWS, 384), F32),
            shape((2, HD, ROWS), BF16),
            shape((2, HD, ROWS), BF16),
            shape((ROWS, 128), BF16),
            shape((D, 384), BF16),
            shape((16, 16, 384), BF16),
        ],
        compiler_params=params(),
        name="project",
        cost_estimate=takes(6),
    )(blocks, x, *w_first, *w_second, cosine, sine, gains)


def lane_masks():
    low = (lane_of((1, 128)) < 64).astype(F32)
    return low.astype(BF16), (1.0 - low).astype(BF16)


def allowed_keys(queries, is_own, at, count, kinfo_ref, qinfo_ref):
    info = kinfo_ref[pl.ds(at, count), :]
    seg = jnp.where(is_own, info[:, queries : queries + 1], info[:, 2:3])
    pos = jnp.where(is_own, info[:, 3:4], -1)
    return (seg == qinfo_ref[queries : queries + 1, :]) & (pos <= qinfo_ref[2:3, :])


def for_queries(blk_ref, slot, own_at, sets, work):
    block = blk_ref[slot]
    for queries in range(sets):
        own = blk_ref[own_at + queries]

        @pl.when((block == 0) | (block == own))
        def _(queries=queries, own=own):
            work(queries, True, block == own)

        @pl.when((block > 0) & (block < own))
        def _(queries=queries):
            work(queries, False, None)


def forward_kernel(
    blk_ref, q_first, q_second, kv0, kv1, kv2, kv3, kinfo_ref, qinfo_ref, bias_ref,
    mixed_ref, out_ref, lse_ref, send_ref, kv_all, q_t, acc,
):
    for group, ref in enumerate((kv0, kv1, kv2, kv3)):
        kv_all[group * 4 : (group + 1) * 4] = ref[...]
    acc[...] = jnp.zeros_like(acc)
    row = lax.broadcasted_iota(jnp.int32, (64, ROWS), 0)
    bias = jnp.where(row == 0, bias_ref[0:1, :], 0.0).astype(BF16)
    for head in range(QPK):
        q_t[head, :64, :] = (q_first, q_second)[head // 2][head % 2]
        q_t[head, 64:, :] = bias
    keep_k, keep_v = lane_masks()

    def step(slot, carry):
        def work(queries, masked, is_own):
            kv = kv_all[slot]
            keys = kv * keep_k + (keep_v if not masked else jnp.zeros_like(keep_v))
            vals = (kv * keep_v + keep_k).astype(F32).T.astype(BF16)[56:]
            if masked:
                allowed = allowed_keys(queries, is_own, 0, ROWS, kinfo_ref, qinfo_ref)
            for head in range(QPK):
                scores = jnp.dot(keys, q_t[head], preferred_element_type=F32)
                probs = jnp.exp(scores)
                if masked:
                    probs = jnp.where(allowed, probs, 0.0)
                acc[head] += jnp.dot(vals, probs.astype(BF16), preferred_element_type=F32)

        for_queries(blk_ref, slot, 16, 1, work)
        return carry

    lax.fori_loop(0, 16, step, 0)
    heads = []
    logs = []
    for head in range(QPK):
        total = acc[head, 0:1, :]
        heads.append(acc[head, 8:, :] / total)
        logs.append(jnp.log(total))
    mixed_ref[...] = jnp.concatenate(heads, axis=0).T.astype(BF16)
    rest = jnp.zeros((6, ROWS), F32)
    out_ref[:64], out_ref[64:] = heads[0], heads[1]
    lse_ref[...] = jnp.concatenate(logs[:2] + [rest], axis=0)
    send_ref[:64], send_ref[64:128] = heads[2], heads[3]
    send_ref[128:] = jnp.concatenate(logs[2:] + [rest], axis=0)


def attend(blocks, q_first, q_second, kv, kinfo, qinfo, bias):
    return pl.pallas_call(
        forward_kernel,
        in_specs=[pl.BlockSpec(memory_space=pltpu.SMEM)] + vmem_specs(9),
        out_specs=vmem_specs(5),
        out_shape=[
            shape((ROWS, 256), BF16),
            shape((128, ROWS), F32),
            shape((8, ROWS), F32),
            shape((136, ROWS), F32),
            shape((16, ROWS, 128), BF16),
        ],
        scratch_shapes=[
            pltpu.VMEM((QPK, 128, ROWS), BF16),
            pltpu.VMEM((QPK, 72, ROWS), F32),
        ],
        compiler_params=params(),
        name="attend",
        cost_estimate=takes(20),
    )(blocks, q_first, q_second, *kv, kinfo, qinfo, bias)


def three_rows(row, value, at):
    high = value.astype(BF16).astype(F32)
    rest = value - high
    middle = rest.astype(BF16).astype(F32)
    low = rest - middle
    return (
        jnp.where(row == at, high, 0.0)
        + jnp.where(row == at + 1, middle, 0.0)
        + jnp.where(row == at + 2, low, 0.0)
    )


def mixed_grad_kernel(near_ref, far_ref, w_ref, own_ref, send_ref):
    w = w_ref[...]
    for half, ref in enumerate((near_ref, far_ref)):
        part = jnp.dot(ref[...], w, preferred_element_type=F32).astype(BF16)
        own_ref[half * 256 : (half + 1) * 256] = part[:, :128]
        send_ref[half * 256 : (half + 1) * 256] = part[:, 128:]


def mixed_grad(near, far, down_out):
    whole = lambda dims: pl.BlockSpec(dims, lambda i: (0, 0))
    return pl.pallas_call(
        mixed_grad_kernel,
        grid=(1,),
        in_specs=[whole((256, D)), whole((256, D)), pl.BlockSpec((D, 256), lambda i: (0, 4))],
        out_specs=[whole((ROWS, 128))] * 2,
        out_shape=[shape((ROWS, 128), BF16)] * 2,
        compiler_params=params(),
        name="mixed_grad",
        cost_estimate=takes(2),
    )(near, far, down_out)


def ready_kernel(do_own, do_other, out_own, lse_own, out_other, q_own, q_other, bias_ref, q_t, do_t, q_pad, do_pad):
    row = lax.broadcasted_iota(jnp.int32, (64, ROWS), 0)
    low_half = lane_of((ROWS, 128)) < 64
    for queries in range(2):
        do = (do_own, do_other)[queries][...].astype(F32)
        q_ref = (q_own, q_other)[queries]
        q = jnp.concatenate([q_ref[0].astype(F32), q_ref[1].astype(F32)], axis=0).T
        do_turned = do.T
        dots = do_turned * (out_own, out_other)[queries][:128, :]
        for part in range(2):
            head = 2 * queries + part
            at = slice(part * 64, (part + 1) * 64)
            delta = jnp.sum(dots[at, :], axis=0, keepdims=True)
            lse = (out_other[128 + part : 129 + part, :] if queries else lse_own[part : part + 1, :])
            extra = three_rows(row, -lse, 0)
            extra = extra + jnp.where(row == 3, bias_ref[queries : queries + 1, :], 0.0)
            q_t[head, :64, :] = q_ref[part]
            q_t[head, 64:, :] = extra.astype(BF16)
            do_t[head, :64, :] = three_rows(row, -delta, 0).astype(BF16)
            do_t[head, 64:, :] = do_turned[at, :].astype(BF16)
            q_head = pltpu.roll(q, 64, 1) if part else q
            do_head = do if part else pltpu.roll(do, 64, 1)
            q_pad[head] = jnp.where(low_half, q_head, 0.0).astype(BF16)
            do_pad[head] = jnp.where(low_half, 0.0, do_head).astype(BF16)


def ready(*given):
    return pl.pallas_call(
        ready_kernel,
        in_specs=vmem_specs(len(given)),
        out_specs=vmem_specs(4),
        out_shape=[shape((QPK, 128, ROWS), BF16)] * 2 + [shape((QPK, ROWS, 128), BF16)] * 2,
        compiler_params=params(),
        name="ready",
        cost_estimate=takes(2.5),
    )(*given)


def backward_kernel(first, last, count, blk_ref, q_t, do_t, q_pad, do_pad, kv_all, kinfo_ref, qinfo_ref, *rest):
    dq_t, total = rest[-2:]
    outs = rest[-2 - count : -2]
    if first:
        dq_t[...] = jnp.zeros_like(dq_t)
    else:
        dq_t[...] = rest[0][...]
    keep_k, keep_v = lane_masks()
    keep_v_masked = jnp.where(lane_of((1, 128)) == 67, 0.0, keep_v.astype(F32)).astype(BF16)

    def step(slot, carry):
        total[...] = jnp.zeros_like(total)

        def work(queries, masked, is_own):
            kv = kv_all[blk_ref[4 * count + 2 + slot]]
            keys = kv * keep_k + (keep_v_masked if masked else keep_v)
            vals = kv * keep_v + keep_k
            keys_turned = kv.astype(F32).T[:64, :].astype(BF16)
            if masked:
                allowed = allowed_keys(queries, is_own, 0, ROWS, kinfo_ref, qinfo_ref)
            for head in (2 * queries, 2 * queries + 1):
                scores = jnp.dot(keys, q_t[head], preferred_element_type=F32)
                probs = jnp.exp(scores)
                if masked:
                    probs = jnp.where(allowed, probs, 0.0)
                grads = jnp.dot(vals, do_t[head], preferred_element_type=F32)
                grads = (probs * grads).astype(BF16)
                term = jnp.dot(probs.astype(BF16), do_pad[head], preferred_element_type=F32)
                total[...] += term + jnp.dot(grads, q_pad[head], preferred_element_type=F32)
                dq_t[head * 64 : (head + 1) * 64, :] += jnp.dot(
                    keys_turned, grads, preferred_element_type=F32
                )

        for_queries(blk_ref, slot, 4 * count, 2, work)

        for index, ref in enumerate(outs):

            @pl.when(slot // 4 == index)
            def _(index=index, ref=ref):
                ref[slot - 4 * index] = total[...].astype(BF16)

        return carry

    lax.fori_loop(0, 4 * count, step, 0)
    if last:
        dq = (dq_t[...].T * 0.125).astype(BF16)
        rest[1][...] = dq[:, :128]
        rest[2][...] = dq[:, 128:]


def attend_back(first, last, count, blocks, operands, kv, kinfo, qinfo, dq=None):
    given = [*operands, kv, kinfo, qinfo] + ([] if first else [dq])
    dkv = [shape((4, ROWS, 128), BF16)] * count
    pair = shape((ROWS, 128), BF16)
    outs = [pair, pair] + dkv if last else dkv + [shape((256, ROWS), F32)]
    return pl.pallas_call(
        functools.partial(backward_kernel, first, last, count),
        in_specs=[pl.BlockSpec(memory_space=pltpu.SMEM)] + vmem_specs(len(given)),
        out_specs=vmem_specs(len(outs)),
        out_shape=outs,
        scratch_shapes=([pltpu.VMEM((256, ROWS), F32)] if last else [])
        + [pltpu.VMEM((ROWS, 128), F32)],
        compiler_params=params(),
        name="attend_back",
        cost_estimate=takes(BACK_US * count),
    )(blocks, *given)


def heads_back_kernel(proj_ref, own_ref, other_ref, kv_ref, cos_ref, sin_ref, gain_ref, out_ref, sum_ref):
    lane = lane_of((proj_ref.shape[0], 128))
    low_half = lane < 64
    first = (lane & 63) < 32
    cosine = cos_ref[...]
    sine = jnp.where(first, sin_ref[...], -sin_ref[...])
    sums = []
    for pair in range(3):
        at = slice(pair * 128, (pair + 1) * 128)
        u = proj_ref[:, at]
        grad = (own_ref, other_ref, kv_ref)[pair][...].astype(F32)
        scale = lax.rsqrt(head_sums(u * u, low_half) * (1.0 / HD) + EPS_NORM)
        hat = u * scale
        turned = grad * cosine + turn(grad, first) * sine
        sums.append(jnp.sum(turned * hat, axis=0, keepdims=True))
        grad_hat = turned * gain_ref[pair // 2 : pair // 2 + 1, :]
        mean = head_sums(grad_hat * hat, low_half) * (1.0 / HD)
        back = scale * (grad_hat - hat * mean)
        if pair == 2:
            back = jnp.where(low_half, back, grad)
        out_ref[:, at] = back.astype(BF16)

    @pl.when(pl.program_id(0) == 0)
    def _():
        sum_ref[...] = jnp.zeros_like(sum_ref)

    sum_ref[0:1, :] += sums[0] + sums[1]
    sum_ref[1:2, :] += sums[2]


def heads_back(proj, own, other, kv, cosine, sine, gains):
    tile = 128
    row = lambda width: pl.BlockSpec((tile, width), lambda i: (i, 0))
    whole = pl.BlockSpec((8, 128), lambda i: (0, 0))
    return pl.pallas_call(
        heads_back_kernel,
        grid=(ROWS // tile,),
        in_specs=[row(384), row(128), row(128), row(128), row(128), row(128), whole],
        out_specs=[row(384), whole],
        out_shape=[shape((ROWS, 384), BF16), shape((8, 128), F32)],
        compiler_params=params(),
        name="heads_back",
        cost_estimate=takes(2),
    )(proj, own, other, kv, cosine, sine, gains)


def out_kernel(mixed_ref, w_ref, out_ref):
    out_ref[...] = dot_cols(mixed_ref[...], w_ref[...]).astype(out_ref.dtype)


def out_project(half, mixed, down_out, kind):
    return pl.pallas_call(
        out_kernel,
        grid=(1,),
        in_specs=[
            pl.BlockSpec((256, 256), lambda i: (half, 0)),
            pl.BlockSpec((D, 256), lambda i: (0, 4)),
        ],
        out_specs=pl.BlockSpec((256, D), lambda i: (0, 0)),
        out_shape=shape((256, D), kind),
        compiler_params=params(),
        name="out_project",
        cost_estimate=takes(1.8),
    )(mixed, down_out)


def ffn_kernel(
    near_ref, far_ref, grad_ref, gate_w, up_w, rows_w, act_ref, gate_ref, up_ref, near_out, far_out, x_all, both
):
    step = pl.program_id(0)

    @pl.when(step == 0)
    def _():
        x_all[:256] = near_ref[...]
        x_all[256:] = far_ref[...]

    for tile in range(4):

        @pl.when(step == tile)
        def _(tile=tile):
            x = x_all[...]
            gate = jnp.dot(x, gate_w[...], preferred_element_type=F32)
            up = jnp.dot(x, up_w[...], preferred_element_type=F32)
            inner = grad_ref[...]
            sigmoid = jax.nn.sigmoid(gate)
            activated = gate * sigmoid
            act_ref[...] = (activated * up).astype(BF16)
            grad_gate = (inner * up * sigmoid * (1.0 + gate * (1.0 - sigmoid))).astype(BF16)
            grad_up = (inner * activated).astype(BF16)
            gate_ref[...] = grad_gate
            up_ref[...] = grad_up
            both[:, tile * 256 : (tile + 1) * 256] = grad_gate
            both[:, 1024 + tile * 256 : 1024 + (tile + 1) * 256] = grad_up

    @pl.when(step >= 4)
    def _():
        part = dot_cols(both[...], rows_w[...])
        near_out[...] = part[:256]
        far_out[...] = part[256:].astype(BF16)


def feed_forward(near, far, grad_inner, gate_up):
    whole = lambda dims: pl.BlockSpec(dims, lambda j: (0, 0))
    tile = pl.BlockSpec((ROWS, 256), lambda j: (0, jnp.minimum(j, 3)))
    last = lambda j: jnp.maximum(j - 4, 0)
    return pl.pallas_call(
        ffn_kernel,
        grid=(8,),
        in_specs=[
            whole((256, D)),
            whole((256, D)),
            tile,
            pl.BlockSpec((D, 256), lambda j: (0, jnp.minimum(j, 3))),
            pl.BlockSpec((D, 256), lambda j: (0, 4 + jnp.minimum(j, 3))),
            pl.BlockSpec((512, 2048), lambda j: (last(j), 0)),
        ],
        out_specs=[tile, tile, tile]
        + [pl.BlockSpec((256, 512), lambda j: (0, last(j)))] * 2,
        out_shape=[shape((ROWS, 1024), BF16)] * 3 + [shape((256, D), F32), shape((256, D), BF16)],
        scratch_shapes=[pltpu.VMEM((ROWS, D), BF16), pltpu.VMEM((ROWS, 2048), BF16)],
        compiler_params=params(),
        name="feed_forward",
        cost_estimate=takes(13),
    )(near, far, grad_inner, gate_up, gate_up, gate_up)


def inner_grad_kernel(dy_ref, w_ref, out_ref):
    out_ref[...] = jnp.dot(dy_ref[...], w_ref[...], preferred_element_type=F32)


def inner_grad(dy, down_out):
    return pl.pallas_call(
        inner_grad_kernel,
        grid=(4,),
        in_specs=[
            pl.BlockSpec((ROWS, D), lambda j: (0, 0)),
            pl.BlockSpec((D, 256), lambda j: (0, j)),
        ],
        out_specs=pl.BlockSpec((ROWS, 256), lambda j: (0, j)),
        out_shape=shape((ROWS, 1024), F32),
        compiler_params=params(),
        name="inner_grad",
        cost_estimate=takes(5.5),
    )(dy, down_out)


def ffn_out_kernel(act_ref, w_ref, near_ref, far_ref, acc):
    step = pl.program_id(0)
    term = dot_cols(act_ref[...], w_ref[...])

    @pl.when(step == 0)
    def _():
        acc[...] = term

    @pl.when(step > 0)
    def _():
        acc[...] += term

    @pl.when(step == pl.num_programs(0) - 1)
    def _():
        near_ref[...] = acc[:256]
        far_ref[...] = acc[256:].astype(BF16)


def ffn_out(act, down_out):
    whole = lambda dims: pl.BlockSpec(dims, lambda j: (0, 0))
    return pl.pallas_call(
        ffn_out_kernel,
        grid=(4,),
        in_specs=[
            pl.BlockSpec((ROWS, 256), lambda j: (0, j)),
            pl.BlockSpec((D, 256), lambda j: (0, j)),
        ],
        out_specs=[whole((256, D)), whole((256, D))],
        out_shape=[shape((256, D), F32), shape((256, D), BF16)],
        scratch_shapes=[pltpu.VMEM((ROWS, D), F32)],
        compiler_params=params(),
        name="ffn_out",
        cost_estimate=takes(6.5),
    )(act, down_out)


def out_grad_kernel(blk_ref, near_ref, far_ref, mixed_ref, out_ref, turned):
    turned[:, :256] = near_ref[...].astype(F32).T.astype(BF16)
    turned[:, 256:] = far_ref[...].astype(F32).T.astype(BF16)
    mixed = mixed_ref[...]
    for slot in range(16):
        at = pl.ds(pl.multiple_of(blk_ref[slot] * 128, 128), 128)
        out = jnp.dot(turned[at, :], mixed, preferred_element_type=F32)
        out_ref[slot // 4, slot % 4] = out.astype(BF16)


def out_grad(blocks, near, far, mixed):
    return pl.pallas_call(
        out_grad_kernel,
        in_specs=[pl.BlockSpec(memory_space=pltpu.SMEM)] + vmem_specs(3),
        out_specs=vmem_specs(1)[0],
        out_shape=shape((4, 4, 128, 256), BF16),
        scratch_shapes=[pltpu.VMEM((D, ROWS), BF16)],
        compiler_params=params(),
        name="out_grad",
        cost_estimate=takes(2),
    )(blocks, near, far, mixed)


def qkv_out_grad_kernel(blk_ref, across_ref, grad_ref, parts_ref, u_ref, v_ref):
    grad = grad_ref[...]
    for slot in range(16):
        at_y, at_x = slot // 4, slot % 4
        at = pl.ds(pl.multiple_of(blk_ref[slot] * 128, 128), 128)
        part = jnp.dot(across_ref[at, :], grad, preferred_element_type=F32).astype(BF16)
        u_ref[at_y, at_x, :, :384] = part[:64]
        u_ref[at_y, at_x, :, 384:] = parts_ref[at_y, at_x, :64]
        v_ref[at_x, at_y, :, :384] = part[64:]
        v_ref[at_x, at_y, :, 384:] = parts_ref[at_y, at_x, 64:]


def qkv_out_grad(blocks, across, grad, out_parts):
    return pl.pallas_call(
        qkv_out_grad_kernel,
        in_specs=[pl.BlockSpec(memory_space=pltpu.SMEM)] + vmem_specs(3),
        out_specs=vmem_specs(2),
        out_shape=[shape((4, 4, 64, 640), BF16)] * 2,
        compiler_params=params(),
        name="qkv_out_grad",
        cost_estimate=takes(3),
    )(blocks, across, grad, out_parts)


def attn_back_kernel(grad_ref, w_ref, x_ref, near_ref, far_ref, gain_ref):
    step = pl.program_id(0)
    part = dot_cols(grad_ref[...], w_ref[...])
    x = x_ref[...].astype(F32)
    sums = jnp.sum(part * (x * inverse_rms(x)), axis=0, keepdims=True)

    @pl.when(step == 0)
    def _():
        gain_ref[...] = sums

    @pl.when(step > 0)
    def _():
        gain_ref[...] += sums

    @pl.when(step < 2)
    def _():
        far_ref[...] = part.astype(BF16)

    @pl.when(step >= 2)
    def _():
        near_ref[...] = part


def attn_back(grad, w, x):
    tile = 128
    turn_rows = lambda i: ((i + 2) % 4, 0)
    return pl.pallas_call(
        attn_back_kernel,
        grid=(4,),
        in_specs=[
            pl.BlockSpec((tile, 384), turn_rows),
            pl.BlockSpec((D, 384), lambda i: (0, 0)),
            pl.BlockSpec((tile, D), turn_rows),
        ],
        out_specs=[
            pl.BlockSpec((tile, D), lambda i: (jnp.maximum(i - 2, 0), 0)),
            pl.BlockSpec((tile, D), lambda i: (jnp.minimum(i, 1), 0)),
            pl.BlockSpec((1, D), lambda i: (0, 0)),
        ],
        out_shape=[shape((256, D), F32), shape((256, D), BF16), shape((1, D), F32)],
        compiler_params=params(),
        name="attn_back",
        cost_estimate=takes(6),
    )(grad, w, x)


def weight_grad_kernel(parts, wide, *refs):
    lhs, rhs = refs[:parts], refs[parts : parts + len(wide)]
    out_ref, turned = refs[-2:]
    step = pl.program_id(0)

    @pl.when(step == 0)
    def _():
        rows = ROWS // parts
        for index, ref in enumerate(lhs):
            turned[:, index * rows : (index + 1) * rows] = ref[...].astype(F32).T.astype(BF16)

    start = 0
    for ref, count in zip(rhs, wide, strict=True):

        @pl.when((step >= start) & (step < start + count))
        def _(ref=ref):
            out_ref[...] = jnp.dot(turned[...], ref[...], preferred_element_type=F32).astype(BF16)

        start += count


def weight_grad(lhs, rhs, at, flat=None):
    wide = [a.shape[1] // 256 for a in rhs]
    starts = [sum(wide[:i]) for i in range(len(wide))]
    given = [*lhs, *rhs] + ([] if flat is None else [flat])
    specs = [pl.BlockSpec(a.shape, lambda i: (0, 0)) for a in lhs]
    for start, count in zip(starts, wide, strict=True):
        specs.append(
            pl.BlockSpec(
                (ROWS, 256),
                lambda i, start=start, count=count: (0, jnp.clip(i - start, 0, count - 1)),
            )
        )
    if flat is not None:
        specs.append(pl.BlockSpec(memory_space=pl.ANY))
    return pl.pallas_call(
        functools.partial(weight_grad_kernel, len(lhs), wide),
        grid=(sum(wide),),
        in_specs=specs,
        out_specs=pl.BlockSpec((D, 256), lambda i: (0, at + i)),
        out_shape=shape((D, FLAT_GRAD), BF16),
        scratch_shapes=[pltpu.VMEM((D, ROWS), BF16)],
        input_output_aliases={} if flat is None else {len(given) - 1: 0},
        compiler_params=params(),
        name="weight_grad",
        cost_estimate=takes(1.25 * sum(wide)),
    )(*given)


def step_kernel(wide, *refs):
    count = len(wide)
    squares = []
    for index, (given, start, columns, turned, row) in enumerate(wide):
        weight, first, second = refs[at_of(wide) + 3 * index : at_of(wide) + 3 * index + 3]
        base = at_of(wide) + 3 * count + 3 * index
        first_out, second_out, direction_out = refs[base : base + 3]
        total = None
        for part in range(2 if len(weight.shape) == 3 else 1):
            grad = refs[given][:, start : start + columns].astype(F32)
            start += columns
            if turned:
                grad = grad.T
            pick = (part,) if len(weight.shape) == 3 else (slice(None),)
            first_new, second_new, direction = adapt(weight[pick], first[pick], second[pick], grad)
            first_out[pick] = first_new
            second_out[pick] = second_new
            direction_out[pick] = direction
            sums = column_squares(direction)
            total = sums if total is None else total + sums
        squares.append((row, total))
    refs[-1][...] = eight_rows([dict(squares).get(row) for row in range(8)])


def at_of(wide):
    return 1 + max(entry[0] for entry in wide)


def take_step(grads, matrices, wide):
    given = [*grads, *[a for matrix in matrices for a in matrix]]
    outs = [shape(matrix[0].shape, F32) for matrix in matrices for _ in range(3)]
    out = pl.pallas_call(
        functools.partial(step_kernel, wide),
        grid=(1,),
        in_specs=whole_specs(given),
        out_specs=whole_specs(outs + [shape((8, 128), F32)]),
        out_shape=outs + [shape((8, 128), F32)],
        compiler_params=params(),
        name="take_step",
        cost_estimate=takes(4),
    )(*given)
    return [out[3 * i : 3 * i + 3] for i in range(len(matrices))], out[-1]


def finish_kernel(*refs):
    sums = refs[0]
    weights, directions = refs[1:5], refs[5:9]
    gains = (refs[9:12], refs[12:15])
    outs = refs[15:19]
    gain_outs = (refs[19:22], refs[22:25])
    stats_ref = refs[25]
    row = lax.broadcasted_iota(jnp.int32, (3, 6), 0)
    column = lax.broadcasted_iota(jnp.int32, (3, 6), 1)
    stats = jnp.zeros((3, 6), F32)

    def total(a):
        return jnp.sum(jnp.sum(a, axis=1, keepdims=True), axis=0, keepdims=True)

    def keep(stats, index, weight_norm, step_norm):
        ratio = weight_norm / (step_norm + EPS_ADAM)
        values = jnp.where(row == 0, weight_norm, jnp.where(row == 1, step_norm, ratio))
        return jnp.where(column == index, values, stats), ratio

    for index in range(4):
        weight_norm = jnp.sqrt(total(sums[2:3, 256 + index * 128 : 384 + index * 128]))
        step_norm = jnp.sqrt(total(sums[2:3, 768 + index * 128 : 896 + index * 128]))
        stats, ratio = keep(stats, index, weight_norm, step_norm)
        weight, direction, out = weights[index], directions[index], outs[index]
        if len(weight.shape) == 3:
            for part in range(2):
                out[part] = weight[part] - RATE * ratio * direction[part]
        else:
            out[...] = weight[...] - RATE * ratio * direction[...]
    query_gain = sums[2:3, 0:64] + sums[2:3, 64:128]
    head_grad = jnp.concatenate([query_gain, sums[2:3, 128:192]], axis=0)
    for index, grad in enumerate((sums[0:2, :], head_grad)):
        weight, first, second = (ref[...] for ref in gains[index])
        first_new, second_new, direction = adapt(weight, first, second, grad)
        weight_norm = jnp.sqrt(total(weight * weight))
        step_norm = jnp.sqrt(total(direction * direction))
        stats, ratio = keep(stats, 4 + index, weight_norm, step_norm)
        new_out, first_out, second_out = gain_outs[index]
        new_out[...] = weight - RATE * ratio * direction
        first_out[...] = first_new
        second_out[...] = second_new
    stats_ref[...] = stats


def finish(sums, weights, directions, norm_set, head_set):
    outs = [shape(w.shape, F32) for w in weights]
    outs += [shape(norm_set[0].shape, F32)] * 3 + [shape(head_set[0].shape, F32)] * 3
    outs += [shape((3, 6), F32)]
    given = (sums, *weights, *directions, *norm_set, *head_set)
    return pl.pallas_call(
        finish_kernel,
        grid=(1,),
        in_specs=whole_specs(given),
        out_specs=whole_specs(outs),
        out_shape=outs,
        compiler_params=params(),
        name="finish",
        cost_estimate=takes(3),
    )(*given)


def norm_back(grad_in, normed, inv_scale, gain):
    grad_hat = grad_in * gain
    return inv_scale * (grad_hat - normed * jnp.mean(grad_hat * normed, axis=-1, keepdims=True))


def dot_cols(a, b):
    return lax.dot_general(a, b, (((1,), (1,)), ((), ())), preferred_element_type=F32)


def in_order(a, row_table):
    return jnp.concatenate([lax.dynamic_slice_in_dim(a, row_table[j] * CH, CH, 0) for j in range(8)])


def local(
    tokens,
    segments,
    weight_qkv,
    weight_out,
    weight_gate_up,
    weight_down,
    norm_gains,
    head_gains,
    first_qkv,
    first_out,
    first_gate_up,
    first_down,
    first_norm,
    first_head,
    second_qkv,
    second_out,
    second_gate_up,
    second_down,
    second_norm,
    second_head,
    cotangent,
):
    seg_low = jnp.concatenate([segments >> 6, segments & 63]).astype(BF16).reshape(4, 256)
    seg_low = jnp.pad(seg_low, ((0, 12), (0, 128)))
    qkv_low = weight_qkv.astype(BF16)
    w_first, w_second, tokens = gather_both(
        jnp.concatenate([qkv_low[:64], seg_low], axis=0), qkv_low[64:], tokens
    )

    dp = lax.axis_index("dp")
    tensor = lax.axis_index("tensor")
    y, x = dp >> 2, dp & 3
    z, core = tensor >> 1, tensor & 1
    slots = jnp.arange(8, dtype=jnp.int32)
    row_table = 2 * ((z + slots) & 3) + (core ^ (slots >> 2))
    sixteen = jnp.arange(16, dtype=jnp.int32)
    blocks = ((((sixteen >> 2) + y) & 3) << 2) + ((sixteen + x) & 3)
    blocks_turned = ((((sixteen) + y) & 3) << 2) + (((sixteen >> 2) + x) & 3)
    own_blocks = jnp.stack([dp, 15 - dp])
    zero_slot = ((-y & 3) << 2) + (-x & 3)
    partner_slot = (((3 - 2 * y) & 3) << 2) + ((3 - 2 * x) & 3)

    down_out, gate_up, weight_squares = pack(weight_qkv, weight_out, weight_gate_up, weight_down)
    down_out = lax.all_gather(down_out, "dp", axis=0, tiled=True)
    gate_up = lax.all_gather(gate_up, "dp", axis=0, tiled=True)

    attn_in = prepare(row_table, tokens, norm_gains[0:1])
    token_ids = (row_table[:, None] * CH + jnp.arange(CH, dtype=jnp.int32)[None, :]).reshape(ROWS)
    frequency = ROPE_BASE ** (-(jnp.arange(HD // 2, dtype=F32) * 2.0 / HD))
    angles = (dp * ROWS + token_ids).astype(F32)[:, None] * jnp.tile(frequency, 4)[None, :]
    cosine, sine = jnp.cos(angles), jnp.sin(angles)
    gain_rows = jnp.concatenate(
        [
            jnp.concatenate([head_gains[0:1], head_gains[0:1]], axis=1),
            jnp.concatenate([head_gains[1:2], jnp.ones((1, HD), F32)], axis=1),
            jnp.zeros((6, 128), F32),
        ]
    )
    projected, q_own, q_send, local_kv, full_qkv, all_segs = project(
        blocks, attn_in, w_first, w_second, cosine, sine, gain_rows
    )
    kv_groups, (all_segs, tokens, cotangent) = gather_dp(local_kv, (all_segs, tokens, cotangent))
    kv_groups, (across, x_rows, dy) = beside(
        kv_groups, arrange(row_table, tokens, cotangent, attn_in)
    )

    def block_segs(slot):
        got = lax.dynamic_slice(all_segs, (slot, 0, 0), (1, 4, 256)).astype(jnp.int32).reshape(2, ROWS)
        return got[0] * 64 + got[1]

    partner_segs = block_segs(partner_slot)
    seg_rows = in_order(segments, row_table)
    first_rows = in_order(block_segs(zero_slot), row_table)
    partner_rows = in_order(partner_segs, row_table)
    kinfo = jnp.stack([seg_rows, partner_rows, first_rows, token_ids], axis=1)
    qinfo = jnp.concatenate(
        [seg_rows[None], partner_rows[None], token_ids[None], jnp.zeros((5, ROWS), jnp.int32)]
    )
    bias = jnp.concatenate(
        [
            jnp.where(seg_rows == segments[0], 0.0, OFF).astype(F32)[None],
            jnp.where(partner_rows == partner_segs[0], 0.0, OFF).astype(F32)[None],
            jnp.zeros((6, ROWS), F32),
        ]
    )
    mixed, out_own, log_own, out_send, kv_all = attend(
        jnp.concatenate([blocks, own_blocks]), q_own, q_send, kv_groups, kinfo, qinfo, bias
    )

    far = out_project(1, mixed, down_out, BF16)
    near = out_project(0, mixed, down_out, F32)
    own_tokens = x_rows[:CH].astype(F32)
    attn_rows, grad_inner = scatter_tensor(near, far, inner_grad(dy, down_out))
    hidden_one = own_tokens + attn_rows
    scale_two = inverse_rms(hidden_one)
    normed_two = hidden_one * scale_two
    ffn_in, (out_other, q_other) = gather_tensor(
        (normed_two * norm_gains[1]).astype(BF16), (from_partner(out_send), from_partner(q_send))
    )
    inner_act, grad_gate, grad_up, near, far = feed_forward(*ffn_in, grad_inner, gate_up)

    grads = weight_grad([dy], [inner_act], 8)
    grads = weight_grad(ffn_in, [grad_gate, grad_up], 0, grads)
    grad_ffn_in, grads = scatter_tensor(near, far, grads)
    grads = lax.psum_scatter(grads, "dp", scatter_dimension=0, tiled=True)
    gain_ffn = jnp.sum(grad_ffn_in * normed_two, axis=0)
    grad_hidden = dy[:CH].astype(F32) + norm_back(grad_ffn_in, normed_two, scale_two, norm_gains[1])
    ffn_parts = ffn_out(inner_act, down_out)
    grad_attn, (ffn_near, ffn_far) = gather_tensor(grad_hidden.astype(BF16), ffn_parts)

    do_own, do_send = mixed_grad(*grad_attn, down_out)
    do_other = from_partner(do_send)
    out_parts = out_grad(blocks, *grad_attn, mixed)
    do_other, out_parts = beside(do_other, out_parts)
    ffn_far = from_core(ffn_far)
    operands = ready(do_own, do_other, out_own, log_own, out_other, q_own, q_other, bias)

    def back_groups(groups, first, last, state):
        info = jnp.concatenate(
            [blocks[4 * k : 4 * k + 4] for k in groups]
            + [own_blocks]
            + [sixteen[4 * k : 4 * k + 4] for k in groups]
        )
        return attend_back(first, last, len(groups), info, operands, kv_all, kinfo, qinfo, state)

    got = {}
    part, state = back_groups((2,), True, False, None)
    got[2] = from_y(part, -2)
    part, state = back_groups((1,), False, False, state)
    got[1] = from_y(part, -1)
    (got[2], ffn_far), state = beside((got[2], ffn_far), state)
    ffn_near = (ffn_near + ffn_far.astype(F32)).reshape(4, CH, D)
    ffn_low = ffn_near.astype(BF16)
    ffn_got = {k: from_z(ffn_low[k], -k) for k in (2, 1, 3)}
    part, state = back_groups((3,), False, False, state)
    got[3] = from_y(part, -3)
    (got[1], ffn_got), state = beside((got[1], ffn_got), state)
    dq_own, dq_send, own_part = back_groups((0,), False, True, state)
    dq_other = from_partner(dq_send)
    block_rows = (hidden_one + sum_four(ffn_near[0], ffn_got)).astype(BF16)
    block_out = lax.all_gather(block_rows, "tensor", axis=0, tiled=True)

    line = sum_four(own_part, got)
    low = line.astype(BF16)
    got = {k: from_x(low[k], -k) for k in (2, 1, 3)}
    got, dq_other = beside(got, dq_other)
    grad_kv = sum_four(line[0], got).astype(BF16)
    grad_projected, gain_heads = heads_back(
        projected, dq_own, dq_other, grad_kv, cosine, sine, gain_rows
    )
    parts_u, parts_v = qkv_out_grad(blocks, across, grad_projected, out_parts)
    got_u, got_v = send(parts_u, from_y), send(parts_v, from_x)

    (gate_up_step, down_step), later_squares = take_step(
        [grads],
        [(weight_gate_up, first_gate_up, second_gate_up), (weight_down, first_down, second_down)],
        ((0, 0, 1024, False, 2), (0, 2048, 1024, True, 3)),
    )
    grad_projected, _ = beside(grad_projected, (parts_u, parts_v))
    near, far, gain_attn = attn_back(grad_projected, full_qkv, x_rows)
    near = near + from_core(far).astype(F32)
    (got_u, got_v), (near, later_squares, block_out) = beside(
        (got_u, got_v), (near, later_squares, block_out)
    )
    late_grad = jnp.concatenate(
        [scatter_rest(parts_u[0], got_u, from_x), scatter_rest(parts_v[0], got_v, from_y)]
    )
    (qkv_step, out_step), qkv_squares = take_step(
        [late_grad],
        [(weight_qkv, first_qkv, second_qkv), (weight_out, first_out, second_out)],
        ((0, 0, 384, False, 0), (0, 384, 256, True, 1)),
    )
    squares = jnp.concatenate(
        [
            gain_heads[0:1],
            gain_heads[1:2],
            weight_squares[:4].reshape(1, 512),
            (later_squares + qkv_squares)[:4].reshape(1, 512),
            jnp.zeros((1, D - 1280), F32),
        ],
        axis=1,
    )
    sums = jnp.concatenate([gain_attn, gain_ffn[None], squares, jnp.zeros((1, D), F32)])
    near, _ = beside(near, sums)
    grad_attn_in = scatter_ring(near)
    scale_one = inverse_rms(own_tokens)
    normed_one = own_tokens * scale_one
    input_grad = (
        grad_hidden + norm_back(grad_attn_in, normed_one, scale_one, norm_gains[0])
    ).astype(BF16)
    input_grad = lax.all_gather(input_grad, "tensor", axis=0, tiled=True)

    sums = sum_all(sums)
    steps = (qkv_step, out_step, gate_up_step, down_step)
    done = finish(
        sums,
        (weight_qkv, weight_out, weight_gate_up, weight_down),
        [step[2] for step in steps],
        (norm_gains, first_norm, second_norm),
        (head_gains, first_head, second_head),
    )
    return (
        block_out,
        input_grad,
        *done[:4],
        done[4],
        done[7],
        *[step[0] for step in steps],
        done[5],
        done[8],
        *[step[1] for step in steps],
        done[6],
        done[9],
        done[10],
    )


def solution(mesh):
    matrix_specs = (P("dp", "tensor"), P("tensor", "dp"), P(None, "dp", "tensor"), P("tensor", "dp"), P(), P())
    in_specs = (P("dp", None), P("dp"), *matrix_specs, *matrix_specs, *matrix_specs, P("dp", None))
    out_specs = (P("dp", None), P("dp", None), *matrix_specs, *matrix_specs, *matrix_specs, P())
    return jax.shard_map(local, mesh=mesh, in_specs=in_specs, out_specs=out_specs, check_vma=False)
```

profile of v0, /device:TPU:1, one launch (start us, length us, event | category | flops | bytes accessed | tf_op | source)
XLA Modules:
  0.0 448.0 jit_solution(4645337641345765158)
XLA Ops:
  41.1 5.3 %prepare.1.x_ref.in_ref = bf16[512,2048]{1,0:T(8,128)(2,1)S(1)} custom-call(s32[8]{0:T(128)S(1)} %get-tuple-element.307.row_ref, bf16[512,2048]{1,0:T(8,128)(2,1)} %tok_ref.1, f32[1,2048]{1,0:T(1,128)S(1)} %get-tuple-element.344.gain_ref), custom_call_target="tpu_custom_call" | custom-call | flops 4400000000 | tf_op jit(solution)/shard_map/prepare/pallas_call | solution.py:170
  49.4 6.6 %project.1 = (f32[512,384]{1,0:T(8,128)S(1)}, bf16[2,64,512]{2,1,0:T(8,128)(2,1)S(1)}, bf16[2,64,512]{2,1,0:T(8,128)(2,1)S(1)}, bf16[512,128]{1,0:T(8,128)(2,1)S...) custom-call(s32[16]{0:T(128)S(1)} %and_add_fusion.blk_ref, bf16[512,2048]{1,0:T(8,128)(2,1)} %copy-done.39, ...), custom_call_target="tpu_custom_call" | custom-call | flops 6600000000 | tf_op jit(solution)/shard_map/project/pallas_call | solution.py:336
  74.9 8.5 %arrange.1 = (bf16[2048,512]{1,0:T(8,128)(2,1)S(1)}, bf16[512,2048]{1,0:T(8,128)(2,1)}, bf16[512,2048]{1,0:T(8,128)(2,1)}) custom-call(s32[8]{0:T(128)S(1)} %get-tuple-element.307.row_ref, bf16[512,2048]{1,0:T(8,128)(2,1)} %tok_ref.1, bf16[512,2048]{1,0:T(8,128)(2,1)} %cot_ref, bf16[512,2048]{1,0:T(8,128)(2,1)} %copy-done.39), custom_call_target="tpu_custom_call" | custom-call | flops 7699999744 | tf_op jit(solution)/shard_map/arrange/pallas_call | solution.py:200
  85.0 13.9 %collective-permute-done.17.kv3 = bf16[4,512,128]{2,1,0:T(8,128)(2,1)} collective-permute-done((bf16[4,512,128]{2,1,0:T(8,128)(2,1)S(1)}, bf16[4,512,128]{2,1,0:T(8,128)(2,1)}, u32[]{:S(2)}, u32[]{:S(2)}) %collective-permute-start.17) | collective-permute-done | bytes 524320 | tf_op jit(solution)/shard_map/ppermute | solution.py:71
  107.3 23.3 %collective-permute-start.25 = (f32[136,512]{1,0:T(8,128)S(1)}, f32[136,512]{1,0:T(8,128)S(1)}, u32[]{:S(2)}, u32[]{:S(2)}) collective-permute-start(f32[136,512]{1,0:T(8,128)S(1)} %get-tuple-element.188), channel_id=1, source_target_pairs={{0,120},{8,112},{16,104},{24,96},{32,88},{40,80},{48,72},{56,64},{... | collective-permute-start | bytes 835592 | tf_op jit(solution)/shard_map/ppermute | solution.py:83
  137.2 5.5 %inner_grad.1.grad_ref = f32[512,1024]{1,0:T(8,128)S(1)} custom-call(bf16[512,2048]{1,0:T(8,128)(2,1)} %get-tuple-element.174.dy_ref.refs_0_, bf16[2048,1280]{1,0:T(8,128)(2,1)} %all-gather.5.cloned.1.call-done.w_ref), custom_call_target="tpu_custom_call" | custom-call | flops 6049999872 | tf_op jit(solution)/shard_map/inner_grad/pallas_call | solution.py:726
  153.9 10.5 %collective-permute-done.26.q_other = bf16[2,64,512]{2,1,0:T(8,128)(2,1)S(1)} collective-permute-done((bf16[2,64,512]{2,1,0:T(8,128)(2,1)S(1)}, bf16[2,64,512]{2,1,0:T(8,128)(2,1)S(1)}, u32[]{:S(2)}, u32[]{:S(2)}) %collective-permute-start.26) | collective-permute-done | bytes 131104 | tf_op jit(solution)/shard_map/ppermute | solution.py:83
  171.2 16.9 %feed_forward.1 = (bf16[512,1024]{1,0:T(8,128)(2,1)S(1)}, bf16[512,1024]{1,0:T(8,128)(2,1)S(1)}, bf16[512,1024]{1,0:T(8,128)(2,1)S(1)}, f32[256,2048]{1,0:T(8,128)}, bf16[256,2048]{1,0:T(8,128)(2,1)}) custom-call(bf16[256,2048]{1,0:T(8,128)(2,1)} %copy-done, bf16[256,2048]{1,0:T(8,128)(2,1)} %collective-permute-done.27.far_ref.refs_1_, ...), custom_call_target="tpu_custom_call" | custom-call | flops 14300000256 | tf_op jit(solution)/shard_map/feed_forward/pallas_call | solution.py:700
  188.5 5.1 %weight_grad.2.refs_4_ = bf16[2048,3072]{1,0:T(8,128)(2,1)} custom-call(bf16[512,2048]{1,0:T(8,128)(2,1)S(1)} %copy-done.5, bf16[512,1024]{1,0:T(8,128)(2,1)S(1)} %get-tuple-element.198.refs_1_.act_ref), custom_call_target="tpu_custom_call" | custom-call | flops 5500000256 | tf_op jit(solution)/shard_map/weight_grad/pallas_call | solution.py:905
  199.1 10.5 %weight_grad.3 = bf16[2048,3072]{1,0:T(8,128)(2,1)} custom-call(bf16[256,2048]{1,0:T(8,128)(2,1)S(1)} %copy-done.1, bf16[256,2048]{1,0:T(8,128)(2,1)} %collective-permute-done.27.far_ref.refs_1_, bf16[512,1024]{1,0:T(8,128)(2,1)S(1)} %get-tuple-element.196.refs_2_, bf16[512,1024]{1,0:T(8,128)(2,1)} %copy-done.41, ...), custom_call_target="tpu_custom_call", output_to_operand_aliasing={{}: (4, {})} | custom-call | flops 11000000512 | tf_op jit(solution)/shard_map/weight_grad/pallas_call | solution.py:905
  218.9 7.5 %ffn_out.1 = (f32[256,2048]{1,0:T(8,128)}, bf16[256,2048]{1,0:T(8,128)(2,1)S(1)}) custom-call(bf16[512,1024]{1,0:T(8,128)(2,1)S(1)} %copy-done.31, bf16[2048,1280]{1,0:T(8,128)(2,1)} %all-gather.5.cloned.1.call-done.w_ref), custom_call_target="tpu_custom_call" | custom-call | flops 7150000128 | tf_op jit(solution)/shard_map/ffn_out/pallas_call | solution.py:761
  226.4 6.9 %collective-permute-done.34 = bf16[64,2048]{1,0:T(8,128)(2,1)S(1)} collective-permute-done((bf16[64,2048]{1,0:T(8,128)(2,1)S(1)}, bf16[64,2048]{1,0:T(8,128)(2,1)S(1)}, u32[]{:S(2)}, u32[]{:S(2)}) %collective-permute-start.34) | collective-permute-done | bytes 262176 | tf_op jit(solution)/shard_map/ppermute | solution.py:75
  241.8 6.9 %collective-permute-done.36.do_other = bf16[512,128]{1,0:T(8,128)(2,1)S(1)} collective-permute-done((bf16[512,128]{1,0:T(8,128)(2,1)S(1)}, bf16[512,128]{1,0:T(8,128)(2,1)S(1)}, u32[]{:S(2)}, u32[]{:S(2)}) %collective-permute-start.36) | collective-permute-done | bytes 131104 | tf_op jit(solution)/shard_map/ppermute | solution.py:83
  249.1 8.7 %attend_back.4 = (bf16[4,512,128]{2,1,0:T(8,128)(2,1)S(1)}, f32[256,512]{1,0:T(8,128)S(1)}) custom-call(s32[10]{0:T(128)S(1)} %get-tuple-element.391.blk_ref, bf16[4,128,512]{2,1,0:T(8,128)(2,1)S(1)} %get-tuple-element.214.q_t, bf16[4,128,512]{2,1,0:T(8,128)(2,1)S(1)} %get-tuple-element.215.do_t, bf16[4,512,128]{2,1,0:T(8,128)(2,1)S(1)} %get-tuple-element.216.q_pad, ...), custom_call_target="tpu_custom_call" | custom-call | flops 8800000000 | tf_op jit(solution)/shard_map/attend_back/pallas_call | solution.py:582
  262.4 8.9 %attend_back.5 = (bf16[4,512,128]{2,1,0:T(8,128)(2,1)S(1)}, f32[256,512]{1,0:T(8,128)S(1)}) custom-call(s32[10]{0:T(128)S(1)} %get-tuple-element.390.blk_ref, bf16[4,128,512]{2,1,0:T(8,128)(2,1)S(1)} %get-tuple-element.214.q_t, bf16[4,128,512]{2,1,0:T(8,128)(2,1)S(1)} %get-tuple-element.215.do_t, bf16[4,512,128]{2,1,0:T(8,128)(2,1)S(1)} %get-tuple-element.216.q_pad, ...), custom_call_target="tpu_custom_call" | custom-call | flops 8800000000 | tf_op jit(solution)/shard_map/attend_back/pallas_call | solution.py:582
  271.5 11.8 %collective-permute-done.38 = bf16[4,512,128]{2,1,0:T(8,128)(2,1)S(1)} collective-permute-done((bf16[4,512,128]{2,1,0:T(8,128)(2,1)S(1)}, bf16[4,512,128]{2,1,0:T(8,128)(2,1)S(1)}, u32[]{:S(2)}, u32[]{:S(2)}) %collective-permute-start.38) | collective-permute-done | bytes 524320 | tf_op jit(solution)/shard_map/ppermute | solution.py:71
  286.5 8.6 %attend_back.6 = (bf16[4,512,128]{2,1,0:T(8,128)(2,1)S(1)}, f32[256,512]{1,0:T(8,128)S(1)}) custom-call(s32[10]{0:T(128)S(1)} %get-tuple-element.392.blk_ref, bf16[4,128,512]{2,1,0:T(8,128)(2,1)S(1)} %get-tuple-element.214.q_t, bf16[4,128,512]{2,1,0:T(8,128)(2,1)S(1)} %get-tuple-element.215.do_t, bf16[4,512,128]{2,1,0:T(8,128)(2,1)S(1)} %get-tuple-element.216.q_pad, ...), custom_call_target="tpu_custom_call" | custom-call | flops 8800000000 | tf_op jit(solution)/shard_map/attend_back/pallas_call | solution.py:582
  298.9 10.6 %attend_back.7 = (bf16[512,128]{1,0:T(8,128)(2,1)S(1)}, bf16[512,128]{1,0:T(8,128)(2,1)S(1)}, bf16[4,512,128]{2,1,0:T(8,128)(2,1)S(1)}) custom-call(s32[10]{0:T(128)S(1)} %get-tuple-element.389.blk_ref, bf16[4,128,512]{2,1,0:T(8,128)(2,1)S(1)} %get-tuple-element.214.q_t, bf16[4,128,512]{2,1,0:T(8,128)(2,1)S(1)} %get-tuple-element.215.do_t, ...), custom_call_target="tpu_custom_call" | custom-call | flops 8800000000 | tf_op jit(solution)/shard_map/attend_back/pallas_call | solution.py:582
  313.6 6.0 %collective-permute-start.45 = (bf16[512,128]{1,0:T(8,128)(2,1)S(1)}, bf16[512,128]{1,0:T(8,128)(2,1)S(1)}, u32[]{:S(2)}, u32[]{:S(2)}) collective-permute-start(bf16[512,128]{1,0:T(8,128)(2,1)S(1)} %get-tuple-element.328), channel_id=1, source_target_pairs={{0,16},{8,24},{16,0},{24,8},{32,48},{40,56},{48,32},{56,40},{64,80... | collective-permute-start | bytes 393224 | tf_op jit(solution)/shard_map/ppermute | solution.py:67
  320.4 8.2 %collective-permute-done.44 = bf16[512,128]{1,0:T(8,128)(2,1)S(1)} collective-permute-done((bf16[512,128]{1,0:T(8,128)(2,1)S(1)}, bf16[512,128]{1,0:T(8,128)(2,1)S(1)}, u32[]{:S(2)}, u32[]{:S(2)}) %collective-permute-start.44) | collective-permute-done | bytes 131104 | tf_op jit(solution)/shard_map/ppermute | solution.py:67
  334.1 5.4 %attn_back.1 = (f32[256,2048]{1,0:T(8,128)}, bf16[256,2048]{1,0:T(8,128)(2,1)S(1)}, f32[1,2048]{1,0:T(1,128)S(1)}) custom-call(bf16[512,384]{1,0:T(8,128)(2,1)S(1)} %get-tuple-element.243.grad_ref, bf16[2048,384]{1,0:T(8,128)(2,1)S(1)} %copy-done.44, bf16[512,2048]{1,0:T(8,128)(2,1)} %get-tuple-element.175.x_ref), custom_call_target="tpu_custom_call" | custom-call | flops 6600000000 | tf_op jit(solution)/shard_map/attn_back/pallas_call | solution.py:850
  344.1 7.5 %collective-permute-start.48 = (bf16[4,64,640]{2,1,0:T(8,128)(2,1)S(1)}, bf16[4,64,640]{2,1,0:T(8,128)(2,1)S(1)}, u32[]{:S(2)}, u32[]{:S(2)}) collective-permute-start(bf16[4,64,640]{2,1,0:T(8,128)(2,1)S(1)} %get-tuple-element.314), channel_id=1, source_target_pairs={{0,32},{8,40},{16,48},{24,56},{32,64},{40,72},{48,80},{56,88},{64,... | collective-permute-start | bytes 983048 | tf_op jit(solution)/shard_map/ppermute | solution.py:71
  395.9 6.1 %collective-permute-done.61 = bf16[64,2048]{1,0:T(8,128)(2,1)S(1)} collective-permute-done((bf16[64,2048]{1,0:T(8,128)(2,1)S(1)}, bf16[64,2048]{1,0:T(8,128)(2,1)S(1)}, u32[]{:S(2)}, u32[]{:S(2)}) %collective-permute-start.61) | collective-permute-done | bytes 262176 | tf_op jit(solution)/shard_map/ppermute | solution.py:75
  424.7 8.2 %collective-permute-start.73 = (f32[4,2048]{1,0:T(4,128)S(1)}, f32[4,2048]{1,0:T(4,128)S(1)}, u32[]{:S(2)}, u32[]{:S(2)}) collective-permute-start(f32[4,2048]{1,0:T(4,128)S(1)} %add_add_fusion.1), channel_id=1, source_target_pairs={{0,1},{1,0},{2,3},{3,2},{4,5},{5,4},{6,7},{7,6},{8,9},{9,8},{10,11... | collective-permute-start | bytes 98312 | tf_op jit(solution)/shard_map/ppermute | solution.py:79
  (393 shorter events, 210.5 us)
Async XLA Ops:
  7.2 97.3 %all-gather.5.cloned.1.call-start = ((), (), s32[]{:S(2)}) async-start(), calls=%async_computation.1 | async-start | bytes 5570560 | tf_op jit(solution)/shard_map/all_gather | solution.py:1081
  13.1 158.0 %all-gather.7.cloned.1.call-start = ((), (), s32[]{:S(2)}) async-start(), calls=%async_computation.2 | async-start | bytes 8912896 | tf_op jit(solution)/shard_map/all_gather | solution.py:1082
  13.9 346.9 %reduce-scatter.2.cloned.1.call-start = ((), (), s32[]{:S(2)}) async-start(), calls=%async_computation.3 | async-start | bytes 13369344 | tf_op jit(solution)/shard_map/reduce_scatter | solution.py:1142
  14.1 19.1 %collective-permute-start = (bf16[80,384]{1,0:T(8,128)(2,1)S(1)}, bf16[80,384]{1,0:T(8,128)(2,1)S(1)}, u32[]{:S(2)}, u32[]{:S(2)}) collective-permute-start(bf16[80,384]{1,0:T(8,128)(2,1)S(1)} %get-tuple-element.342), channel_id=1, source_target_pairs={{0,24},{8,0},{16,8},{24,16},{32,56},{40,32},{48,40},{56,48},{64,88... | collective-permute-start | bytes 184328 | tf_op jit(solution)/shard_map/ppermute | solution.py:67
  17.5 15.8 %collective-permute-start.1 = (bf16[80,384]{1,0:T(8,128)(2,1)S(1)}, bf16[80,384]{1,0:T(8,128)(2,1)S(1)}, u32[]{:S(2)}, u32[]{:S(2)}) collective-permute-start(bf16[80,384]{1,0:T(8,128)(2,1)S(1)} %get-tuple-element.342), channel_id=1, source_target_pairs={{0,16},{8,24},{16,0},{24,8},{32,48},{40,56},{48,32},{56,40},{64,80... | collective-permute-start | bytes 184328 | tf_op jit(solution)/shard_map/ppermute | solution.py:67
  18.0 15.2 %collective-permute-start.2 = (bf16[80,384]{1,0:T(8,128)(2,1)S(1)}, bf16[80,384]{1,0:T(8,128)(2,1)S(1)}, u32[]{:S(2)}, u32[]{:S(2)}) collective-permute-start(bf16[80,384]{1,0:T(8,128)(2,1)S(1)} %get-tuple-element.342), channel_id=1, source_target_pairs={{0,8},{8,16},{16,24},{24,0},{32,40},{40,48},{48,56},{56,32},{64,72... | collective-permute-start | bytes 184328 | tf_op jit(solution)/shard_map/ppermute | solution.py:67
  71.8 27.1 %collective-permute-start.17 = (bf16[4,512,128]{2,1,0:T(8,128)(2,1)S(1)}, bf16[4,512,128]{2,1,0:T(8,128)(2,1)}, u32[]{:S(2)}, u32[]{:S(2)}) collective-permute-start(bf16[4,512,128]{2,1,0:T(8,128)(2,1)S(1)} %pad_maximum_fusion.2.kv0), channel_id=1, source_target_pairs={{0,32},{8,40},{16,48},{24,56},{32,64},{40,72},{48,80},{56,88},{64,... | collective-permute-start | bytes 1572872 | tf_op jit(solution)/shard_map/ppermute | solution.py:71
  106.2 26.1 %collective-permute-start.18 = (bf16[256,2048]{1,0:T(8,128)(2,1)S(1)}, bf16[256,2048]{1,0:T(8,128)(2,1)S(1)}, u32[]{:S(2)}, u32[]{:S(2)}) collective-permute-start(bf16[256,2048]{1,0:T(8,128)(2,1)S(1)} %out_project.3), channel_id=1, source_target_pairs={{0,1},{1,0},{2,3},{3,2},{4,5},{5,4},{6,7},{7,6},{8,9},{9,8},{10,11... | collective-permute-start | bytes 3145736 | tf_op jit(solution)/shard_map/ppermute | solution.py:79
  107.3 57.0 %collective-permute-start.25 = (f32[136,512]{1,0:T(8,128)S(1)}, f32[136,512]{1,0:T(8,128)S(1)}, u32[]{:S(2)}, u32[]{:S(2)}) collective-permute-start(f32[136,512]{1,0:T(8,128)S(1)} %get-tuple-element.188), channel_id=1, source_target_pairs={{0,120},{8,112},{16,104},{24,96},{32,88},{40,80},{48,72},{56,64},{... | collective-permute-start | bytes 835592 | tf_op jit(solution)/shard_map/ppermute | solution.py:83
  149.2 15.1 %collective-permute-start.22 = (bf16[64,2048]{1,0:T(8,128)(2,1)S(1)}, bf16[64,2048]{1,0:T(8,128)(2,1)S(1)}, u32[]{:S(2)}, u32[]{:S(2)}) collective-permute-start(bf16[64,2048]{1,0:T(8,128)(2,1)S(1)} %multiply_convert_fusion), channel_id=1, source_target_pairs={{0,6},{1,7},{2,0},{3,1},{4,2},{5,3},{6,4},{7,5},{8,14},{9,15},{10,... | collective-permute-start | bytes 786440 | tf_op jit(solution)/shard_map/ppermute | solution.py:75
  212.0 161.0 %all-gather.9.cloned.1.call-start = ((), (), s32[]{:S(2)}) async-start(), calls=%async_computation.4 | async-start | bytes 2359296 | tf_op jit(solution)/shard_map/all_gather | solution.py:1178
  217.9 15.4 %collective-permute-start.34 = (bf16[64,2048]{1,0:T(8,128)(2,1)S(1)}, bf16[64,2048]{1,0:T(8,128)(2,1)S(1)}, u32[]{:S(2)}, u32[]{:S(2)}) collective-permute-start(bf16[64,2048]{1,0:T(8,128)(2,1)S(1)} %fusion.33), channel_id=1, source_target_pairs={{0,2},{1,3},{2,4},{3,5},{4,6},{5,7},{6,0},{7,1},{8,10},{9,11},{10,... | collective-permute-start | bytes 786440 | tf_op jit(solution)/shard_map/ppermute | solution.py:75
  234.4 37.1 %collective-permute-start.39 = (bf16[256,2048]{1,0:T(8,128)(2,1)S(1)}, bf16[256,2048]{1,0:T(8,128)(2,1)S(1)}, u32[]{:S(2)}, u32[]{:S(2)}) collective-permute-start(bf16[256,2048]{1,0:T(8,128)(2,1)S(1)} %get-tuple-element.223), channel_id=1, source_target_pairs={{0,1},{1,0},{2,3},{3,2},{4,5},{5,4},{6,7},{7,6},{8,9},{9,8},{10,11... | collective-permute-start | bytes 3145736 | tf_op jit(solution)/shard_map/ppermute | solution.py:79
  257.9 25.4 %collective-permute-start.38 = (bf16[4,512,128]{2,1,0:T(8,128)(2,1)S(1)}, bf16[4,512,128]{2,1,0:T(8,128)(2,1)S(1)}, u32[]{:S(2)}, u32[]{:S(2)}) collective-permute-start(bf16[4,512,128]{2,1,0:T(8,128)(2,1)S(1)} %get-tuple-element.222), channel_id=1, source_target_pairs={{0,64},{8,72},{16,80},{24,88},{32,96},{40,104},{48,112},{56,120},{... | collective-permute-start | bytes 1572872 | tf_op jit(solution)/shard_map/ppermute | solution.py:71
  271.4 27.5 %collective-permute-start.37 = (bf16[4,512,128]{2,1,0:T(8,128)(2,1)S(1)}, bf16[4,512,128]{2,1,0:T(8,128)(2,1)}, u32[]{:S(2)}, u32[]{:S(2)}) collective-permute-start(bf16[4,512,128]{2,1,0:T(8,128)(2,1)S(1)} %get-tuple-element.220), channel_id=1, source_target_pairs={{0,32},{8,40},{16,48},{24,56},{32,64},{40,72},{48,80},{56,88},{64,... | collective-permute-start | bytes 1572872 | tf_op jit(solution)/shard_map/ppermute | solution.py:71
  295.2 15.8 %collective-permute-start.43 = (bf16[4,512,128]{2,1,0:T(8,128)(2,1)S(1)}, bf16[4,512,128]{2,1,0:T(8,128)(2,1)}, u32[]{:S(2)}, u32[]{:S(2)}) collective-permute-start(bf16[4,512,128]{2,1,0:T(8,128)(2,1)S(1)} %get-tuple-element.233), channel_id=1, source_target_pairs={{0,96},{8,104},{16,112},{24,120},{32,0},{40,8},{48,16},{56,24},{64... | collective-permute-start | bytes 1572872 | tf_op jit(solution)/shard_map/ppermute | solution.py:71
  310.9 125.8 %all-gather.11.cloned.1.call-start = ((), (), s32[]{:S(2)}) async-start(), calls=%async_computation.5 | async-start | bytes 2359296 | tf_op jit(solution)/shard_map/all_gather | solution.py:1228
  312.5 16.1 %collective-permute-start.44 = (bf16[512,128]{1,0:T(8,128)(2,1)S(1)}, bf16[512,128]{1,0:T(8,128)(2,1)S(1)}, u32[]{:S(2)}, u32[]{:S(2)}) collective-permute-start(bf16[512,128]{1,0:T(8,128)(2,1)S(1)} %get-tuple-element.329), channel_id=1, source_target_pairs={{0,8},{8,16},{16,24},{24,0},{32,40},{40,48},{48,56},{56,32},{64,72... | collective-permute-start | bytes 393224 | tf_op jit(solution)/shard_map/ppermute | solution.py:67
  339.4 16.0 %collective-permute-start.54 = (bf16[256,2048]{1,0:T(8,128)(2,1)S(1)}, bf16[256,2048]{1,0:T(8,128)(2,1)S(1)}, u32[]{:S(2)}, u32[]{:S(2)}) collective-permute-start(bf16[256,2048]{1,0:T(8,128)(2,1)S(1)} %get-tuple-element.246), channel_id=1, source_target_pairs={{0,1},{1,0},{2,3},{3,2},{4,5},{5,4},{6,7},{7,6},{8,9},{9,8},{10,11... | collective-permute-start | bytes 3145736 | tf_op jit(solution)/shard_map/ppermute | solution.py:79
  344.1 16.0 %collective-permute-start.48 = (bf16[4,64,640]{2,1,0:T(8,128)(2,1)S(1)}, bf16[4,64,640]{2,1,0:T(8,128)(2,1)S(1)}, u32[]{:S(2)}, u32[]{:S(2)}) collective-permute-start(bf16[4,64,640]{2,1,0:T(8,128)(2,1)S(1)} %get-tuple-element.314), channel_id=1, source_target_pairs={{0,32},{8,40},{16,48},{24,56},{32,64},{40,72},{48,80},{56,88},{64,... | collective-permute-start | bytes 983048 | tf_op jit(solution)/shard_map/ppermute | solution.py:71
  351.6 19.2 %collective-permute-start.49 = (bf16[4,64,640]{2,1,0:T(8,128)(2,1)}, bf16[4,64,640]{2,1,0:T(8,128)(2,1)}, u32[]{:S(2)}, u32[]{:S(2)}) collective-permute-start(bf16[4,64,640]{2,1,0:T(8,128)(2,1)} %get-tuple-element.313), channel_id=1, source_target_pairs={{0,64},{8,72},{16,80},{24,88},{32,96},{40,104},{48,112},{56,120},{... | collective-permute-start | bytes 983048 | tf_op jit(solution)/shard_map/ppermute | solution.py:71
  351.6 19.2 %collective-permute-start.50 = (bf16[4,64,640]{2,1,0:T(8,128)(2,1)}, bf16[4,64,640]{2,1,0:T(8,128)(2,1)}, u32[]{:S(2)}, u32[]{:S(2)}) collective-permute-start(bf16[4,64,640]{2,1,0:T(8,128)(2,1)} %get-tuple-element.312), channel_id=1, source_target_pairs={{0,96},{8,104},{16,112},{24,120},{32,0},{40,8},{48,16},{56,24},{64... | collective-permute-start | bytes 983048 | tf_op jit(solution)/shard_map/ppermute | solution.py:71
  355.0 15.8 %collective-permute-start.51 = (bf16[4,64,640]{2,1,0:T(8,128)(2,1)}, bf16[4,64,640]{2,1,0:T(8,128)(2,1)}, u32[]{:S(2)}, u32[]{:S(2)}) collective-permute-start(bf16[4,64,640]{2,1,0:T(8,128)(2,1)} %get-tuple-element.311), channel_id=1, source_target_pairs={{0,8},{8,16},{16,24},{24,0},{32,40},{40,48},{48,56},{56,32},{64,72... | collective-permute-start | bytes 983048 | tf_op jit(solution)/shard_map/ppermute | solution.py:67
  355.5 17.5 %collective-permute-start.52 = (bf16[4,64,640]{2,1,0:T(8,128)(2,1)}, bf16[4,64,640]{2,1,0:T(8,128)(2,1)}, u32[]{:S(2)}, u32[]{:S(2)}) collective-permute-start(bf16[4,64,640]{2,1,0:T(8,128)(2,1)} %get-tuple-element.310), channel_id=1, source_target_pairs={{0,16},{8,24},{16,0},{24,8},{32,48},{40,56},{48,32},{56,40},{64,80... | collective-permute-start | bytes 983048 | tf_op jit(solution)/shard_map/ppermute | solution.py:67
  (115 other events, 1291.8 us)
Sparse Core Ops, SparseCore 0:
  13.3 74.0 all-gather.4
  90.0 75.5 all-gather.6
  212.1 122.3 reduce-scatter.1
  336.1 24.8 all-gather.8
  405.9 27.2 all-gather.10
where the time goes:
time: 457 us; the launch traced here: 448 us
  Pallas kernels  135 us (30%)
  starting transfers between devices  125 us (27%)
  waiting for transfers between devices  118 us (26%)
  local copies, waits for them, and re-layouts  28.3 us (6%)
  other arithmetic  21.1 us (5%)
  between operations  20.3 us (4%)
    pallas_call x4, Pallas kernels, attend_back(): pl.pallas_call(functools.partial(backward_kernel, first, last, count), in...  36.9 us
    ppermute x21, waiting for transfers between devices, from_y(): return lax.ppermute(a, 'dp', perm_y(k))  36.1 us
    ppermute x21, starting transfers between devices, from_x(): return lax.ppermute(a, 'dp', perm_x(k))  32 us
    ppermute x21, waiting for transfers between devices, from_z(): return lax.ppermute(a, 'tensor', perm_z(k))  30.7 us
    ppermute x21, starting transfers between devices, from_y(): return lax.ppermute(a, 'dp', perm_y(k))  29.3 us
    ppermute x21, waiting for transfers between devices, from_x(): return lax.ppermute(a, 'dp', perm_x(k))  27.4 us
    ppermute x4, starting transfers between devices, from_partner(): return lax.ppermute(a, 'dp', PERM_PARTNER)  25.1 us
    ppermute x21, starting transfers between devices, from_z(): return lax.ppermute(a, 'tensor', perm_z(k))  23.8 us
  transfers between devices with their start and end apart: 79, of which 36 were waited for; matrix products, arithmetic and copies ran while one was open for 4% of the time, Pallas kernels for 26%

commit v1 on v0

--- a/solution.py
+++ b/solution.py
@@ -28,7 +28,6 @@
 BF16 = jnp.bfloat16
 OFF = -1e5
 VMEM_LIMIT = 50 * 1024 * 1024
-BACK_US = 8
 
 
 def inverse_rms(array_in):
@@ -87,15 +86,14 @@
     return lax.optimization_barrier((arrays, work))
 
 
-def gather_both(u, v, later):
+def gather_both(u, v):
     row = {k: from_x(u, k) for k in (2, 1, 3)}
     column = {k: from_y(v, k) for k in (2, 1, 3)}
-    (row, column), later = beside((row, column), later)
     row = jnp.stack([u, row[1], row[2], row[3]])
     column = jnp.stack([v, column[1], column[2], column[3]])
     second = {k: (from_y(row, k), from_x(column, k)) for k in (2, 1, 3)}
     first = [row] + [second[k][0] for k in (1, 2, 3)]
-    return first, [column] + [second[k][1] for k in (1, 2, 3)], later
+    return first, [column] + [second[k][1] for k in (1, 2, 3)]
 
 
 def gather_dp(a, later):
@@ -121,10 +119,7 @@
 
 
 def scatter_tensor(near, far, work=None):
-    return scatter_ring(near.astype(F32) + from_core(far.astype(BF16)).astype(F32), work)
-
-
-def scatter_ring(near, work=None):
+    near = near.astype(F32) + from_core(far.astype(BF16)).astype(F32)
     parts = near.reshape(4, CH, near.shape[-1])
     low = parts.astype(BF16)
     got = {k: from_z(low[k], -k) for k in (2, 1, 3)}
@@ -524,13 +519,10 @@
     )(*given)
 
 
-def backward_kernel(first, last, count, blk_ref, q_t, do_t, q_pad, do_pad, kv_all, kinfo_ref, qinfo_ref, *rest):
-    dq_t, total = rest[-2:]
-    outs = rest[-2 - count : -2]
-    if first:
-        dq_t[...] = jnp.zeros_like(dq_t)
-    else:
-        dq_t[...] = rest[0][...]
+def backward_kernel(
+    blk_ref, q_t, do_t, q_pad, do_pad, kv_all, kinfo_ref, qinfo_ref, own_ref, other_ref, u_ref, v_ref, dq_t, total
+):
+    dq_t[...] = jnp.zeros_like(dq_t)
     keep_k, keep_v = lane_masks()
     keep_v_masked = jnp.where(lane_of((1, 128)) == 67, 0.0, keep_v.astype(F32)).astype(BF16)
 
@@ -538,7 +530,7 @@
         total[...] = jnp.zeros_like(total)
 
         def work(queries, masked, is_own):
-            kv = kv_all[blk_ref[4 * count + 2 + slot]]
+            kv = kv_all[slot]
             keys = kv * keep_k + (keep_v_masked if masked else keep_v)
             vals = kv * keep_v + keep_k
             keys_turned = kv.astype(F32).T[:64, :].astype(BF16)
@@ -557,85 +549,78 @@
                     keys_turned, grads, preferred_element_type=F32
                 )
 
-        for_queries(blk_ref, slot, 4 * count, 2, work)
-
-        for index, ref in enumerate(outs):
-
-            @pl.when(slot // 4 == index)
-            def _(index=index, ref=ref):
-                ref[slot - 4 * index] = total[...].astype(BF16)
-
+        for_queries(blk_ref, slot, 16, 2, work)
+        u_ref[slot // 4, slot % 4] = total[:256].astype(BF16)
+        v_ref[slot % 4, slot // 4] = total[256:].astype(BF16)
         return carry
 
-    lax.fori_loop(0, 4 * count, step, 0)
-    if last:
-        dq = (dq_t[...].T * 0.125).astype(BF16)
-        rest[1][...] = dq[:, :128]
-        rest[2][...] = dq[:, 128:]
-
-
-def attend_back(first, last, count, blocks, operands, kv, kinfo, qinfo, dq=None):
-    given = [*operands, kv, kinfo, qinfo] + ([] if first else [dq])
-    dkv = [shape((4, ROWS, 128), BF16)] * count
+    lax.fori_loop(0, 16, step, 0)
+    dq = (dq_t[...].T * 0.125).astype(BF16)
+    own_ref[...] = dq[:, :128]
+    other_ref[...] = dq[:, 128:]
+
+
+def attend_back(blocks, operands, kv, kinfo, qinfo):
     pair = shape((ROWS, 128), BF16)
-    outs = [pair, pair] + dkv if last else dkv + [shape((256, ROWS), F32)]
-    return pl.pallas_call(
-        functools.partial(backward_kernel, first, last, count),
-        in_specs=[pl.BlockSpec(memory_space=pltpu.SMEM)] + vmem_specs(len(given)),
-        out_specs=vmem_specs(len(outs)),
-        out_shape=outs,
-        scratch_shapes=([pltpu.VMEM((256, ROWS), F32)] if last else [])
-        + [pltpu.VMEM((ROWS, 128), F32)],
+    half = shape((4, 4, 256, 128), BF16)
+    return pl.pallas_call(
+        backward_kernel,
+        in_specs=[pl.BlockSpec(memory_space=pltpu.SMEM)] + vmem_specs(7),
+        out_specs=vmem_specs(4),
+        out_shape=[pair, pair, half, half],
+        scratch_shapes=[pltpu.VMEM((256, ROWS), F32), pltpu.VMEM((ROWS, 128), F32)],
         compiler_params=params(),
         name="attend_back",
-        cost_estimate=takes(BACK_US * count),
-    )(blocks, *given)
-
-
-def heads_back_kernel(proj_ref, own_ref, other_ref, kv_ref, cos_ref, sin_ref, gain_ref, out_ref, sum_ref):
+        cost_estimate=takes(36),
+    )(blocks, *operands, kv, kinfo, qinfo)
+
+
+def heads_back_kernel(pairs, proj_ref, *refs):
+    grads = refs[: len(pairs)]
+    cos_ref, sin_ref, gain_ref, out_ref, sum_ref = refs[len(pairs) :]
     lane = lane_of((proj_ref.shape[0], 128))
     low_half = lane < 64
     first = (lane & 63) < 32
     cosine = cos_ref[...]
     sine = jnp.where(first, sin_ref[...], -sin_ref[...])
-    sums = []
-    for pair in range(3):
-        at = slice(pair * 128, (pair + 1) * 128)
-        u = proj_ref[:, at]
-        grad = (own_ref, other_ref, kv_ref)[pair][...].astype(F32)
+    sums = None
+    for index, pair in enumerate(pairs):
+        u = proj_ref[:, pair * 128 : (pair + 1) * 128]
+        grad = grads[index][...].astype(F32)
         scale = lax.rsqrt(head_sums(u * u, low_half) * (1.0 / HD) + EPS_NORM)
         hat = u * scale
         turned = grad * cosine + turn(grad, first) * sine
-        sums.append(jnp.sum(turned * hat, axis=0, keepdims=True))
+        part = jnp.sum(turned * hat, axis=0, keepdims=True)
+        sums = part if sums is None else sums + part
         grad_hat = turned * gain_ref[pair // 2 : pair // 2 + 1, :]
         mean = head_sums(grad_hat * hat, low_half) * (1.0 / HD)
         back = scale * (grad_hat - hat * mean)
         if pair == 2:
             back = jnp.where(low_half, back, grad)
-        out_ref[:, at] = back.astype(BF16)
+        out_ref[:, index * 128 : (index + 1) * 128] = back.astype(BF16)
 
     @pl.when(pl.program_id(0) == 0)
     def _():
         sum_ref[...] = jnp.zeros_like(sum_ref)
 
-    sum_ref[0:1, :] += sums[0] + sums[1]
-    sum_ref[1:2, :] += sums[2]
-
-
-def heads_back(proj, own, other, kv, cosine, sine, gains):
+    sum_ref[0:1, :] += sums
+
+
+def heads_back(pairs, proj, grads, cosine, sine, gains):
     tile = 128
     row = lambda width: pl.BlockSpec((tile, width), lambda i: (i, 0))
     whole = pl.BlockSpec((8, 128), lambda i: (0, 0))
-    return pl.pallas_call(
-        heads_back_kernel,
+    wide = 128 * len(pairs)
+    return pl.pallas_call(
+        functools.partial(heads_back_kernel, pairs),
         grid=(ROWS // tile,),
-        in_specs=[row(384), row(128), row(128), row(128), row(128), row(128), whole],
-        out_specs=[row(384), whole],
-        out_shape=[shape((ROWS, 384), BF16), shape((8, 128), F32)],
+        in_specs=[row(384)] + [row(128)] * (len(pairs) + 2) + [whole],
+        out_specs=[row(wide), whole],
+        out_shape=[shape((ROWS, wide), BF16), shape((8, 128), F32)],
         compiler_params=params(),
         name="heads_back",
-        cost_estimate=takes(2),
-    )(proj, own, other, kv, cosine, sine, gains)
+        cost_estimate=takes(len(pairs)),
+    )(proj, *grads, cosine, sine, gains)
 
 
 def out_kernel(mixed_ref, w_ref, out_ref):
@@ -659,63 +644,59 @@
 
 
 def ffn_kernel(
-    near_ref, far_ref, grad_ref, gate_w, up_w, rows_w, act_ref, gate_ref, up_ref, near_out, far_out, x_all, both
+    near_ref, far_ref, grad_ref, w_in, act_ref, gate_ref, up_ref, near_out, far_out, w, x_all, both, sems
 ):
-    step = pl.program_id(0)
-
-    @pl.when(step == 0)
-    def _():
-        x_all[:256] = near_ref[...]
-        x_all[256:] = far_ref[...]
-
+    tiles = []
     for tile in range(4):
-
-        @pl.when(step == tile)
-        def _(tile=tile):
-            x = x_all[...]
-            gate = jnp.dot(x, gate_w[...], preferred_element_type=F32)
-            up = jnp.dot(x, up_w[...], preferred_element_type=F32)
-            inner = grad_ref[...]
-            sigmoid = jax.nn.sigmoid(gate)
-            activated = gate * sigmoid
-            act_ref[...] = (activated * up).astype(BF16)
-            grad_gate = (inner * up * sigmoid * (1.0 + gate * (1.0 - sigmoid))).astype(BF16)
-            grad_up = (inner * activated).astype(BF16)
-            gate_ref[...] = grad_gate
-            up_ref[...] = grad_up
-            both[:, tile * 256 : (tile + 1) * 256] = grad_gate
-            both[:, 1024 + tile * 256 : 1024 + (tile + 1) * 256] = grad_up
-
-    @pl.when(step >= 4)
-    def _():
-        part = dot_cols(both[...], rows_w[...])
-        near_out[...] = part[:256]
-        far_out[...] = part[256:].astype(BF16)
+        at = (slice(tile * 256, (tile + 1) * 256), slice(1024 + tile * 256, 1024 + (tile + 1) * 256))
+        pair = [
+            pltpu.make_async_copy(w_in.at[:, part], w.at[:, part], sems.at[2 * tile + i])
+            for i, part in enumerate(at)
+        ]
+        for copy in pair:
+            copy.start()
+        tiles.append((at, pair))
+    x_all[:256] = near_ref[...]
+    x_all[256:] = far_ref[...]
+    for (gate_at, up_at), pair in tiles:
+        for copy in pair:
+            copy.wait()
+        x = x_all[...]
+        gate = jnp.dot(x, w[:, gate_at], preferred_element_type=F32)
+        up = jnp.dot(x, w[:, up_at], preferred_element_type=F32)
+        inner = grad_ref[:, gate_at]
+        sigmoid = jax.nn.sigmoid(gate)
+        activated = gate * sigmoid
+        act_ref[:, gate_at] = (activated * up).astype(BF16)
+        grad_gate = (inner * up * sigmoid * (1.0 + gate * (1.0 - sigmoid))).astype(BF16)
+        grad_up = (inner * activated).astype(BF16)
+        gate_ref[:, gate_at] = grad_gate
+        up_ref[:, gate_at] = grad_up
+        both[:, gate_at] = grad_gate
+        both[:, up_at] = grad_up
+    for tile in range(4):
+        at = slice(tile * 512, (tile + 1) * 512)
+        part = dot_cols(both[...], w[at, :])
+        near_out[:, at] = part[:256]
+        far_out[:, at] = part[256:].astype(BF16)
 
 
 def feed_forward(near, far, grad_inner, gate_up):
-    whole = lambda dims: pl.BlockSpec(dims, lambda j: (0, 0))
-    tile = pl.BlockSpec((ROWS, 256), lambda j: (0, jnp.minimum(j, 3)))
-    last = lambda j: jnp.maximum(j - 4, 0)
     return pl.pallas_call(
         ffn_kernel,
-        grid=(8,),
-        in_specs=[
-            whole((256, D)),
-            whole((256, D)),
-            tile,
-            pl.BlockSpec((D, 256), lambda j: (0, jnp.minimum(j, 3))),
-            pl.BlockSpec((D, 256), lambda j: (0, 4 + jnp.minimum(j, 3))),
-            pl.BlockSpec((512, 2048), lambda j: (last(j), 0)),
+        in_specs=vmem_specs(3) + [pl.BlockSpec(memory_space=pl.ANY)],
+        out_specs=vmem_specs(5),
+        out_shape=[shape((ROWS, 1024), BF16)] * 3 + [shape((256, D), F32), shape((256, D), BF16)],
+        scratch_shapes=[
+            pltpu.VMEM((D, 2048), BF16),
+            pltpu.VMEM((ROWS, D), BF16),
+            pltpu.VMEM((ROWS, 2048), BF16),
+            pltpu.SemaphoreType.DMA((8,)),
         ],
-        out_specs=[tile, tile, tile]
-        + [pl.BlockSpec((256, 512), lambda j: (0, last(j)))] * 2,
-        out_shape=[shape((ROWS, 1024), BF16)] * 3 + [shape((256, D), F32), shape((256, D), BF16)],
-        scratch_shapes=[pltpu.VMEM((ROWS, D), BF16), pltpu.VMEM((ROWS, 2048), BF16)],
         compiler_params=params(),
         name="feed_forward",
         cost_estimate=takes(13),
-    )(near, far, grad_inner, gate_up, gate_up, gate_up)
+    )(near, far, grad_inner, gate_up)
 
 
 def inner_grad_kernel(dy_ref, w_ref, out_ref):
@@ -797,35 +778,88 @@
     )(blocks, near, far, mixed)
 
 
-def qkv_out_grad_kernel(blk_ref, across_ref, grad_ref, parts_ref, u_ref, v_ref):
+def query_out_grad_kernel(blk_ref, across_ref, grad_ref, parts_ref, out_ref):
+    grad = grad_ref[...]
+    for slot in range(16):
+        at = pl.ds(pl.multiple_of(blk_ref[slot] * 128, 128), 128)
+        part = jnp.dot(across_ref[at, :], grad, preferred_element_type=F32)
+        out_ref[slot // 4, slot % 4, :, :256] = part.astype(BF16)
+        out_ref[slot // 4, slot % 4, :, 256:] = parts_ref[slot // 4, slot % 4]
+
+
+def query_out_grad(blocks, across, grad, out_parts):
+    return pl.pallas_call(
+        query_out_grad_kernel,
+        in_specs=[pl.BlockSpec(memory_space=pltpu.SMEM)] + vmem_specs(3),
+        out_specs=vmem_specs(1)[0],
+        out_shape=shape((4, 4, 128, 512), BF16),
+        compiler_params=params(),
+        name="query_out_grad",
+        cost_estimate=takes(2),
+    )(blocks, across, grad, out_parts)
+
+
+def key_grad_kernel(blk_ref, across_ref, grad_ref, parts_ref, u_ref, v_ref):
     grad = grad_ref[...]
     for slot in range(16):
         at_y, at_x = slot // 4, slot % 4
         at = pl.ds(pl.multiple_of(blk_ref[slot] * 128, 128), 128)
         part = jnp.dot(across_ref[at, :], grad, preferred_element_type=F32).astype(BF16)
-        u_ref[at_y, at_x, :, :384] = part[:64]
-        u_ref[at_y, at_x, :, 384:] = parts_ref[at_y, at_x, :64]
-        v_ref[at_x, at_y, :, :384] = part[64:]
-        v_ref[at_x, at_y, :, 384:] = parts_ref[at_y, at_x, 64:]
-
-
-def qkv_out_grad(blocks, across, grad, out_parts):
-    return pl.pallas_call(
-        qkv_out_grad_kernel,
+        u_ref[at_y, at_x, :, :512] = parts_ref[at_y, at_x, :64]
+        u_ref[at_y, at_x, :, 512:] = part[:64]
+        v_ref[at_x, at_y, :, :512] = parts_ref[at_y, at_x, 64:]
+        v_ref[at_x, at_y, :, 512:] = part[64:]
+
+
+def key_grad(blocks, across, grad, parts):
+    return pl.pallas_call(
+        key_grad_kernel,
         in_specs=[pl.BlockSpec(memory_space=pltpu.SMEM)] + vmem_specs(3),
         out_specs=vmem_specs(2),
         out_shape=[shape((4, 4, 64, 640), BF16)] * 2,
         compiler_params=params(),
-        name="qkv_out_grad",
-        cost_estimate=takes(3),
-    )(blocks, across, grad, out_parts)
-
-
-def attn_back_kernel(grad_ref, w_ref, x_ref, near_ref, far_ref, gain_ref):
+        name="key_grad",
+        cost_estimate=takes(2),
+    )(blocks, across, grad, parts)
+
+
+def attn_back_kernel(grad_ref, w_ref, x_ref, part_ref, gain_ref):
+    step = pl.program_id(0)
+    part = dot_cols(grad_ref[...], w_ref[...])
+    part_ref[...] = part.astype(BF16)
+    x = x_ref[...].astype(F32)
+    sums = jnp.sum(part * (x * inverse_rms(x)), axis=0, keepdims=True)
+
+    @pl.when(step == 0)
+    def _():
+        gain_ref[...] = sums
+
+    @pl.when(step > 0)
+    def _():
+        gain_ref[...] += sums
+
+
+def attn_back(grad, w, x):
+    tile = 128
+    row = lambda width: pl.BlockSpec((tile, width), lambda i: (i, 0))
+    return pl.pallas_call(
+        attn_back_kernel,
+        grid=(4,),
+        in_specs=[row(256), pl.BlockSpec((D, 256), lambda i: (0, 0)), row(D)],
+        out_specs=[row(D), pl.BlockSpec((1, D), lambda i: (0, 0))],
+        out_shape=[shape((ROWS, D), BF16), shape((1, D), F32)],
+        compiler_params=params(),
+        name="attn_back",
+        cost_estimate=takes(5),
+    )(grad, w, x)
+
+
+def attn_back_rest_kernel(row_ref, grad_ref, w_ref, x_ref, part_ref, out_ref, gain_ref):
     step = pl.program_id(0)
     part = dot_cols(grad_ref[...], w_ref[...])
     x = x_ref[...].astype(F32)
     sums = jnp.sum(part * (x * inverse_rms(x)), axis=0, keepdims=True)
+    part = (part + part_ref[...].astype(F32)).astype(BF16)
 
     @pl.when(step == 0)
     def _():
@@ -835,36 +869,30 @@
     def _():
         gain_ref[...] += sums
 
-    @pl.when(step < 2)
-    def _():
-        far_ref[...] = part.astype(BF16)
-
-    @pl.when(step >= 2)
-    def _():
-        near_ref[...] = part
-
-
-def attn_back(grad, w, x):
+    for half in range(2):
+        at = pl.multiple_of(row_ref[2 * step + half] * CH, CH)
+        out_ref[pl.ds(at, CH), :] = part[half * CH : (half + 1) * CH]
+
+
+def attn_back_rest(row_table, grad, w, x, part):
     tile = 128
-    turn_rows = lambda i: ((i + 2) % 4, 0)
-    return pl.pallas_call(
-        attn_back_kernel,
-        grid=(4,),
-        in_specs=[
-            pl.BlockSpec((tile, 384), turn_rows),
-            pl.BlockSpec((D, 384), lambda i: (0, 0)),
-            pl.BlockSpec((tile, D), turn_rows),
-        ],
-        out_specs=[
-            pl.BlockSpec((tile, D), lambda i: (jnp.maximum(i - 2, 0), 0)),
-            pl.BlockSpec((tile, D), lambda i: (jnp.minimum(i, 1), 0)),
-            pl.BlockSpec((1, D), lambda i: (0, 0)),
-        ],
-        out_shape=[shape((256, D), F32), shape((256, D), BF16), shape((1, D), F32)],
-        compiler_params=params(),
-        name="attn_back",
-        cost_estimate=takes(6),
-    )(grad, w, x)
+    row = lambda width: pl.BlockSpec((tile, width), lambda i, r: (i, 0))
+    return pl.pallas_call(
+        attn_back_rest_kernel,
+        grid_spec=pltpu.PrefetchScalarGridSpec(
+            num_scalar_prefetch=1,
+            grid=(4,),
+            in_specs=[row(128), pl.BlockSpec((D, 128), lambda i, r: (0, 2)), row(D), row(D)],
+            out_specs=[
+                pl.BlockSpec((ROWS, D), lambda i, r: (0, 0)),
+                pl.BlockSpec((1, D), lambda i, r: (0, 0)),
+            ],
+        ),
+        out_shape=[shape((ROWS, D), BF16), shape((1, D), F32)],
+        compiler_params=params(),
+        name="attn_back_rest",
+        cost_estimate=takes(4),
+    )(row_table, grad, w, x, part)
 
 
 def weight_grad_kernel(parts, wide, *refs):
@@ -914,6 +942,24 @@
         name="weight_grad",
         cost_estimate=takes(1.25 * sum(wide)),
     )(*given)
+
+
+def keep_kernel(in_ref, out_ref):
+    out_ref[...] = in_ref[...]
+
+
+def keep(a):
+    block = pl.BlockSpec((128, D), lambda i: (i, 0))
+    return pl.pallas_call(
+        keep_kernel,
+        grid=(4,),
+        in_specs=[block],
+        out_specs=block,
+        out_shape=shape((ROWS, D), BF16),
+        compiler_params=params(),
+        name="keep",
+        cost_estimate=takes(2),
+    )(a)
 
 
 def step_kernel(wide, *refs):
@@ -1031,7 +1077,9 @@
 
 
 def in_order(a, row_table):
-    return jnp.concatenate([lax.dynamic_slice_in_dim(a, row_table[j] * CH, CH, 0) for j in range(8)])
+    chunks = a.reshape(8, CH)
+    pick = row_table[:, None, None] == jnp.arange(8, dtype=jnp.int32)[None, :, None]
+    return jnp.sum(jnp.where(pick, chunks[None], 0), axis=1).reshape(ROWS)
 
 
 def local(
@@ -1060,9 +1108,7 @@
     seg_low = jnp.concatenate([segments >> 6, segments & 63]).astype(BF16).reshape(4, 256)
     seg_low = jnp.pad(seg_low, ((0, 12), (0, 128)))
     qkv_low = weight_qkv.astype(BF16)
-    w_first, w_second, tokens = gather_both(
-        jnp.concatenate([qkv_low[:64], seg_low], axis=0), qkv_low[64:], tokens
-    )
+    w_first, w_second = gather_both(jnp.concatenate([qkv_low[:64], seg_low], axis=0), qkv_low[64:])
 
     dp = lax.axis_index("dp")
     tensor = lax.axis_index("tensor")
@@ -1102,7 +1148,9 @@
     )
 
     def block_segs(slot):
-        got = lax.dynamic_slice(all_segs, (slot, 0, 0), (1, 4, 256)).astype(jnp.int32).reshape(2, ROWS)
+        pick = (sixteen == slot)[:, None, None]
+        got = jnp.sum(jnp.where(pick, all_segs[:, :4, :256].astype(jnp.int32), 0), axis=0)
+        got = got.reshape(2, ROWS)
         return got[0] * 64 + got[1]
 
     partner_segs = block_segs(partner_slot)
@@ -1120,8 +1168,9 @@
             jnp.zeros((6, ROWS), F32),
         ]
     )
+    block_info = jnp.concatenate([blocks, own_blocks])
     mixed, out_own, log_own, out_send, kv_all = attend(
-        jnp.concatenate([blocks, own_blocks]), q_own, q_send, kv_groups, kinfo, qinfo, bias
+        block_info, q_own, q_send, kv_groups, kinfo, qinfo, bias
     )
 
     far = out_project(1, mixed, down_out, BF16)
@@ -1148,78 +1197,47 @@
     do_own, do_send = mixed_grad(*grad_attn, down_out)
     do_other = from_partner(do_send)
     out_parts = out_grad(blocks, *grad_attn, mixed)
-    do_other, out_parts = beside(do_other, out_parts)
-    ffn_far = from_core(ffn_far)
-    operands = ready(do_own, do_other, out_own, log_own, out_other, q_own, q_other, bias)
-
-    def back_groups(groups, first, last, state):
-        info = jnp.concatenate(
-            [blocks[4 * k : 4 * k + 4] for k in groups]
-            + [own_blocks]
-            + [sixteen[4 * k : 4 * k + 4] for k in groups]
-        )
-        return attend_back(first, last, len(groups), info, operands, kv_all, kinfo, qinfo, state)
-
-    got = {}
-    part, state = back_groups((2,), True, False, None)
-    got[2] = from_y(part, -2)
-    part, state = back_groups((1,), False, False, state)
-    got[1] = from_y(part, -1)
-    (got[2], ffn_far), state = beside((got[2], ffn_far), state)
+    (do_other, ffn_far), out_parts = beside((do_other, from_core(ffn_far)), out_parts)
     ffn_near = (ffn_near + ffn_far.astype(F32)).reshape(4, CH, D)
     ffn_low = ffn_near.astype(BF16)
     ffn_got = {k: from_z(ffn_low[k], -k) for k in (2, 1, 3)}
-    part, state = back_groups((3,), False, False, state)
-    got[3] = from_y(part, -3)
-    (got[1], ffn_got), state = beside((got[1], ffn_got), state)
-    dq_own, dq_send, own_part = back_groups((0,), False, True, state)
+    operands = ready(do_own, do_other, out_own, log_own, out_other, q_own, q_other, bias)
+    dq_own, dq_send, part_u, part_v = attend_back(block_info, operands, kv_all, kinfo, qinfo)
+    dq_send, ffn_got = beside(dq_send, ffn_got)
     dq_other = from_partner(dq_send)
+    part_v, dq_other = beside(part_v, dq_other)
+    got_u, got_v = send(part_u, from_y), send(part_v, from_x)
+    grad_query, gain_query = heads_back(
+        (0, 1), projected, [dq_own, dq_other], cosine, sine, gain_rows
+    )
+    parts = query_out_grad(blocks, across, grad_query, out_parts)
+    attn_part, gain_attn = attn_back(grad_query, full_qkv, x_rows)
+    (got_u, got_v), (parts, attn_part) = beside((got_u, got_v), (parts, attn_part))
     block_rows = (hidden_one + sum_four(ffn_near[0], ffn_got)).astype(BF16)
-    block_out = lax.all_gather(block_rows, "tensor", axis=0, tiled=True)
-
-    line = sum_four(own_part, got)
-    low = line.astype(BF16)
-    got = {k: from_x(low[k], -k) for k in (2, 1, 3)}
-    got, dq_other = beside(got, dq_other)
-    grad_kv = sum_four(line[0], got).astype(BF16)
-    grad_projected, gain_heads = heads_back(
-        projected, dq_own, dq_other, grad_kv, cosine, sine, gain_rows
-    )
-    parts_u, parts_v = qkv_out_grad(blocks, across, grad_projected, out_parts)
+    line_u, line_v = sum_four(part_u[0], got_u), sum_four(part_v[0], got_v)
+    low_u, low_v = line_u.astype(BF16), line_v.astype(BF16)
+    got_u = {k: from_x(low_u[k], -k) for k in (2, 1, 3)}
+    got_v = {k: from_y(low_v[k], -k) for k in (2, 1, 3)}
+    grad_kv = jnp.concatenate([sum_four(line_u[0], got_u), sum_four(line_v[0], got_v)]).astype(BF16)
+    grad_kv, gain_key = heads_back((2,), projected, [grad_kv], cosine, sine, gain_rows)
+    parts_u, parts_v = key_grad(blocks, across, grad_kv, parts)
     got_u, got_v = send(parts_u, from_y), send(parts_v, from_x)
 
+    grad_kv, _ = beside(grad_kv, (parts_u, parts_v))
+    block_out = keep(lax.all_gather(block_rows, "tensor", axis=0, tiled=True))
+    partial, gain_rest = attn_back_rest(row_table, grad_kv, full_qkv, x_rows, attn_part)
+    partial, grads = beside(partial, grads)
+    grad_attn_in = lax.psum_scatter(partial, "tensor", scatter_dimension=0, tiled=True).astype(F32)
     (gate_up_step, down_step), later_squares = take_step(
         [grads],
         [(weight_gate_up, first_gate_up, second_gate_up), (weight_down, first_down, second_down)],
         ((0, 0, 1024, False, 2), (0, 2048, 1024, True, 3)),
     )
-    grad_projected, _ = beside(grad_projected, (parts_u, parts_v))
-    near, far, gain_attn = attn_back(grad_projected, full_qkv, x_rows)
-    near = near + from_core(far).astype(F32)
-    (got_u, got_v), (near, later_squares, block_out) = beside(
-        (got_u, got_v), (near, later_squares, block_out)
-    )
-    late_grad = jnp.concatenate(
-        [scatter_rest(parts_u[0], got_u, from_x), scatter_rest(parts_v[0], got_v, from_y)]
-    )
-    (qkv_step, out_step), qkv_squares = take_step(
-        [late_grad],
-        [(weight_qkv, first_qkv, second_qkv), (weight_out, first_out, second_out)],
-        ((0, 0, 384, False, 0), (0, 384, 256, True, 1)),
-    )
-    squares = jnp.concatenate(
-        [
-            gain_heads[0:1],
-            gain_heads[1:2],
-            weight_squares[:4].reshape(1, 512),
-            (later_squares + qkv_squares)[:4].reshape(1, 512),
-            jnp.zeros((1, D - 1280), F32),
-        ],
-        axis=1,
-    )
-    sums = jnp.concatenate([gain_attn, gain_ffn[None], squares, jnp.zeros((1, D), F32)])
-    near, _ = beside(near, sums)
-    grad_attn_in = scatter_ring(near)
+    (got_u, got_v), (later_squares, block_out) = beside((got_u, got_v), (later_squares, block_out))
+    late_u = scatter_rest(parts_u[0], got_u, from_x)
+    late_v = scatter_rest(parts_v[0], got_v, from_y)
+    grad_attn_in, _ = beside(grad_attn_in, (late_u, late_v))
+    late_grad = jnp.concatenate([late_u, late_v])
     scale_one = inverse_rms(own_tokens)
     normed_one = own_tokens * scale_one
     input_grad = (
@@ -1227,6 +1245,22 @@
     ).astype(BF16)
     input_grad = lax.all_gather(input_grad, "tensor", axis=0, tiled=True)
 
+    (qkv_step, out_step), qkv_squares = take_step(
+        [jnp.concatenate([late_grad[:, :256], late_grad[:, 512:]], axis=1), late_grad],
+        [(weight_qkv, first_qkv, second_qkv), (weight_out, first_out, second_out)],
+        ((0, 0, 384, False, 0), (1, 256, 256, True, 1)),
+    )
+    squares = jnp.concatenate(
+        [
+            gain_query[0:1],
+            gain_key[0:1],
+            weight_squares[:4].reshape(1, 512),
+            (later_squares + qkv_squares)[:4].reshape(1, 512),
+            jnp.zeros((1, D - 1280), F32),
+        ],
+        axis=1,
+    )
+    sums = jnp.concatenate([gain_attn + gain_rest, gain_ffn[None], squares, jnp.zeros((1, D), F32)])
     sums = sum_all(sums)
     steps = (qkv_step, out_step, gate_up_step, down_step)
     done = finish(

time: 457 us -> 436 us (0.954)
  starting transfers between devices: 125 us -> 109 us
  local copies, waits for them, and re-layouts: 28.3 us -> 21.5 us
  waiting for transfers between devices: 118 us -> 124 us
    ppermute x7 -> x6, starting transfers between devices: 14.9 us -> 7.41 us  [from_core(): return lax.ppermute(a, 'tensor', PERM_CORE)]
    ppermute x21 -> x24, waiting for transfers between devices: 27.4 us -> 34.3 us  [from_x(): return lax.ppermute(a, 'dp', perm_x(k))]
    ppermute x21 -> x18, waiting for transfers between devices: 30.7 us -> 24.2 us  [from_z(): return lax.ppermute(a, 'tensor', perm_z(k))]
    ppermute x21 -> x24, starting transfers between devices: 32 us -> 25.7 us  [from_x(): return lax.ppermute(a, 'dp', perm_x(k))]
    unnamed x128 -> x136, local copies, waits for them, and re-layouts: 21.9 us -> 16 us
    ppermute x21 -> x24, starting transfers between devices: 29.3 us -> 26.3 us  [from_y(): return lax.ppermute(a, 'dp', perm_y(k))]
    pallas_call x8 -> x9, Pallas kernels: 64.5 us -> 67.4 us  [the longest x1 32.4 us: attend_back(): pl.pallas_call(backward_kernel, in_specs=[pl.BlockSpec(memory_space=pltpu...]
    ppermute x21 -> x18, starting transfers between devices: 23.8 us -> 21.5 us  [from_z(): return lax.ppermute(a, 'tensor', perm_z(k))]
  transfers between devices with their start and end apart: 79 -> 82, of which waited for: 36 -> 34; matrix products, arithmetic and copies ran while one was open for 4% -> 4% of each run, Pallas kernels for 26% -> 28%
where the time goes in v1:
time: 436 us; the launch traced here: 427 us
  Pallas kernels  138 us (32%)
  waiting for transfers between devices  124 us (28%)
  starting transfers between devices  109 us (25%)
  local copies, waits for them, and re-layouts  21.5 us (5%)
  other arithmetic  19 us (4%)
  between operations  16 us (4%)
    ppermute x24, waiting for transfers between devices, from_y(): return lax.ppermute(a, 'dp', perm_y(k))  35.8 us
    ppermute x24, waiting for transfers between devices, from_x(): return lax.ppermute(a, 'dp', perm_x(k))  34.3 us
    pallas_call x1, Pallas kernels, attend_back(): pl.pallas_call(backward_kernel, in_specs=[pl.BlockSpec(memory_space=pltpu...  32.4 us
    ppermute x4, starting transfers between devices, from_partner(): return lax.ppermute(a, 'dp', PERM_PARTNER)  27.2 us
    ppermute x24, starting transfers between devices, from_y(): return lax.ppermute(a, 'dp', perm_y(k))  26.3 us
    ppermute x24, starting transfers between devices, from_x(): return lax.ppermute(a, 'dp', perm_x(k))  25.7 us
    ppermute x18, waiting for transfers between devices, from_z(): return lax.ppermute(a, 'tensor', perm_z(k))  24.2 us
    ppermute x18, starting transfers between devices, from_z(): return lax.ppermute(a, 'tensor', perm_z(k))  21.5 us
  transfers between devices with their start and end apart: 82, of which 34 were waited for; matrix products, arithmetic and copies ran while one was open for 4% of the time, Pallas kernels for 28%

profile of v1, /device:TPU:1, one launch (start us, length us, event | category | flops | bytes accessed | tf_op | source)
XLA Modules:
  0.0 427.2 jit_solution(2550639218789209643)
XLA Ops:
  25.1 5.3 %prepare.1.x_ref.in_ref = bf16[512,2048]{1,0:T(8,128)(2,1)S(1)} custom-call(s32[8]{0:T(128)S(1)} %get-tuple-element.304.row_ref, bf16[512,2048]{1,0:T(8,128)(2,1)} %tok_ref.2, f32[1,2048]{1,0:T(1,128)S(1)} %get-tuple-element.345.gain_ref), custom_call_target="tpu_custom_call" | custom-call | flops 4400000000 | tf_op jit(solution)/shard_map/prepare/pallas_call | solution.py:165
  49.4 6.7 %project.1 = (f32[512,384]{1,0:T(8,128)S(1)}, bf16[2,64,512]{2,1,0:T(8,128)(2,1)S(1)}, bf16[2,64,512]{2,1,0:T(8,128)(2,1)S(1)}, bf16[512,128]{1,0:T(8,128)(2,1)S...) custom-call(s32[16]{0:T(128)S(1)} %and_add_fusion.blk_ref, bf16[512,2048]{1,0:T(8,128)(2,1)} %copy-done.45, ...), custom_call_target="tpu_custom_call" | custom-call | flops 6600000000 | tf_op jit(solution)/shard_map/project/pallas_call | solution.py:331
  75.9 8.5 %arrange.1 = (bf16[2048,512]{1,0:T(8,128)(2,1)S(1)}, bf16[512,2048]{1,0:T(8,128)(2,1)}, bf16[512,2048]{1,0:T(8,128)(2,1)}) custom-call(s32[8]{0:T(128)S(1)} %get-tuple-element.304.row_ref, bf16[512,2048]{1,0:T(8,128)(2,1)} %tok_ref.2, bf16[512,2048]{1,0:T(8,128)(2,1)} %cot_ref, bf16[512,2048]{1,0:T(8,128)(2,1)} %copy-done.45), custom_call_target="tpu_custom_call" | custom-call | flops 7699999744 | tf_op jit(solution)/shard_map/arrange/pallas_call | solution.py:195
  85.8 14.0 %collective-permute-done.17.kv3 = bf16[4,512,128]{2,1,0:T(8,128)(2,1)} collective-permute-done((bf16[4,512,128]{2,1,0:T(8,128)(2,1)S(1)}, bf16[4,512,128]{2,1,0:T(8,128)(2,1)}, u32[]{:S(2)}, u32[]{:S(2)}) %collective-permute-start.17) | collective-permute-done | bytes 524320 | tf_op jit(solution)/shard_map/ppermute | solution.py:70
  99.8 4.7 %attend.1 = (bf16[512,256]{1,0:T(8,128)(2,1)S(1)}, f32[128,512]{1,0:T(8,128)S(1)}, f32[8,512]{1,0:T(8,128)S(1)}, f32[136,512]{1,0:T(8,128)S(1)}, bf16[16,512,128]{2,1,0:T(8,128)(2,1)}) custom-call(s32[18]{0:T(128)S(1)} %pad_add_fusion.1.blk_ref, bf16[2,64,512]{2,1,0:T(8,128)(2,1)S(1)} %copy-done.51, bf16[2,64,512]{2,1,0:T(8,128)(2,1)S(1)} %get-tuple-element.165.q_second, ...), custom_call_target="tpu_custom_call" | custom-call | flops 22000001024 | tf_op jit(solution)/shard_map/attend/pallas_call | solution.py:429
  107.2 25.3 %collective-permute-start.25 = (f32[136,512]{1,0:T(8,128)S(1)}, f32[136,512]{1,0:T(8,128)S(1)}, u32[]{:S(2)}, u32[]{:S(2)}) collective-permute-start(f32[136,512]{1,0:T(8,128)S(1)} %get-tuple-element.176), channel_id=1, source_target_pairs={{0,120},{8,112},{16,104},{24,96},{32,88},{40,80},{48,72},{56,64},{... | collective-permute-start | bytes 835592 | tf_op jit(solution)/shard_map/ppermute | solution.py:82
  138.6 5.5 %inner_grad.1.grad_ref = f32[512,1024]{1,0:T(8,128)S(1)} custom-call(bf16[512,2048]{1,0:T(8,128)(2,1)} %get-tuple-element.162.dy_ref.refs_0_, bf16[2048,1280]{1,0:T(8,128)(2,1)} %all-gather.5.cloned.1.call-done.w_ref), custom_call_target="tpu_custom_call" | custom-call | flops 6049999872 | tf_op jit(solution)/shard_map/inner_grad/pallas_call | solution.py:707
  144.2 6.2 %collective-permute-done.20 = bf16[64,2048]{1,0:T(8,128)(2,1)S(1)} collective-permute-done((bf16[64,2048]{1,0:T(8,128)(2,1)S(1)}, bf16[64,2048]{1,0:T(8,128)(2,1)S(1)}, u32[]{:S(2)}, u32[]{:S(2)}) %collective-permute-start.20) | collective-permute-done | bytes 262176 | tf_op jit(solution)/shard_map/ppermute | solution.py:74
  155.7 8.9 %collective-permute-done.26.q_other = bf16[2,64,512]{2,1,0:T(8,128)(2,1)S(1)} collective-permute-done((bf16[2,64,512]{2,1,0:T(8,128)(2,1)S(1)}, bf16[2,64,512]{2,1,0:T(8,128)(2,1)S(1)}, u32[]{:S(2)}, u32[]{:S(2)}) %collective-permute-start.26) | collective-permute-done | bytes 131104 | tf_op jit(solution)/shard_map/ppermute | solution.py:82
  165.3 4.0 collective-permute-done.24
  173.0 15.4 %feed_forward.1 = (bf16[512,1024]{1,0:T(8,128)(2,1)S(1)}, bf16[512,1024]{1,0:T(8,128)(2,1)S(1)}, bf16[512,1024]{1,0:T(8,128)(2,1)S(1)}, f32[256,2048]{1,0:T(8,128)}, bf16[256,2048]{1,0:T(8,128)(2,1)}) custom-call(bf16[256,2048]{1,0:T(8,128)(2,1)} %copy-done, bf16[256,2048]{1,0:T(8,128)(2,1)} %collective-permute-done.27.far_ref.refs_1_, ...), custom_call_target="tpu_custom_call" | custom-call | flops 14300000256 | tf_op jit(solution)/shard_map/feed_forward/pallas_call | solution.py:685
  189.0 5.1 %weight_grad.2.refs_4_ = bf16[2048,3072]{1,0:T(8,128)(2,1)} custom-call(bf16[512,2048]{1,0:T(8,128)(2,1)S(1)} %copy-done.5, bf16[512,1024]{1,0:T(8,128)(2,1)S(1)} %get-tuple-element.186.refs_1_.act_ref), custom_call_target="tpu_custom_call" | custom-call | flops 5500000256 | tf_op jit(solution)/shard_map/weight_grad/pallas_call | solution.py:933
  199.4 10.5 %weight_grad.3 = bf16[2048,3072]{1,0:T(8,128)(2,1)} custom-call(bf16[256,2048]{1,0:T(8,128)(2,1)S(1)} %copy-done.1, bf16[256,2048]{1,0:T(8,128)(2,1)} %collective-permute-done.27.far_ref.refs_1_, bf16[512,1024]{1,0:T(8,128)(2,1)S(1)} %get-tuple-element.184.refs_2_, bf16[512,1024]{1,0:T(8,128)(2,1)} %copy-done.47, ...), custom_call_target="tpu_custom_call", output_to_operand_aliasing={{}: (4, {})} | custom-call | flops 11000000512 | tf_op jit(solution)/shard_map/weight_grad/pallas_call | solution.py:933
  218.8 7.5 %ffn_out.1 = (f32[256,2048]{1,0:T(8,128)}, bf16[256,2048]{1,0:T(8,128)(2,1)S(1)}) custom-call(bf16[512,1024]{1,0:T(8,128)(2,1)S(1)} %copy-done.40, bf16[2048,1280]{1,0:T(8,128)(2,1)} %all-gather.5.cloned.1.call-done.w_ref), custom_call_target="tpu_custom_call" | custom-call | flops 7150000128 | tf_op jit(solution)/shard_map/ffn_out/pallas_call | solution.py:742
  226.2 7.3 %collective-permute-done.34 = bf16[64,2048]{1,0:T(8,128)(2,1)S(1)} collective-permute-done((bf16[64,2048]{1,0:T(8,128)(2,1)S(1)}, bf16[64,2048]{1,0:T(8,128)(2,1)S(1)}, u32[]{:S(2)}, u32[]{:S(2)}) %collective-permute-start.34) | collective-permute-done | bytes 262176 | tf_op jit(solution)/shard_map/ppermute | solution.py:74
  241.0 7.7 %collective-permute-done.36.do_other = bf16[512,128]{1,0:T(8,128)(2,1)S(1)} collective-permute-done((bf16[512,128]{1,0:T(8,128)(2,1)S(1)}, bf16[512,128]{1,0:T(8,128)(2,1)S(1)}, u32[]{:S(2)}, u32[]{:S(2)}) %collective-permute-start.36) | collective-permute-done | bytes 131104 | tf_op jit(solution)/shard_map/ppermute | solution.py:82
  252.6 32.4 %attend_back.1 = (bf16[512,128]{1,0:T(8,128)(2,1)S(1)}, bf16[512,128]{1,0:T(8,128)(2,1)S(1)}, bf16[4,4,256,128]{3,2,1,0:T(8,128)(2,1)S(1)}, bf16[4,4,256,128]{3,2,1,0:T(8,128)(2,1)}) custom-call(s32[18]{0:T(128)S(1)} %pad_add_fusion.1.blk_ref, bf16[4,128,512]{2,1,0:T(8,128)(2,1)S(1)} %get-tuple-element.203.q_t, ...), custom_call_target="tpu_custom_call" | custom-call | flops 39600001024 | tf_op jit(solution)/shard_map/attend_back/pallas_call | solution.py:566
  295.4 13.3 %collective-permute-done.38 = bf16[4,256,128]{2,1,0:T(8,128)(2,1)S(1)} collective-permute-done((bf16[4,256,128]{2,1,0:T(8,128)(2,1)S(1)}, bf16[4,256,128]{2,1,0:T(8,128)(2,1)S(1)}, u32[]{:S(2)}, u32[]{:S(2)}) %collective-permute-start.38) | collective-permute-done | bytes 262176 | tf_op jit(solution)/shard_map/ppermute | solution.py:70
  333.9 5.7 %attn_back_rest.1 = (bf16[512,2048]{1,0:T(8,128)(2,1)}, f32[1,2048]{1,0:T(1,128)S(1)}) custom-call(s32[8]{0:T(128)S(1)} %copy-done.13, bf16[512,128]{1,0:T(8,128)(2,1)S(1)} %get-tuple-element.231.grad_ref, bf16[2048,384]{1,0:T(8,128)(2,1)S(1)} %copy-done.44, bf16[512,2048]{1,0:T(8,128)(2,1)} %get-tuple-element.163.x_ref, bf16[512,2048]{1,0:T(8,128)(2,1)} %copy-done.41), custom_call_target="tpu_custom_call" | custom-call | flops 4400000000 | tf_op jit(solution)/shard_map/attn_back_rest/pallas_call | solution.py:880
  354.4 4.9 %take_step.2 = (f32[2,128,1024]{2,1,0:T(8,128)}, f32[2,128,1024]{2,1,0:T(8,128)}, f32[2,128,1024]{2,1,0:T(8,128)S(1)}, f32[1024,128]{1,0:T(8,128)}, f32[1024,128...) custom-call(bf16[128,3072]{1,0:T(8,128)(2,1)S(1)} %copy-done.17, f32[2,128,1024]{2,1,0:T(8,128)} %refs_3_.5, ...), custom_call_target="tpu_custom_call" | custom-call | flops 4400000000 | tf_op jit(solution)/shard_map/take_step/pallas_call | solution.py:996
  372.5 4.3 %collective-permute-done.64 = bf16[64,640]{1,0:T(8,128)(2,1)S(1)} collective-permute-done((bf16[64,640]{1,0:T(8,128)(2,1)S(1)}, bf16[64,640]{1,0:T(8,128)(2,1)S(1)}, u32[]{:S(2)}, u32[]{:S(2)}) %collective-permute-start.64) | collective-permute-done | bytes 81952 | tf_op jit(solution)/shard_map/ppermute | solution.py:70
  400.3 4.4 %collective-permute-start.73 = (f32[4,2048]{1,0:T(4,128)S(1)}, f32[4,2048]{1,0:T(4,128)S(1)}, u32[]{:S(2)}, u32[]{:S(2)}) collective-permute-start(f32[4,2048]{1,0:T(4,128)S(1)} %add_add_fusion.1), channel_id=1, source_target_pairs={{0,6},{1,7},{2,0},{3,1},{4,2},{5,3},{6,4},{7,5},{8,14},{9,15},{10,... | collective-permute-start | bytes 98312 | tf_op jit(solution)/shard_map/ppermute | solution.py:74
  406.0 4.1 collective-permute-done.74
  410.1 4.1 collective-permute-start.75
  (410 shorter events, 195.5 us)
Async XLA Ops:
  7.2 97.3 %all-gather.5.cloned.1.call-start = ((), (), s32[]{:S(2)}) async-start(), calls=%async_computation.2 | async-start | bytes 5570560 | tf_op jit(solution)/shard_map/all_gather | solution.py:1127
  13.1 159.9 %all-gather.7.cloned.1.call-start = ((), (), s32[]{:S(2)}) async-start(), calls=%async_computation.3 | async-start | bytes 8912896 | tf_op jit(solution)/shard_map/all_gather | solution.py:1128
  13.9 325.7 %reduce-scatter.3.cloned.1.call-start = ((), (), s32[]{:S(2)}) async-start(), calls=%async_computation.4 | async-start | bytes 13369344 | tf_op jit(solution)/shard_map/reduce_scatter | solution.py:1191
  14.1 19.0 %collective-permute-start.2 = (bf16[80,384]{1,0:T(8,128)(2,1)S(1)}, bf16[80,384]{1,0:T(8,128)(2,1)S(1)}, u32[]{:S(2)}, u32[]{:S(2)}) collective-permute-start(bf16[80,384]{1,0:T(8,128)(2,1)S(1)} %get-tuple-element.343), channel_id=1, source_target_pairs={{0,8},{8,16},{16,24},{24,0},{32,40},{40,48},{48,56},{56,32},{64,72... | collective-permute-start | bytes 184328 | tf_op jit(solution)/shard_map/ppermute | solution.py:66
  16.2 16.9 %collective-permute-start.1 = (bf16[80,384]{1,0:T(8,128)(2,1)S(1)}, bf16[80,384]{1,0:T(8,128)(2,1)S(1)}, u32[]{:S(2)}, u32[]{:S(2)}) collective-permute-start(bf16[80,384]{1,0:T(8,128)(2,1)S(1)} %get-tuple-element.343), channel_id=1, source_target_pairs={{0,16},{8,24},{16,0},{24,8},{32,48},{40,56},{48,32},{56,40},{64,80... | collective-permute-start | bytes 184328 | tf_op jit(solution)/shard_map/ppermute | solution.py:66
  71.8 28.0 %collective-permute-start.17 = (bf16[4,512,128]{2,1,0:T(8,128)(2,1)S(1)}, bf16[4,512,128]{2,1,0:T(8,128)(2,1)}, u32[]{:S(2)}, u32[]{:S(2)}) collective-permute-start(bf16[4,512,128]{2,1,0:T(8,128)(2,1)S(1)} %pad_maximum_fusion.2.kv0), channel_id=1, source_target_pairs={{0,32},{8,40},{16,48},{24,56},{32,64},{40,72},{48,80},{56,88},{64,... | collective-permute-start | bytes 1572872 | tf_op jit(solution)/shard_map/ppermute | solution.py:70
  106.2 28.0 %collective-permute-start.18 = (bf16[256,2048]{1,0:T(8,128)(2,1)S(1)}, bf16[256,2048]{1,0:T(8,128)(2,1)S(1)}, u32[]{:S(2)}, u32[]{:S(2)}) collective-permute-start(bf16[256,2048]{1,0:T(8,128)(2,1)S(1)} %out_project.3), channel_id=1, source_target_pairs={{0,1},{1,0},{2,3},{3,2},{4,5},{5,4},{6,7},{7,6},{8,9},{9,8},{10,11... | collective-permute-start | bytes 3145736 | tf_op jit(solution)/shard_map/ppermute | solution.py:78
  107.2 57.4 %collective-permute-start.25 = (f32[136,512]{1,0:T(8,128)S(1)}, f32[136,512]{1,0:T(8,128)S(1)}, u32[]{:S(2)}, u32[]{:S(2)}) collective-permute-start(f32[136,512]{1,0:T(8,128)S(1)} %get-tuple-element.176), channel_id=1, source_target_pairs={{0,120},{8,112},{16,104},{24,96},{32,88},{40,80},{48,72},{56,64},{... | collective-permute-start | bytes 835592 | tf_op jit(solution)/shard_map/ppermute | solution.py:82
  134.9 15.5 %collective-permute-start.20 = (bf16[64,2048]{1,0:T(8,128)(2,1)S(1)}, bf16[64,2048]{1,0:T(8,128)(2,1)S(1)}, u32[]{:S(2)}, u32[]{:S(2)}) collective-permute-start(bf16[64,2048]{1,0:T(8,128)(2,1)S(1)} %get-tuple-element.325), channel_id=1, source_target_pairs={{0,4},{1,5},{2,6},{3,7},{4,0},{5,1},{6,2},{7,3},{8,12},{9,13},{10,... | collective-permute-start | bytes 786440 | tf_op jit(solution)/shard_map/ppermute | solution.py:74
  196.7 14.8 %collective-permute-start.29 = (bf16[64,2048]{1,0:T(8,128)(2,1)}, bf16[64,2048]{1,0:T(8,128)(2,1)S(1)}, u32[]{:S(2)}, u32[]{:S(2)}) collective-permute-start(bf16[64,2048]{1,0:T(8,128)(2,1)} %get-tuple-element.323), channel_id=1, source_target_pairs={{0,2},{1,3},{2,4},{3,5},{4,6},{5,7},{6,0},{7,1},{8,10},{9,11},{10,... | collective-permute-start | bytes 786440 | tf_op jit(solution)/shard_map/ppermute | solution.py:74
  196.7 14.8 %collective-permute-start.30 = (bf16[64,2048]{1,0:T(8,128)(2,1)}, bf16[64,2048]{1,0:T(8,128)(2,1)S(1)}, u32[]{:S(2)}, u32[]{:S(2)}) collective-permute-start(bf16[64,2048]{1,0:T(8,128)(2,1)} %get-tuple-element.322), channel_id=1, source_target_pairs={{0,4},{1,5},{2,6},{3,7},{4,0},{5,1},{6,2},{7,3},{8,12},{9,13},{10,... | collective-permute-start | bytes 786440 | tf_op jit(solution)/shard_map/ppermute | solution.py:74
  212.6 137.8 %all-gather.9.cloned.1.call-start = ((), (), s32[]{:S(2)}) async-start(), calls=%async_computation.5 | async-start | bytes 2359296 | tf_op jit(solution)/shard_map/all_gather | solution.py:1227
  218.5 15.1 %collective-permute-start.34 = (bf16[64,2048]{1,0:T(8,128)(2,1)S(1)}, bf16[64,2048]{1,0:T(8,128)(2,1)S(1)}, u32[]{:S(2)}, u32[]{:S(2)}) collective-permute-start(bf16[64,2048]{1,0:T(8,128)(2,1)S(1)} %fusion.40), channel_id=1, source_target_pairs={{0,2},{1,3},{2,4},{3,5},{4,6},{5,7},{6,0},{7,1},{8,10},{9,11},{10,... | collective-permute-start | bytes 786440 | tf_op jit(solution)/shard_map/ppermute | solution.py:74
  249.2 35.8 %collective-permute-start.41 = (bf16[64,2048]{1,0:T(8,128)(2,1)S(1)}, bf16[64,2048]{1,0:T(8,128)(2,1)S(1)}, u32[]{:S(2)}, u32[]{:S(2)}) collective-permute-start(bf16[64,2048]{1,0:T(8,128)(2,1)S(1)} %get-tuple-element.317), channel_id=1, source_target_pairs={{0,2},{1,3},{2,4},{3,5},{4,6},{5,7},{6,0},{7,1},{8,10},{9,11},{10,... | collective-permute-start | bytes 786440 | tf_op jit(solution)/shard_map/ppermute | solution.py:74
  249.3 35.7 %collective-permute-start.42 = (bf16[64,2048]{1,0:T(8,128)(2,1)S(1)}, bf16[64,2048]{1,0:T(8,128)(2,1)S(1)}, u32[]{:S(2)}, u32[]{:S(2)}) collective-permute-start(bf16[64,2048]{1,0:T(8,128)(2,1)S(1)} %get-tuple-element.316), channel_id=1, source_target_pairs={{0,4},{1,5},{2,6},{3,7},{4,0},{5,1},{6,2},{7,3},{8,12},{9,13},{10,... | collective-permute-start | bytes 786440 | tf_op jit(solution)/shard_map/ppermute | solution.py:74
  250.2 34.8 %collective-permute-start.43 = (bf16[64,2048]{1,0:T(8,128)(2,1)S(1)}, bf16[64,2048]{1,0:T(8,128)(2,1)S(1)}, u32[]{:S(2)}, u32[]{:S(2)}) collective-permute-start(bf16[64,2048]{1,0:T(8,128)(2,1)S(1)} %get-tuple-element.315), channel_id=1, source_target_pairs={{0,6},{1,7},{2,0},{3,1},{4,2},{5,3},{6,4},{7,5},{8,14},{9,15},{10,... | collective-permute-start | bytes 786440 | tf_op jit(solution)/shard_map/ppermute | solution.py:74
  286.6 93.7 %reduce-scatter.5.cloned.1.call-start = ((), (), s32[]{:S(2)}) async-start(), calls=%async_computation.6 | async-start | bytes 2359296 | tf_op jit(solution)/shard_map/reduce_scatter | solution.py:1230
  286.7 22.0 %collective-permute-start.38 = (bf16[4,256,128]{2,1,0:T(8,128)(2,1)S(1)}, bf16[4,256,128]{2,1,0:T(8,128)(2,1)S(1)}, u32[]{:S(2)}, u32[]{:S(2)}) collective-permute-start(bf16[4,256,128]{2,1,0:T(8,128)(2,1)S(1)} %get-tuple-element.320), channel_id=1, source_target_pairs={{0,32},{8,40},{16,48},{24,56},{32,64},{40,72},{48,80},{56,88},{64,... | collective-permute-start | bytes 786440 | tf_op jit(solution)/shard_map/ppermute | solution.py:70
  286.8 29.4 %collective-permute-start.39 = (bf16[4,256,128]{2,1,0:T(8,128)(2,1)S(1)}, bf16[4,256,128]{2,1,0:T(8,128)(2,1)S(1)}, u32[]{:S(2)}, u32[]{:S(2)}) collective-permute-start(bf16[4,256,128]{2,1,0:T(8,128)(2,1)S(1)} %get-tuple-element.319), channel_id=1, source_target_pairs={{0,64},{8,72},{16,80},{24,88},{32,96},{40,104},{48,112},{56,120},{... | collective-permute-start | bytes 786440 | tf_op jit(solution)/shard_map/ppermute | solution.py:70
  286.9 29.4 %collective-permute-start.40 = (bf16[4,256,128]{2,1,0:T(8,128)(2,1)S(1)}, bf16[4,256,128]{2,1,0:T(8,128)(2,1)S(1)}, u32[]{:S(2)}, u32[]{:S(2)}) collective-permute-start(bf16[4,256,128]{2,1,0:T(8,128)(2,1)S(1)} %get-tuple-element.318), channel_id=1, source_target_pairs={{0,96},{8,104},{16,112},{24,120},{32,0},{40,8},{48,16},{56,24},{64... | collective-permute-start | bytes 786440 | tf_op jit(solution)/shard_map/ppermute | solution.py:70
  293.1 23.2 %collective-permute-start.45 = (bf16[4,256,128]{2,1,0:T(8,128)(2,1)S(1)}, bf16[4,256,128]{2,1,0:T(8,128)(2,1)S(1)}, u32[]{:S(2)}, u32[]{:S(2)}) collective-permute-start(bf16[4,256,128]{2,1,0:T(8,128)(2,1)S(1)} %get-tuple-element.314), channel_id=1, source_target_pairs={{0,8},{8,16},{16,24},{24,0},{32,40},{40,48},{48,56},{56,32},{64,72... | collective-permute-start | bytes 786440 | tf_op jit(solution)/shard_map/ppermute | solution.py:66
  293.2 23.1 %collective-permute-start.46 = (bf16[4,256,128]{2,1,0:T(8,128)(2,1)S(1)}, bf16[4,256,128]{2,1,0:T(8,128)(2,1)S(1)}, u32[]{:S(2)}, u32[]{:S(2)}) collective-permute-start(bf16[4,256,128]{2,1,0:T(8,128)(2,1)S(1)} %get-tuple-element.313), channel_id=1, source_target_pairs={{0,16},{8,24},{16,0},{24,8},{32,48},{40,56},{48,32},{56,40},{64,80... | collective-permute-start | bytes 786440 | tf_op jit(solution)/shard_map/ppermute | solution.py:66
  339.7 77.1 %all-gather.11.cloned.1.call-start = ((), (), s32[]{:S(2)}) async-start(), calls=%async_computation.7 | async-start | bytes 2359296 | tf_op jit(solution)/shard_map/all_gather | solution.py:1246
  343.5 15.8 %collective-permute-start.55 = (bf16[4,64,640]{2,1,0:T(8,128)(2,1)}, bf16[4,64,640]{2,1,0:T(8,128)(2,1)}, u32[]{:S(2)}, u32[]{:S(2)}) collective-permute-start(bf16[4,64,640]{2,1,0:T(8,128)(2,1)} %get-tuple-element.310), channel_id=1, source_target_pairs={{0,64},{8,72},{16,80},{24,88},{32,96},{40,104},{48,112},{56,120},{... | collective-permute-start | bytes 983048 | tf_op jit(solution)/shard_map/ppermute | solution.py:70
  (123 other events, 1251.4 us)
Sparse Core Ops, SparseCore 0:
  13.3 66.5 all-gather.4
  82.5 80.5 all-gather.6
  212.7 107.4 reduce-scatter.2
  322.3 24.4 all-gather.8
  349.1 31.1 reduce-scatter.4
  384.9 27.4 all-gather.10

commit v2 on v1

--- a/solution.py
+++ b/solution.py
@@ -27,7 +27,8 @@
 F32 = jnp.float32
 BF16 = jnp.bfloat16
 OFF = -1e5
-VMEM_LIMIT = 50 * 1024 * 1024
+VMEM_LIMIT = 24 * 1024 * 1024
+VMEM_LARGE = 44 * 1024 * 1024
 
 
 def inverse_rms(array_in):
@@ -282,7 +283,7 @@
         out_specs=vmem_specs(3),
         out_shape=[shape((128, 1280), BF16), shape((128, 2048), BF16), shape((8, 128), F32)],
         scratch_shapes=[pltpu.VMEM(a.shape, F32) for a in given] + [pltpu.SemaphoreType.DMA((4,))],
-        compiler_params=params(),
+        compiler_params=params(60 * 1024 * 1024),
         name="pack",
         cost_estimate=takes(2),
     )(*given)
@@ -441,7 +442,7 @@
             pltpu.VMEM((QPK, 128, ROWS), BF16),
             pltpu.VMEM((QPK, 72, ROWS), F32),
         ],
-        compiler_params=params(),
+        compiler_params=params(VMEM_LARGE),
         name="attend",
         cost_estimate=takes(20),
     )(blocks, q_first, q_second, *kv, kinfo, qinfo, bias)
@@ -569,7 +570,7 @@
         out_specs=vmem_specs(4),
         out_shape=[pair, pair, half, half],
         scratch_shapes=[pltpu.VMEM((256, ROWS), F32), pltpu.VMEM((ROWS, 128), F32)],
-        compiler_params=params(),
+        compiler_params=params(VMEM_LARGE),
         name="attend_back",
         cost_estimate=takes(36),
     )(blocks, *operands, kv, kinfo, qinfo)
@@ -693,7 +694,7 @@
             pltpu.VMEM((ROWS, 2048), BF16),
             pltpu.SemaphoreType.DMA((8,)),
         ],
-        compiler_params=params(),
+        compiler_params=params(VMEM_LARGE),
         name="feed_forward",
         cost_estimate=takes(13),
     )(near, far, grad_inner, gate_up)

time: 436 us -> 431 us (0.989)
  Pallas kernels: 138 us -> 101 us
  local copies, waits for them, and re-layouts: 21.5 us -> 40.3 us
  starting transfers between devices: 109 us -> 118 us
  waiting for transfers between devices: 124 us -> 129 us
    unnamed x136 -> x168, local copies, waits for them, and re-layouts: 16 us -> 34.7 us
    pallas_call x1, Pallas kernels: 8.52 us -> 2.22 us  [arrange(): pl.pallas_call(arrange_kernel, grid_spec=pltpu.PrefetchScalarGridSpec(num...]
    all_gather x1, waiting for transfers between devices: 0.02 us -> 5.16 us  [local(): block_out = keep(lax.all_gather(block_rows, 'tensor', axis=0, tiled=True))]
    ppermute x24, waiting for transfers between devices: 34.3 us -> 38.7 us  [from_x(): return lax.ppermute(a, 'dp', perm_x(k))]
  transfers between devices with their start and end apart: 82 -> 82, of which waited for: 34 -> 38; matrix products, arithmetic and copies ran while one was open for 4% -> 4% of each run, Pallas kernels for 28% -> 20%
where the time goes in v2:
time: 431 us; the launch traced here: 423 us
  waiting for transfers between devices  129 us (30%)
  starting transfers between devices  118 us (27%)
  Pallas kernels  101 us (23%)
  local copies, waits for them, and re-layouts  40.3 us (9%)
  other arithmetic  17.9 us (4%)
  between operations  16.1 us (4%)
    ppermute x24, waiting for transfers between devices, from_x(): return lax.ppermute(a, 'dp', perm_x(k))  38.7 us
    ppermute x24, waiting for transfers between devices, from_y(): return lax.ppermute(a, 'dp', perm_y(k))  37.5 us
    unnamed x168, local copies, waits for them, and re-layouts  34.7 us
    pallas_call x1, Pallas kernels, attend_back(): pl.pallas_call(backward_kernel, in_specs=[pl.BlockSpec(memory_space=pltpu...  30.2 us
    ppermute x24, starting transfers between devices, from_y(): return lax.ppermute(a, 'dp', perm_y(k))  29.2 us
    ppermute x4, starting transfers between devices, from_partner(): return lax.ppermute(a, 'dp', PERM_PARTNER)  28.4 us
    ppermute x24, starting transfers between devices, from_x(): return lax.ppermute(a, 'dp', perm_x(k))  28.1 us
    ppermute x18, starting transfers between devices, from_z(): return lax.ppermute(a, 'tensor', perm_z(k))  24.4 us
  transfers between devices with their start and end apart: 82, of which 38 were waited for; matrix products, arithmetic and copies ran while one was open for 4% of the time, Pallas kernels for 20%

profile of v2, /device:TPU:1, one launch (start us, length us, event | category | flops | bytes accessed | tf_op | source)
XLA Modules:
  0.0 423.0 jit_solution(8529066501887703037)
XLA Ops:
  48.2 4.2 project.1
  56.8 5.5 %collective-permute-done.12 = bf16[512,128]{1,0:T(8,128)(2,1)S(1)} collective-permute-done((bf16[512,128]{1,0:T(8,128)(2,1)S(1)}, bf16[512,128]{1,0:T(8,128)(2,1)S(1)}, u32[]{:S(2)}, u32[]{:S(2)}) %collective-permute-start.12) | collective-permute-done | bytes 131104 | tf_op jit(solution)/shard_map/ppermute | solution.py:67
  82.1 4.0 collective-permute-done.15.kv1
  87.7 11.1 %collective-permute-done.17.kv3 = bf16[4,512,128]{2,1,0:T(8,128)(2,1)} collective-permute-done((bf16[4,512,128]{2,1,0:T(8,128)(2,1)S(1)}, bf16[4,512,128]{2,1,0:T(8,128)(2,1)}, u32[]{:S(2)}, u32[]{:S(2)}) %collective-permute-start.17) | collective-permute-done | bytes 524320 | tf_op jit(solution)/shard_map/ppermute | solution.py:71
  111.3 22.4 %collective-permute-start.25 = (f32[136,512]{1,0:T(8,128)S(1)}, f32[136,512]{1,0:T(8,128)S(1)}, u32[]{:S(2)}, u32[]{:S(2)}) collective-permute-start(f32[136,512]{1,0:T(8,128)S(1)} %copy-done.35), channel_id=1, source_target_pairs={{0,120},{8,112},{16,104},{24,96},{32,88},{40,80},{48,72},{56,64},{... | collective-permute-start | bytes 835592 | tf_op jit(solution)/shard_map/ppermute | solution.py:83
  143.9 6.4 %collective-permute-done.20 = bf16[64,2048]{1,0:T(8,128)(2,1)S(1)} collective-permute-done((bf16[64,2048]{1,0:T(8,128)(2,1)S(1)}, bf16[64,2048]{1,0:T(8,128)(2,1)S(1)}, u32[]{:S(2)}, u32[]{:S(2)}) %collective-permute-start.20) | collective-permute-done | bytes 262176 | tf_op jit(solution)/shard_map/ppermute | solution.py:75
  156.3 9.0 %collective-permute-done.26.q_other = bf16[2,64,512]{2,1,0:T(8,128)(2,1)S(1)} collective-permute-done((bf16[2,64,512]{2,1,0:T(8,128)(2,1)S(1)}, bf16[2,64,512]{2,1,0:T(8,128)(2,1)S(1)}, u32[]{:S(2)}, u32[]{:S(2)}) %collective-permute-start.26) | collective-permute-done | bytes 131104 | tf_op jit(solution)/shard_map/ppermute | solution.py:83
  172.4 13.4 %feed_forward.1 = (bf16[512,1024]{1,0:T(8,128)(2,1)S(1)}, bf16[512,1024]{1,0:T(8,128)(2,1)S(1)}, bf16[512,1024]{1,0:T(8,128)(2,1)S(1)}, f32[256,2048]{1,0:T(8,128)S(1)}, bf16[256,2048]{1,0:T(8,128)(2,1)S(1)}) custom-call(bf16[256,2048]{1,0:T(8,128)(2,1)S(1)} %pad_maximum_fusion.near_ref.refs_0_, ...), custom_call_target="tpu_custom_call" | custom-call | flops 14300000256 | tf_op jit(solution)/shard_map/feed_forward/pallas_call | solution.py:686
  186.2 4.2 %weight_grad.2.refs_4_ = bf16[2048,3072]{1,0:T(8,128)(2,1)S(1)} custom-call(bf16[512,2048]{1,0:T(8,128)(2,1)S(1)} %copy-done.13, bf16[512,1024]{1,0:T(8,128)(2,1)S(1)} %get-tuple-element.186.refs_1_.act_ref), custom_call_target="tpu_custom_call" | custom-call | flops 5500000256 | tf_op jit(solution)/shard_map/weight_grad/pallas_call | solution.py:934
  197.2 8.0 %weight_grad.3 = bf16[2048,3072]{1,0:T(8,128)(2,1)S(1)} custom-call(bf16[256,2048]{1,0:T(8,128)(2,1)S(1)} %pad_maximum_fusion.near_ref.refs_0_, bf16[256,2048]{1,0:T(8,128)(2,1)S(1)} %collective-permute-done.27.far_ref.refs_1_, bf16[512,1024]{1,0:T(8,128)(2,1)S(1)} %get-tuple-element.184.refs_2_, ...), custom_call_target="tpu_custom_call", output_to_operand_aliasing={{}: (4, {})} | custom-call | flops 11000000512 | tf_op jit(solution)/shard_map/weight_grad/pallas_call | solution.py:934
  205.1 4.6 %copy-done = bf16[2048,3072]{1,0:T(8,128)(2,1)} copy-done((bf16[2048,3072]{1,0:T(8,128)(2,1)}, bf16[2048,3072]{1,0:T(8,128)(2,1)S(1)}, u32[]{:S(2)}) %copy-start) | copy-done | bytes 12582936
  218.8 5.1 %ffn_out.1 = (f32[256,2048]{1,0:T(8,128)S(1)}, bf16[256,2048]{1,0:T(8,128)(2,1)S(1)}) custom-call(bf16[512,1024]{1,0:T(8,128)(2,1)S(1)} %copy-done.55, bf16[2048,1280]{1,0:T(8,128)(2,1)S(1)} %copy-done.2), custom_call_target="tpu_custom_call" | custom-call | flops 7150000128 | tf_op jit(solution)/shard_map/ffn_out/pallas_call | solution.py:743
  224.0 6.2 %collective-permute-done.34 = bf16[64,2048]{1,0:T(8,128)(2,1)S(1)} collective-permute-done((bf16[64,2048]{1,0:T(8,128)(2,1)S(1)}, bf16[64,2048]{1,0:T(8,128)(2,1)S(1)}, u32[]{:S(2)}, u32[]{:S(2)}) %collective-permute-start.34) | collective-permute-done | bytes 262176 | tf_op jit(solution)/shard_map/ppermute | solution.py:75
  237.6 7.3 %collective-permute-done.36.do_other = bf16[512,128]{1,0:T(8,128)(2,1)S(1)} collective-permute-done((bf16[512,128]{1,0:T(8,128)(2,1)S(1)}, bf16[512,128]{1,0:T(8,128)(2,1)S(1)}, u32[]{:S(2)}, u32[]{:S(2)}) %collective-permute-start.36) | collective-permute-done | bytes 131104 | tf_op jit(solution)/shard_map/ppermute | solution.py:83
  250.6 30.2 %attend_back.1 = (bf16[512,128]{1,0:T(8,128)(2,1)S(1)}, bf16[512,128]{1,0:T(8,128)(2,1)S(1)}, bf16[4,4,256,128]{3,2,1,0:T(8,128)(2,1)S(1)}, bf16[4,4,256,128]{3,2,1,0:T(8,128)(2,1)S(1)}) custom-call(s32[18]{0:T(128)S(1)} %pad_add_fusion.1.blk_ref, bf16[4,128,512]{2,1,0:T(8,128)(2,1)S(1)} %get-tuple-element.203.q_t, ...), custom_call_target="tpu_custom_call" | custom-call | flops 39600001024 | tf_op jit(solution)/shard_map/attend_back/pallas_call | solution.py:567
  292.9 6.1 %collective-permute-done.38 = bf16[4,256,128]{2,1,0:T(8,128)(2,1)S(1)} collective-permute-done((bf16[4,256,128]{2,1,0:T(8,128)(2,1)S(1)}, bf16[4,256,128]{2,1,0:T(8,128)(2,1)S(1)}, u32[]{:S(2)}, u32[]{:S(2)}) %collective-permute-start.38) | collective-permute-done | bytes 262176 | tf_op jit(solution)/shard_map/ppermute | solution.py:71
  312.6 4.1 collective-permute-start.51
  337.4 5.2 %all-gather.9.cloned.1.call-done.in_ref = bf16[512,2048]{1,0:T(8,128)(2,1)} async-done(((bf16[64,2048]{1,0:T(8,128)(2,1)}), bf16[512,2048]{1,0:T(8,128)(2,1)}) %all-gather.9.cloned.1.call-update) | async-done | bytes 2097168 | tf_op jit(solution)/shard_map/all_gather | solution.py:1228
  351.6 4.4 %collective-permute-done.59 = bf16[4,64,640]{2,1,0:T(8,128)(2,1)S(1)} collective-permute-done((bf16[4,64,640]{2,1,0:T(8,128)(2,1)S(1)}, bf16[4,64,640]{2,1,0:T(8,128)(2,1)S(1)}, u32[]{:S(2)}, u32[]{:S(2)}) %collective-permute-start.59) | collective-permute-done | bytes 327712 | tf_op jit(solution)/shard_map/ppermute | solution.py:67
  367.3 4.3 %collective-permute-done.64 = bf16[64,640]{1,0:T(8,128)(2,1)S(1)} collective-permute-done((bf16[64,640]{1,0:T(8,128)(2,1)S(1)}, bf16[64,640]{1,0:T(8,128)(2,1)S(1)}, u32[]{:S(2)}, u32[]{:S(2)}) %collective-permute-start.64) | collective-permute-done | bytes 81952 | tf_op jit(solution)/shard_map/ppermute | solution.py:71
  371.7 4.0 reduce-scatter.5.cloned.1.call-done
  396.0 4.5 %collective-permute-start.73 = (f32[4,2048]{1,0:T(4,128)S(1)}, f32[4,2048]{1,0:T(4,128)S(1)}, u32[]{:S(2)}, u32[]{:S(2)}) collective-permute-start(f32[4,2048]{1,0:T(4,128)S(1)} %add_add_fusion.1), channel_id=1, source_target_pairs={{0,6},{1,7},{2,0},{3,1},{4,2},{5,3},{6,4},{7,5},{8,14},{9,15},{10,... | collective-permute-start | bytes 98312 | tf_op jit(solution)/shard_map/ppermute | solution.py:75
  401.7 4.1 collective-permute-done.74
  405.8 4.2 collective-permute-start.75
  (442 shorter events, 224.6 us)
Async XLA Ops:
  7.2 98.7 %all-gather.5.cloned.1.call-start = ((), (), s32[]{:S(2)}) async-start(), calls=%async_computation.2 | async-start | bytes 5570560 | tf_op jit(solution)/shard_map/all_gather | solution.py:1128
  9.8 162.6 %all-gather.7.cloned.1.call-start = ((), (), s32[]{:S(2)}) async-start(), calls=%async_computation.3 | async-start | bytes 8912896 | tf_op jit(solution)/shard_map/all_gather | solution.py:1129
  10.5 318.7 %reduce-scatter.3.cloned.1.call-start = ((), (), s32[]{:S(2)}) async-start(), calls=%async_computation.4 | async-start | bytes 13369344 | tf_op jit(solution)/shard_map/reduce_scatter | solution.py:1192
  67.7 18.3 %collective-permute-start.15 = (bf16[4,512,128]{2,1,0:T(8,128)(2,1)S(1)}, bf16[4,512,128]{2,1,0:T(8,128)(2,1)}, u32[]{:S(2)}, u32[]{:S(2)}) collective-permute-start(bf16[4,512,128]{2,1,0:T(8,128)(2,1)S(1)} %pad_maximum_fusion.2.kv0), channel_id=1, source_target_pairs={{0,96},{8,104},{16,112},{24,120},{32,0},{40,8},{48,16},{56,24},{64... | collective-permute-start | bytes 1572872 | tf_op jit(solution)/shard_map/ppermute | solution.py:71
  67.8 19.9 %collective-permute-start.16 = (bf16[4,512,128]{2,1,0:T(8,128)(2,1)S(1)}, bf16[4,512,128]{2,1,0:T(8,128)(2,1)}, u32[]{:S(2)}, u32[]{:S(2)}) collective-permute-start(bf16[4,512,128]{2,1,0:T(8,128)(2,1)S(1)} %pad_maximum_fusion.2.kv0), channel_id=1, source_target_pairs={{0,64},{8,72},{16,80},{24,88},{32,96},{40,104},{48,112},{56,120},{... | collective-permute-start | bytes 1572872 | tf_op jit(solution)/shard_map/ppermute | solution.py:71
  68.2 30.6 %collective-permute-start.17 = (bf16[4,512,128]{2,1,0:T(8,128)(2,1)S(1)}, bf16[4,512,128]{2,1,0:T(8,128)(2,1)}, u32[]{:S(2)}, u32[]{:S(2)}) collective-permute-start(bf16[4,512,128]{2,1,0:T(8,128)(2,1)S(1)} %pad_maximum_fusion.2.kv0), channel_id=1, source_target_pairs={{0,32},{8,40},{16,48},{24,56},{32,64},{40,72},{48,80},{56,88},{64,... | collective-permute-start | bytes 1572872 | tf_op jit(solution)/shard_map/ppermute | solution.py:71
  109.9 24.3 %collective-permute-start.18 = (bf16[256,2048]{1,0:T(8,128)(2,1)S(1)}, bf16[256,2048]{1,0:T(8,128)(2,1)S(1)}, u32[]{:S(2)}, u32[]{:S(2)}) collective-permute-start(bf16[256,2048]{1,0:T(8,128)(2,1)S(1)} %out_project.3), channel_id=1, source_target_pairs={{0,1},{1,0},{2,3},{3,2},{4,5},{5,4},{6,7},{7,6},{8,9},{9,8},{10,11... | collective-permute-start | bytes 3145736 | tf_op jit(solution)/shard_map/ppermute | solution.py:79
  111.3 54.1 %collective-permute-start.25 = (f32[136,512]{1,0:T(8,128)S(1)}, f32[136,512]{1,0:T(8,128)S(1)}, u32[]{:S(2)}, u32[]{:S(2)}) collective-permute-start(f32[136,512]{1,0:T(8,128)S(1)} %copy-done.35), channel_id=1, source_target_pairs={{0,120},{8,112},{16,104},{24,96},{32,88},{40,80},{48,72},{56,64},{... | collective-permute-start | bytes 835592 | tf_op jit(solution)/shard_map/ppermute | solution.py:83
  193.1 16.6 %collective-permute-start.29 = (bf16[64,2048]{1,0:T(8,128)(2,1)}, bf16[64,2048]{1,0:T(8,128)(2,1)S(1)}, u32[]{:S(2)}, u32[]{:S(2)}) collective-permute-start(bf16[64,2048]{1,0:T(8,128)(2,1)} %get-tuple-element.323), channel_id=1, source_target_pairs={{0,2},{1,3},{2,4},{3,5},{4,6},{5,7},{6,0},{7,1},{8,10},{9,11},{10,... | collective-permute-start | bytes 786440 | tf_op jit(solution)/shard_map/ppermute | solution.py:75
  193.8 15.9 %collective-permute-start.30 = (bf16[64,2048]{1,0:T(8,128)(2,1)}, bf16[64,2048]{1,0:T(8,128)(2,1)}, u32[]{:S(2)}, u32[]{:S(2)}) collective-permute-start(bf16[64,2048]{1,0:T(8,128)(2,1)} %get-tuple-element.322), channel_id=1, source_target_pairs={{0,4},{1,5},{2,6},{3,7},{4,0},{5,1},{6,2},{7,3},{8,12},{9,13},{10,... | collective-permute-start | bytes 786440 | tf_op jit(solution)/shard_map/ppermute | solution.py:75
  209.7 132.8 %all-gather.9.cloned.1.call-start = ((), (), s32[]{:S(2)}) async-start(), calls=%async_computation.5 | async-start | bytes 2359296 | tf_op jit(solution)/shard_map/all_gather | solution.py:1228
  245.4 35.4 %collective-permute-start.41 = (bf16[64,2048]{1,0:T(8,128)(2,1)S(1)}, bf16[64,2048]{1,0:T(8,128)(2,1)S(1)}, u32[]{:S(2)}, u32[]{:S(2)}) collective-permute-start(bf16[64,2048]{1,0:T(8,128)(2,1)S(1)} %get-tuple-element.317), channel_id=1, source_target_pairs={{0,2},{1,3},{2,4},{3,5},{4,6},{5,7},{6,0},{7,1},{8,10},{9,11},{10,... | collective-permute-start | bytes 786440 | tf_op jit(solution)/shard_map/ppermute | solution.py:75
  245.5 35.3 %collective-permute-start.42 = (bf16[64,2048]{1,0:T(8,128)(2,1)S(1)}, bf16[64,2048]{1,0:T(8,128)(2,1)S(1)}, u32[]{:S(2)}, u32[]{:S(2)}) collective-permute-start(bf16[64,2048]{1,0:T(8,128)(2,1)S(1)} %get-tuple-element.316), channel_id=1, source_target_pairs={{0,4},{1,5},{2,6},{3,7},{4,0},{5,1},{6,2},{7,3},{8,12},{9,13},{10,... | collective-permute-start | bytes 786440 | tf_op jit(solution)/shard_map/ppermute | solution.py:75
  247.3 33.6 %collective-permute-start.43 = (bf16[64,2048]{1,0:T(8,128)(2,1)S(1)}, bf16[64,2048]{1,0:T(8,128)(2,1)S(1)}, u32[]{:S(2)}, u32[]{:S(2)}) collective-permute-start(bf16[64,2048]{1,0:T(8,128)(2,1)S(1)} %get-tuple-element.315), channel_id=1, source_target_pairs={{0,6},{1,7},{2,0},{3,1},{4,2},{5,3},{6,4},{7,5},{8,14},{9,15},{10,... | collective-permute-start | bytes 786440 | tf_op jit(solution)/shard_map/ppermute | solution.py:75
  284.0 91.7 %reduce-scatter.5.cloned.1.call-start = ((), (), s32[]{:S(2)}) async-start(), calls=%async_computation.6 | async-start | bytes 2359296 | tf_op jit(solution)/shard_map/reduce_scatter | solution.py:1231
  284.2 23.4 %collective-permute-start.39 = (bf16[4,256,128]{2,1,0:T(8,128)(2,1)S(1)}, bf16[4,256,128]{2,1,0:T(8,128)(2,1)S(1)}, u32[]{:S(2)}, u32[]{:S(2)}) collective-permute-start(bf16[4,256,128]{2,1,0:T(8,128)(2,1)S(1)} %get-tuple-element.319), channel_id=1, source_target_pairs={{0,64},{8,72},{16,80},{24,88},{32,96},{40,104},{48,112},{56,120},{... | collective-permute-start | bytes 786440 | tf_op jit(solution)/shard_map/ppermute | solution.py:71
  287.4 20.2 %collective-permute-start.40 = (bf16[4,256,128]{2,1,0:T(8,128)(2,1)S(1)}, bf16[4,256,128]{2,1,0:T(8,128)(2,1)S(1)}, u32[]{:S(2)}, u32[]{:S(2)}) collective-permute-start(bf16[4,256,128]{2,1,0:T(8,128)(2,1)S(1)} %get-tuple-element.318), channel_id=1, source_target_pairs={{0,96},{8,104},{16,112},{24,120},{32,0},{40,8},{48,16},{56,24},{64... | collective-permute-start | bytes 786440 | tf_op jit(solution)/shard_map/ppermute | solution.py:71
  288.1 19.5 %collective-permute-start.45 = (bf16[4,256,128]{2,1,0:T(8,128)(2,1)S(1)}, bf16[4,256,128]{2,1,0:T(8,128)(2,1)S(1)}, u32[]{:S(2)}, u32[]{:S(2)}) collective-permute-start(bf16[4,256,128]{2,1,0:T(8,128)(2,1)S(1)} %get-tuple-element.314), channel_id=1, source_target_pairs={{0,8},{8,16},{16,24},{24,0},{32,40},{40,48},{48,56},{56,32},{64,72... | collective-permute-start | bytes 786440 | tf_op jit(solution)/shard_map/ppermute | solution.py:67
  288.2 19.4 %collective-permute-start.46 = (bf16[4,256,128]{2,1,0:T(8,128)(2,1)S(1)}, bf16[4,256,128]{2,1,0:T(8,128)(2,1)S(1)}, u32[]{:S(2)}, u32[]{:S(2)}) collective-permute-start(bf16[4,256,128]{2,1,0:T(8,128)(2,1)S(1)} %get-tuple-element.313), channel_id=1, source_target_pairs={{0,16},{8,24},{16,0},{24,8},{32,48},{40,56},{48,32},{56,40},{64,80... | collective-permute-start | bytes 786440 | tf_op jit(solution)/shard_map/ppermute | solution.py:67
  329.2 83.3 %all-gather.11.cloned.1.call-start = ((), (), s32[]{:S(2)}) async-start(), calls=%async_computation.7 | async-start | bytes 2359296 | tf_op jit(solution)/shard_map/all_gather | solution.py:1247
  331.9 19.7 %collective-permute-start.55 = (bf16[4,64,640]{2,1,0:T(8,128)(2,1)}, bf16[4,64,640]{2,1,0:T(8,128)(2,1)}, u32[]{:S(2)}, u32[]{:S(2)}) collective-permute-start(bf16[4,64,640]{2,1,0:T(8,128)(2,1)} %get-tuple-element.310), channel_id=1, source_target_pairs={{0,64},{8,72},{16,80},{24,88},{32,96},{40,104},{48,112},{56,120},{... | collective-permute-start | bytes 983048 | tf_op jit(solution)/shard_map/ppermute | solution.py:71
  333.8 17.8 %collective-permute-start.56 = (bf16[4,64,640]{2,1,0:T(8,128)(2,1)}, bf16[4,64,640]{2,1,0:T(8,128)(2,1)}, u32[]{:S(2)}, u32[]{:S(2)}) collective-permute-start(bf16[4,64,640]{2,1,0:T(8,128)(2,1)} %get-tuple-element.309), channel_id=1, source_target_pairs={{0,96},{8,104},{16,112},{24,120},{32,0},{40,8},{48,16},{56,24},{64... | collective-permute-start | bytes 983048 | tf_op jit(solution)/shard_map/ppermute | solution.py:71
  334.6 17.0 %collective-permute-start.57 = (bf16[4,64,640]{2,1,0:T(8,128)(2,1)}, bf16[4,64,640]{2,1,0:T(8,128)(2,1)S(1)}, u32[]{:S(2)}, u32[]{:S(2)}) collective-permute-start(bf16[4,64,640]{2,1,0:T(8,128)(2,1)} %get-tuple-element.308), channel_id=1, source_target_pairs={{0,8},{8,16},{16,24},{24,0},{32,40},{40,48},{48,56},{56,32},{64,72... | collective-permute-start | bytes 983048 | tf_op jit(solution)/shard_map/ppermute | solution.py:67
  334.7 16.9 %collective-permute-start.58 = (bf16[4,64,640]{2,1,0:T(8,128)(2,1)}, bf16[4,64,640]{2,1,0:T(8,128)(2,1)}, u32[]{:S(2)}, u32[]{:S(2)}) collective-permute-start(bf16[4,64,640]{2,1,0:T(8,128)(2,1)} %get-tuple-element.307), channel_id=1, source_target_pairs={{0,16},{8,24},{16,0},{24,8},{32,48},{40,56},{48,32},{56,40},{64,80... | collective-permute-start | bytes 983048 | tf_op jit(solution)/shard_map/ppermute | solution.py:67
  (139 other events, 1330.8 us)
Sparse Core Ops, SparseCore 0:
  10.8 80.7 all-gather.4
  94.2 76.8 all-gather.6
  209.9 105.7 reduce-scatter.2
  317.8 24.6 all-gather.8
  344.8 30.8 reduce-scatter.4
  380.5 27.6 all-gather.10

commit v3 on v2

--- a/solution.py
+++ b/solution.py
@@ -423,7 +423,8 @@
     out_ref[:64], out_ref[64:] = heads[0], heads[1]
     lse_ref[...] = jnp.concatenate(logs[:2] + [rest], axis=0)
     send_ref[:64], send_ref[64:128] = heads[2], heads[3]
-    send_ref[128:] = jnp.concatenate(logs[2:] + [rest], axis=0)
+    send_ref[128:136] = jnp.concatenate(logs[2:] + [rest], axis=0)
+    send_ref[136:200], send_ref[200:] = q_second[0].astype(F32), q_second[1].astype(F32)
 
 
 def attend(blocks, q_first, q_second, kv, kinfo, qinfo, bias):
@@ -435,7 +436,7 @@
             shape((ROWS, 256), BF16),
             shape((128, ROWS), F32),
             shape((8, ROWS), F32),
-            shape((136, ROWS), F32),
+            shape((264, ROWS), F32),
             shape((16, ROWS, 128), BF16),
         ],
         scratch_shapes=[
@@ -482,13 +483,16 @@
     )(near, far, down_out)
 
 
-def ready_kernel(do_own, do_other, out_own, lse_own, out_other, q_own, q_other, bias_ref, q_t, do_t, q_pad, do_pad):
+def ready_kernel(do_own, do_other, out_own, lse_own, out_other, q_own, bias_ref, q_t, do_t, q_pad, do_pad):
     row = lax.broadcasted_iota(jnp.int32, (64, ROWS), 0)
     low_half = lane_of((ROWS, 128)) < 64
     for queries in range(2):
         do = (do_own, do_other)[queries][...].astype(F32)
-        q_ref = (q_own, q_other)[queries]
-        q = jnp.concatenate([q_ref[0].astype(F32), q_ref[1].astype(F32)], axis=0).T
+        if queries:
+            across = out_other[136:264, :]
+        else:
+            across = jnp.concatenate([q_own[0].astype(F32), q_own[1].astype(F32)], axis=0)
+        q = across.T
         do_turned = do.T
         dots = do_turned * (out_own, out_other)[queries][:128, :]
         for part in range(2):
@@ -498,7 +502,7 @@
             lse = (out_other[128 + part : 129 + part, :] if queries else lse_own[part : part + 1, :])
             extra = three_rows(row, -lse, 0)
             extra = extra + jnp.where(row == 3, bias_ref[queries : queries + 1, :], 0.0)
-            q_t[head, :64, :] = q_ref[part]
+            q_t[head, :64, :] = across[at, :].astype(BF16)
             q_t[head, 64:, :] = extra.astype(BF16)
             do_t[head, :64, :] = three_rows(row, -delta, 0).astype(BF16)
             do_t[head, 64:, :] = do_turned[at, :].astype(BF16)
@@ -1181,8 +1185,8 @@
     hidden_one = own_tokens + attn_rows
     scale_two = inverse_rms(hidden_one)
     normed_two = hidden_one * scale_two
-    ffn_in, (out_other, q_other) = gather_tensor(
-        (normed_two * norm_gains[1]).astype(BF16), (from_partner(out_send), from_partner(q_send))
+    ffn_in, out_other = gather_tensor(
+        (normed_two * norm_gains[1]).astype(BF16), from_partner(out_send)
     )
     inner_act, grad_gate, grad_up, near, far = feed_forward(*ffn_in, grad_inner, gate_up)
 
@@ -1202,7 +1206,7 @@
     ffn_near = (ffn_near + ffn_far.astype(F32)).reshape(4, CH, D)
     ffn_low = ffn_near.astype(BF16)
     ffn_got = {k: from_z(ffn_low[k], -k) for k in (2, 1, 3)}
-    operands = ready(do_own, do_other, out_own, log_own, out_other, q_own, q_other, bias)
+    operands = ready(do_own, do_other, out_own, log_own, out_other, q_own, bias)
     dq_own, dq_send, part_u, part_v = attend_back(block_info, operands, kv_all, kinfo, qinfo)
     dq_send, ffn_got = beside(dq_send, ffn_got)
     dq_other = from_partner(dq_send)
@@ -1244,7 +1248,7 @@
     input_grad = (
         grad_hidden + norm_back(grad_attn_in, normed_one, scale_one, norm_gains[0])
     ).astype(BF16)
-    input_grad = lax.all_gather(input_grad, "tensor", axis=0, tiled=True)
+    input_grad = keep(lax.all_gather(input_grad, "tensor", axis=0, tiled=True))
 
     (qkv_step, out_step), qkv_squares = take_step(
         [jnp.concatenate([late_grad[:, :256], late_grad[:, 512:]], axis=1), late_grad],

time: 431 us -> 433 us (level)
    ppermute x18, waiting for transfers between devices: 20.7 us -> 27 us  [from_z(): return lax.ppermute(a, 'tensor', perm_z(k))]
    ppermute x4 -> x3, waiting for transfers between devices: 17 us -> 11.1 us  [from_partner(): return lax.ppermute(a, 'dp', PERM_PARTNER)]
    ppermute x4 -> x3, starting transfers between devices: 28.4 us -> 27.1 us  [from_partner(): return lax.ppermute(a, 'dp', PERM_PARTNER)]
    unnamed x168 -> x167, local copies, waits for them, and re-layouts: 34.7 us -> 33.7 us
  transfers between devices with their start and end apart: 82 -> 81, of which waited for: 38 -> 40; matrix products, arithmetic and copies ran while one was open for 4% -> 4% of each run, Pallas kernels for 20% -> 20%
where the time goes in v3:
time: 433 us; the launch traced here: 425 us
  waiting for transfers between devices  131 us (30%)
  starting transfers between devices  118 us (27%)
  Pallas kernels  103 us (24%)
  local copies, waits for them, and re-layouts  39.2 us (9%)
  other arithmetic  17.8 us (4%)
  between operations  16.1 us (4%)
    ppermute x24, waiting for transfers between devices, from_x(): return lax.ppermute(a, 'dp', perm_x(k))  39.5 us
    ppermute x24, waiting for transfers between devices, from_y(): return lax.ppermute(a, 'dp', perm_y(k))  37.4 us
    unnamed x167, local copies, waits for them, and re-layouts  33.7 us
    pallas_call x1, Pallas kernels, attend_back(): pl.pallas_call(backward_kernel, in_specs=[pl.BlockSpec(memory_space=pltpu...  30.2 us
    ppermute x24, starting transfers between devices, from_y(): return lax.ppermute(a, 'dp', perm_y(k))  28.3 us
    ppermute x24, starting transfers between devices, from_x(): return lax.ppermute(a, 'dp', perm_x(k))  28.2 us
    ppermute x3, starting transfers between devices, from_partner(): return lax.ppermute(a, 'dp', PERM_PARTNER)  27.1 us
    ppermute x18, waiting for transfers between devices, from_z(): return lax.ppermute(a, 'tensor', perm_z(k))  27 us
  transfers between devices with their start and end apart: 81, of which 40 were waited for; matrix products, arithmetic and copies ran while one was open for 4% of the time, Pallas kernels for 20%

profile of v3, /device:TPU:1, one launch (start us, length us, event | category | flops | bytes accessed | tf_op | source)
XLA Modules:
  0.0 425.2 jit_solution(15094250806896325492)
XLA Ops:
  39.2 3.9 collective-permute-done.11.v3
  48.2 4.2 project.1
  57.3 5.5 %collective-permute-done.12 = bf16[512,128]{1,0:T(8,128)(2,1)S(1)} collective-permute-done((bf16[512,128]{1,0:T(8,128)(2,1)S(1)}, bf16[512,128]{1,0:T(8,128)(2,1)S(1)}, u32[]{:S(2)}, u32[]{:S(2)}) %collective-permute-start.12) | collective-permute-done | bytes 131104 | tf_op jit(solution)/shard_map/ppermute | solution.py:67
  87.7 11.1 %collective-permute-done.17.kv3 = bf16[4,512,128]{2,1,0:T(8,128)(2,1)} collective-permute-done((bf16[4,512,128]{2,1,0:T(8,128)(2,1)S(1)}, bf16[4,512,128]{2,1,0:T(8,128)(2,1)}, u32[]{:S(2)}, u32[]{:S(2)}) %collective-permute-start.17) | collective-permute-done | bytes 524320 | tf_op jit(solution)/shard_map/ppermute | solution.py:71
  111.5 22.4 %collective-permute-start.25 = (f32[264,512]{1,0:T(8,128)S(1)}, f32[264,512]{1,0:T(8,128)S(1)}, u32[]{:S(2)}, u32[]{:S(2)}) collective-permute-start(f32[264,512]{1,0:T(8,128)S(1)} %copy-done.33), channel_id=1, source_target_pairs={{0,120},{8,112},{16,104},{24,96},{32,88},{40,80},{48,72},{56,64},{... | collective-permute-start | bytes 1622024 | tf_op jit(solution)/shard_map/ppermute | solution.py:83
  144.0 6.4 %collective-permute-done.20 = bf16[64,2048]{1,0:T(8,128)(2,1)S(1)} collective-permute-done((bf16[64,2048]{1,0:T(8,128)(2,1)S(1)}, bf16[64,2048]{1,0:T(8,128)(2,1)S(1)}, u32[]{:S(2)}, u32[]{:S(2)}) %collective-permute-start.20) | collective-permute-done | bytes 262176 | tf_op jit(solution)/shard_map/ppermute | solution.py:75
  158.1 6.8 %collective-permute-done.22 = bf16[64,2048]{1,0:T(8,128)(2,1)S(1)} collective-permute-done((bf16[64,2048]{1,0:T(8,128)(2,1)S(1)}, bf16[64,2048]{1,0:T(8,128)(2,1)S(1)}, u32[]{:S(2)}, u32[]{:S(2)}) %collective-permute-start.22) | collective-permute-done | bytes 262176 | tf_op jit(solution)/shard_map/ppermute | solution.py:75
  164.8 4.2 collective-permute-done.24
  173.7 13.4 %feed_forward.1 = (bf16[512,1024]{1,0:T(8,128)(2,1)S(1)}, bf16[512,1024]{1,0:T(8,128)(2,1)S(1)}, bf16[512,1024]{1,0:T(8,128)(2,1)S(1)}, f32[256,2048]{1,0:T(8,128)S(1)}, bf16[256,2048]{1,0:T(8,128)(2,1)S(1)}) custom-call(bf16[256,2048]{1,0:T(8,128)(2,1)S(1)} %pad_maximum_fusion.near_ref.refs_0_, ...), custom_call_target="tpu_custom_call" | custom-call | flops 14300000256 | tf_op jit(solution)/shard_map/feed_forward/pallas_call | solution.py:690
  187.8 4.2 weight_grad.2.refs_4_
  199.7 8.0 %weight_grad.3 = bf16[2048,3072]{1,0:T(8,128)(2,1)S(1)} custom-call(bf16[256,2048]{1,0:T(8,128)(2,1)S(1)} %pad_maximum_fusion.near_ref.refs_0_, bf16[256,2048]{1,0:T(8,128)(2,1)S(1)} %collective-permute-done.26.far_ref.refs_1_, bf16[512,1024]{1,0:T(8,128)(2,1)S(1)} %get-tuple-element.183.refs_2_, ...), custom_call_target="tpu_custom_call", output_to_operand_aliasing={{}: (4, {})} | custom-call | flops 11000000512 | tf_op jit(solution)/shard_map/weight_grad/pallas_call | solution.py:938
  207.7 4.6 %copy-done = bf16[2048,3072]{1,0:T(8,128)(2,1)} copy-done((bf16[2048,3072]{1,0:T(8,128)(2,1)}, bf16[2048,3072]{1,0:T(8,128)(2,1)S(1)}, u32[]{:S(2)}) %copy-start) | copy-done | bytes 12582936
  221.4 5.1 %ffn_out.1 = (f32[256,2048]{1,0:T(8,128)S(1)}, bf16[256,2048]{1,0:T(8,128)(2,1)S(1)}) custom-call(bf16[512,1024]{1,0:T(8,128)(2,1)S(1)} %copy-done.53, bf16[2048,1280]{1,0:T(8,128)(2,1)S(1)} %copy-done.2), custom_call_target="tpu_custom_call" | custom-call | flops 7150000128 | tf_op jit(solution)/shard_map/ffn_out/pallas_call | solution.py:747
  226.5 5.3 %collective-permute-done.33 = bf16[64,2048]{1,0:T(8,128)(2,1)S(1)} collective-permute-done((bf16[64,2048]{1,0:T(8,128)(2,1)S(1)}, bf16[64,2048]{1,0:T(8,128)(2,1)S(1)}, u32[]{:S(2)}, u32[]{:S(2)}) %collective-permute-start.33) | collective-permute-done | bytes 262176 | tf_op jit(solution)/shard_map/ppermute | solution.py:75
  239.7 7.2 %collective-permute-done.35.do_other = bf16[512,128]{1,0:T(8,128)(2,1)S(1)} collective-permute-done((bf16[512,128]{1,0:T(8,128)(2,1)S(1)}, bf16[512,128]{1,0:T(8,128)(2,1)S(1)}, u32[]{:S(2)}, u32[]{:S(2)}) %collective-permute-start.35) | collective-permute-done | bytes 131104 | tf_op jit(solution)/shard_map/ppermute | solution.py:83
  253.0 30.2 %attend_back.1 = (bf16[512,128]{1,0:T(8,128)(2,1)S(1)}, bf16[512,128]{1,0:T(8,128)(2,1)S(1)}, bf16[4,4,256,128]{3,2,1,0:T(8,128)(2,1)S(1)}, bf16[4,4,256,128]{3,2,1,0:T(8,128)(2,1)S(1)}) custom-call(s32[18]{0:T(128)S(1)} %pad_add_fusion.1.blk_ref, bf16[4,128,512]{2,1,0:T(8,128)(2,1)S(1)} %get-tuple-element.201.q_t, ...), custom_call_target="tpu_custom_call" | custom-call | flops 39600001024 | tf_op jit(solution)/shard_map/attend_back/pallas_call | solution.py:571
  295.3 6.5 %collective-permute-done.37 = bf16[4,256,128]{2,1,0:T(8,128)(2,1)S(1)} collective-permute-done((bf16[4,256,128]{2,1,0:T(8,128)(2,1)S(1)}, bf16[4,256,128]{2,1,0:T(8,128)(2,1)S(1)}, u32[]{:S(2)}, u32[]{:S(2)}) %collective-permute-start.37) | collective-permute-done | bytes 262176 | tf_op jit(solution)/shard_map/ppermute | solution.py:71
  315.0 3.9 collective-permute-start.50
  339.3 5.1 %all-gather.9.cloned.1.call-done.in_ref = bf16[512,2048]{1,0:T(8,128)(2,1)} async-done(((bf16[64,2048]{1,0:T(8,128)(2,1)}), bf16[512,2048]{1,0:T(8,128)(2,1)}) %all-gather.9.cloned.1.call-update) | async-done | bytes 2097168 | tf_op jit(solution)/shard_map/all_gather | solution.py:1232
  353.5 5.6 %collective-permute-done.58 = bf16[4,64,640]{2,1,0:T(8,128)(2,1)S(1)} collective-permute-done((bf16[4,64,640]{2,1,0:T(8,128)(2,1)S(1)}, bf16[4,64,640]{2,1,0:T(8,128)(2,1)S(1)}, u32[]{:S(2)}, u32[]{:S(2)}) %collective-permute-start.58) | collective-permute-done | bytes 327712 | tf_op jit(solution)/shard_map/ppermute | solution.py:67
  369.8 4.1 collective-permute-done.63
  397.8 4.6 %collective-permute-start.72 = (f32[4,2048]{1,0:T(4,128)S(1)}, f32[4,2048]{1,0:T(4,128)S(1)}, u32[]{:S(2)}, u32[]{:S(2)}) collective-permute-start(f32[4,2048]{1,0:T(4,128)S(1)} %add_add_fusion.1), channel_id=1, source_target_pairs={{0,6},{1,7},{2,0},{3,1},{4,2},{5,3},{6,4},{7,5},{8,14},{9,15},{10,... | collective-permute-start | bytes 98312 | tf_op jit(solution)/shard_map/ppermute | solution.py:75
  403.7 3.9 collective-permute-done.73
  407.7 4.2 collective-permute-start.74
  (440 shorter events, 228.7 us)
Async XLA Ops:
  7.2 98.9 %all-gather.5.cloned.1.call-start = ((), (), s32[]{:S(2)}) async-start(), calls=%async_computation.2 | async-start | bytes 5570560 | tf_op jit(solution)/shard_map/all_gather | solution.py:1132
  9.8 163.9 %all-gather.7.cloned.1.call-start = ((), (), s32[]{:S(2)}) async-start(), calls=%async_computation.3 | async-start | bytes 8912896 | tf_op jit(solution)/shard_map/all_gather | solution.py:1133
  10.5 320.9 %reduce-scatter.3.cloned.1.call-start = ((), (), s32[]{:S(2)}) async-start(), calls=%async_computation.4 | async-start | bytes 13369344 | tf_op jit(solution)/shard_map/reduce_scatter | solution.py:1196
  68.2 17.6 %collective-permute-start.15 = (bf16[4,512,128]{2,1,0:T(8,128)(2,1)S(1)}, bf16[4,512,128]{2,1,0:T(8,128)(2,1)}, u32[]{:S(2)}, u32[]{:S(2)}) collective-permute-start(bf16[4,512,128]{2,1,0:T(8,128)(2,1)S(1)} %pad_maximum_fusion.2.kv0), channel_id=1, source_target_pairs={{0,96},{8,104},{16,112},{24,120},{32,0},{40,8},{48,16},{56,24},{64... | collective-permute-start | bytes 1572872 | tf_op jit(solution)/shard_map/ppermute | solution.py:71
  68.2 19.4 %collective-permute-start.16 = (bf16[4,512,128]{2,1,0:T(8,128)(2,1)S(1)}, bf16[4,512,128]{2,1,0:T(8,128)(2,1)}, u32[]{:S(2)}, u32[]{:S(2)}) collective-permute-start(bf16[4,512,128]{2,1,0:T(8,128)(2,1)S(1)} %pad_maximum_fusion.2.kv0), channel_id=1, source_target_pairs={{0,64},{8,72},{16,80},{24,88},{32,96},{40,104},{48,112},{56,120},{... | collective-permute-start | bytes 1572872 | tf_op jit(solution)/shard_map/ppermute | solution.py:71
  68.6 30.2 %collective-permute-start.17 = (bf16[4,512,128]{2,1,0:T(8,128)(2,1)S(1)}, bf16[4,512,128]{2,1,0:T(8,128)(2,1)}, u32[]{:S(2)}, u32[]{:S(2)}) collective-permute-start(bf16[4,512,128]{2,1,0:T(8,128)(2,1)S(1)} %pad_maximum_fusion.2.kv0), channel_id=1, source_target_pairs={{0,32},{8,40},{16,48},{24,56},{32,64},{40,72},{48,80},{56,88},{64,... | collective-permute-start | bytes 1572872 | tf_op jit(solution)/shard_map/ppermute | solution.py:71
  110.1 24.3 %collective-permute-start.18 = (bf16[256,2048]{1,0:T(8,128)(2,1)S(1)}, bf16[256,2048]{1,0:T(8,128)(2,1)S(1)}, u32[]{:S(2)}, u32[]{:S(2)}) collective-permute-start(bf16[256,2048]{1,0:T(8,128)(2,1)S(1)} %out_project.3), channel_id=1, source_target_pairs={{0,1},{1,0},{2,3},{3,2},{4,5},{5,4},{6,7},{7,6},{8,9},{9,8},{10,11... | collective-permute-start | bytes 3145736 | tf_op jit(solution)/shard_map/ppermute | solution.py:79
  111.5 46.6 %collective-permute-start.25 = (f32[264,512]{1,0:T(8,128)S(1)}, f32[264,512]{1,0:T(8,128)S(1)}, u32[]{:S(2)}, u32[]{:S(2)}) collective-permute-start(f32[264,512]{1,0:T(8,128)S(1)} %copy-done.33), channel_id=1, source_target_pairs={{0,120},{8,112},{16,104},{24,96},{32,88},{40,80},{48,72},{56,64},{... | collective-permute-start | bytes 1622024 | tf_op jit(solution)/shard_map/ppermute | solution.py:83
  194.8 17.5 %collective-permute-start.28 = (bf16[64,2048]{1,0:T(8,128)(2,1)}, bf16[64,2048]{1,0:T(8,128)(2,1)S(1)}, u32[]{:S(2)}, u32[]{:S(2)}) collective-permute-start(bf16[64,2048]{1,0:T(8,128)(2,1)} %get-tuple-element.321), channel_id=1, source_target_pairs={{0,2},{1,3},{2,4},{3,5},{4,6},{5,7},{6,0},{7,1},{8,10},{9,11},{10,... | collective-permute-start | bytes 786440 | tf_op jit(solution)/shard_map/ppermute | solution.py:75
  196.0 16.2 %collective-permute-start.29 = (bf16[64,2048]{1,0:T(8,128)(2,1)}, bf16[64,2048]{1,0:T(8,128)(2,1)S(1)}, u32[]{:S(2)}, u32[]{:S(2)}) collective-permute-start(bf16[64,2048]{1,0:T(8,128)(2,1)} %get-tuple-element.320), channel_id=1, source_target_pairs={{0,4},{1,5},{2,6},{3,7},{4,0},{5,1},{6,2},{7,3},{8,12},{9,13},{10,... | collective-permute-start | bytes 786440 | tf_op jit(solution)/shard_map/ppermute | solution.py:75
  212.3 132.1 %all-gather.9.cloned.1.call-start = ((), (), s32[]{:S(2)}) async-start(), calls=%async_computation.5 | async-start | bytes 2359296 | tf_op jit(solution)/shard_map/all_gather | solution.py:1232
  247.4 35.8 %collective-permute-start.40 = (bf16[64,2048]{1,0:T(8,128)(2,1)S(1)}, bf16[64,2048]{1,0:T(8,128)(2,1)S(1)}, u32[]{:S(2)}, u32[]{:S(2)}) collective-permute-start(bf16[64,2048]{1,0:T(8,128)(2,1)S(1)} %get-tuple-element.315), channel_id=1, source_target_pairs={{0,2},{1,3},{2,4},{3,5},{4,6},{5,7},{6,0},{7,1},{8,10},{9,11},{10,... | collective-permute-start | bytes 786440 | tf_op jit(solution)/shard_map/ppermute | solution.py:75
  247.5 35.7 %collective-permute-start.41 = (bf16[64,2048]{1,0:T(8,128)(2,1)S(1)}, bf16[64,2048]{1,0:T(8,128)(2,1)S(1)}, u32[]{:S(2)}, u32[]{:S(2)}) collective-permute-start(bf16[64,2048]{1,0:T(8,128)(2,1)S(1)} %get-tuple-element.314), channel_id=1, source_target_pairs={{0,4},{1,5},{2,6},{3,7},{4,0},{5,1},{6,2},{7,3},{8,12},{9,13},{10,... | collective-permute-start | bytes 786440 | tf_op jit(solution)/shard_map/ppermute | solution.py:75
  249.1 34.1 %collective-permute-start.42 = (bf16[64,2048]{1,0:T(8,128)(2,1)S(1)}, bf16[64,2048]{1,0:T(8,128)(2,1)S(1)}, u32[]{:S(2)}, u32[]{:S(2)}) collective-permute-start(bf16[64,2048]{1,0:T(8,128)(2,1)S(1)} %get-tuple-element.313), channel_id=1, source_target_pairs={{0,6},{1,7},{2,0},{3,1},{4,2},{5,3},{6,4},{7,5},{8,14},{9,15},{10,... | collective-permute-start | bytes 786440 | tf_op jit(solution)/shard_map/ppermute | solution.py:75
  286.3 91.1 %reduce-scatter.5.cloned.1.call-start = ((), (), s32[]{:S(2)}) async-start(), calls=%async_computation.6 | async-start | bytes 2359296 | tf_op jit(solution)/shard_map/reduce_scatter | solution.py:1235
  286.5 24.0 %collective-permute-start.38 = (bf16[4,256,128]{2,1,0:T(8,128)(2,1)S(1)}, bf16[4,256,128]{2,1,0:T(8,128)(2,1)S(1)}, u32[]{:S(2)}, u32[]{:S(2)}) collective-permute-start(bf16[4,256,128]{2,1,0:T(8,128)(2,1)S(1)} %get-tuple-element.317), channel_id=1, source_target_pairs={{0,64},{8,72},{16,80},{24,88},{32,96},{40,104},{48,112},{56,120},{... | collective-permute-start | bytes 786440 | tf_op jit(solution)/shard_map/ppermute | solution.py:71
  289.8 20.7 %collective-permute-start.39 = (bf16[4,256,128]{2,1,0:T(8,128)(2,1)S(1)}, bf16[4,256,128]{2,1,0:T(8,128)(2,1)S(1)}, u32[]{:S(2)}, u32[]{:S(2)}) collective-permute-start(bf16[4,256,128]{2,1,0:T(8,128)(2,1)S(1)} %get-tuple-element.316), channel_id=1, source_target_pairs={{0,96},{8,104},{16,112},{24,120},{32,0},{40,8},{48,16},{56,24},{64... | collective-permute-start | bytes 786440 | tf_op jit(solution)/shard_map/ppermute | solution.py:71
  290.5 20.0 %collective-permute-start.44 = (bf16[4,256,128]{2,1,0:T(8,128)(2,1)S(1)}, bf16[4,256,128]{2,1,0:T(8,128)(2,1)S(1)}, u32[]{:S(2)}, u32[]{:S(2)}) collective-permute-start(bf16[4,256,128]{2,1,0:T(8,128)(2,1)S(1)} %get-tuple-element.312), channel_id=1, source_target_pairs={{0,8},{8,16},{16,24},{24,0},{32,40},{40,48},{48,56},{56,32},{64,72... | collective-permute-start | bytes 786440 | tf_op jit(solution)/shard_map/ppermute | solution.py:67
  290.6 19.9 %collective-permute-start.45 = (bf16[4,256,128]{2,1,0:T(8,128)(2,1)S(1)}, bf16[4,256,128]{2,1,0:T(8,128)(2,1)S(1)}, u32[]{:S(2)}, u32[]{:S(2)}) collective-permute-start(bf16[4,256,128]{2,1,0:T(8,128)(2,1)S(1)} %get-tuple-element.311), channel_id=1, source_target_pairs={{0,16},{8,24},{16,0},{24,8},{32,48},{40,56},{48,32},{56,40},{64,80... | collective-permute-start | bytes 786440 | tf_op jit(solution)/shard_map/ppermute | solution.py:67
  331.4 83.0 %all-gather.11.cloned.1.call-start = ((), (), s32[]{:S(2)}) async-start(), calls=%async_computation.7 | async-start | bytes 2359296 | tf_op jit(solution)/shard_map/all_gather | solution.py:1251
  334.1 19.3 %collective-permute-start.54 = (bf16[4,64,640]{2,1,0:T(8,128)(2,1)}, bf16[4,64,640]{2,1,0:T(8,128)(2,1)}, u32[]{:S(2)}, u32[]{:S(2)}) collective-permute-start(bf16[4,64,640]{2,1,0:T(8,128)(2,1)} %get-tuple-element.308), channel_id=1, source_target_pairs={{0,64},{8,72},{16,80},{24,88},{32,96},{40,104},{48,112},{56,120},{... | collective-permute-start | bytes 983048 | tf_op jit(solution)/shard_map/ppermute | solution.py:71
  336.0 17.5 %collective-permute-start.55 = (bf16[4,64,640]{2,1,0:T(8,128)(2,1)}, bf16[4,64,640]{2,1,0:T(8,128)(2,1)}, u32[]{:S(2)}, u32[]{:S(2)}) collective-permute-start(bf16[4,64,640]{2,1,0:T(8,128)(2,1)} %get-tuple-element.307), channel_id=1, source_target_pairs={{0,96},{8,104},{16,112},{24,120},{32,0},{40,8},{48,16},{56,24},{64... | collective-permute-start | bytes 983048 | tf_op jit(solution)/shard_map/ppermute | solution.py:71
  336.8 16.7 %collective-permute-start.56 = (bf16[4,64,640]{2,1,0:T(8,128)(2,1)}, bf16[4,64,640]{2,1,0:T(8,128)(2,1)S(1)}, u32[]{:S(2)}, u32[]{:S(2)}) collective-permute-start(bf16[4,64,640]{2,1,0:T(8,128)(2,1)} %get-tuple-element.306), channel_id=1, source_target_pairs={{0,8},{8,16},{16,24},{24,0},{32,40},{40,48},{48,56},{56,32},{64,72... | collective-permute-start | bytes 983048 | tf_op jit(solution)/shard_map/ppermute | solution.py:67
  337.1 16.4 %collective-permute-start.57 = (bf16[4,64,640]{2,1,0:T(8,128)(2,1)}, bf16[4,64,640]{2,1,0:T(8,128)(2,1)}, u32[]{:S(2)}, u32[]{:S(2)}) collective-permute-start(bf16[4,64,640]{2,1,0:T(8,128)(2,1)} %get-tuple-element.305), channel_id=1, source_target_pairs={{0,16},{8,24},{16,0},{24,8},{32,48},{40,56},{48,32},{56,40},{64,80... | collective-permute-start | bytes 983048 | tf_op jit(solution)/shard_map/ppermute | solution.py:67
  (138 other events, 1300.6 us)
Sparse Core Ops, SparseCore 0:
  10.8 79.9 all-gather.4
  93.5 80.1 all-gather.6
  212.4 105.3 reduce-scatter.2
  320.0 24.3 all-gather.8
  346.6 30.7 reduce-scatter.4
  382.2 27.7 all-gather.10
